TPU v7x, 128 devices: a whole 4x4x4 slice. The times are simulated.
128 devices in a mesh: dp: 32 (over z, x, y_lo), mp: 4 (over y_hi, core).
Axes of the slice: x: 4, y: 4 (y_hi: 2, y_lo: 2; y = y_hi * 2 + y_lo), z: 4, core: 2. Of those that a mesh axis runs over, the one named last changes fastest.
Arguments:
- tokens: bfloat16 [32, 512, 768], P('dp'), may hold values from -6 to 6
- segment_lens: int32 [32, 8], P('dp'), may hold values from 1 to 256, as said below
- norm1_gain: float32 [768], replicated, may hold values from 0.5 to 1.5
- norm1_shift: float32 [768], replicated, may hold values from -1.25 to 1.25
- qkv_weight: bfloat16 [768, 12, 192], P(None, 'mp'), may hold values from -0.21875 to 0.21875
- qv_bias: float32 [12, 128], P('mp'), may hold values from -1.25 to 1.25
- out_weight: bfloat16 [768, 768], P('mp'), may hold values from -1.25 to 1.25
- out_bias: float32 [768], replicated, may hold values from -1.25 to 1.25
- norm2_gain: float32 [768], replicated, may hold values from 0.5 to 1.5
- norm2_shift: float32 [768], replicated, may hold values from -1.25 to 1.25
- up_weight: bfloat16 [768, 3072], P(None, 'mp'), may hold values from -0.21875 to 0.21875
- up_bias: float32 [3072], P('mp'), may hold values from -1.25 to 1.25
- down_weight: bfloat16 [3072, 768], P('mp'), may hold values from -0.109375 to 0.109375
- down_bias: float32 [768], replicated, may hold values from -1.25 to 1.25
- cotangent: bfloat16 [32, 512, 768], P('dp'), may hold values from -6 to 6
Outputs:
- mixed: bfloat16 [32, 512, 768], P('dp')
- tokens_grad: float32 [32, 512, 768], P('dp')
- norm1_gain_grad: float32 [768], replicated
- norm1_shift_grad: float32 [768], replicated
- qkv_weight_grad: float32 [768, 12, 192], P(None, 'mp')
- qv_bias_grad: float32 [12, 128], P('mp')
- out_weight_grad: float32 [768, 768], P('mp')
- out_bias_grad: float32 [768], replicated
- norm2_gain_grad: float32 [768], replicated
- norm2_shift_grad: float32 [768], replicated
- up_weight_grad: float32 [768, 3072], P(None, 'mp')
- up_bias_grad: float32 [3072], P('mp')
- down_weight_grad: float32 [3072, 768], P('mp')
- down_bias_grad: float32 [768], replicated
Inputs may be any that keep to these rules, and one draw needn't show every extreme that they name: `segment_lens`: each row's 8 document lengths are positive and sum to at most 512; the first row's sum to exactly 512, and its first document is exactly 256 long. Positions from that sum to the row's end form its padded tail.
All inputs are finite; a program needn't handle non-finite values.
Results may differ from a plain program's by a relative error of at most 0.028.
Values may be sent and summed in bfloat16 or wider, within the bound.
No kernel may reach another device: no remote copies, remote signals or barrier semaphores. Data moves between devices by JAX's collectives and lax.ppermute only.
A program may use at most 64 MiB of HBM per device.

v0:
```python
from functools import partial

import jax
import jax.numpy as jnp
from jax import lax
from jax.sharding import PartitionSpec as P

EPSILON = 1e-05
MASKED = -1e30


def norm_rows(values_in, norm_gain, norm_shift):
    center = values_in - jnp.mean(values_in, axis=-1, keepdims=True)
    spread = jnp.mean(center * center, axis=-1, keepdims=True)
    return center * lax.rsqrt(spread + EPSILON) * norm_gain + norm_shift


def gelu_exact(activation_in):
    return 0.5 * activation_in * (1.0 + jax.scipy.special.erf(activation_in * 0.7071067811865476))


def gelu_slope(activation_in):
    cumulative = 0.5 * (1.0 + jax.scipy.special.erf(activation_in * 0.7071067811865476))
    density = jnp.exp(-0.5 * activation_in * activation_in) * 0.3989422804014327
    return cumulative + activation_in * density


def doc_numbers(lengths, row_length):
    doc_ends = jnp.cumsum(lengths)
    places = jnp.arange(row_length, dtype=jnp.int32)
    return jnp.sum((places[:, None] >= doc_ends[None, :]).astype(jnp.int32), axis=1)


def allowed_pairs(doc_ids, doc_count):
    places = jnp.arange(doc_ids.shape[0], dtype=jnp.int32)
    same_doc = (doc_ids[:, None] == doc_ids[None, :]) & (doc_ids[:, None] < doc_count)
    return same_doc | (places[:, None] == places[None, :])


def contract_rows(left_side, right_side):
    return lax.dot_general(
        left_side, right_side, (((0,), (0,)), ((), ())), preferred_element_type=jnp.float32
    )


def times_transpose(left_side, right_side):
    return lax.dot_general(
        left_side, right_side, (((1,), (1,)), ((), ())), preferred_element_type=jnp.float32
    )


def masked_scores(query_row, key_row, doc_row, doc_count, score_scale):
    scores = (
        jnp.einsum("qhd,khd->hqk", query_row, key_row, preferred_element_type=jnp.float32)
        * score_scale
    )
    return jnp.where(allowed_pairs(doc_row, doc_count)[None], scores, MASKED)


def shards(
    tokens,
    segment_lens,
    norm1_gain,
    norm1_shift,
    qkv_weight,
    qv_bias,
    out_weight,
    out_bias,
    norm2_gain,
    norm2_shift,
    up_weight,
    up_bias,
    down_weight,
    down_bias,
    cotangent,
):
    row_count, row_length, feature_count = tokens.shape
    tokens_here = row_count * row_length
    heads_here = qkv_weight.shape[1]
    head_size = qkv_weight.shape[2] // 3
    doc_count = segment_lens.shape[1]
    score_scale = head_size ** (-0.5)

    def shaped(array_in):
        return array_in.reshape(row_count, row_length, heads_here, head_size)

    x_rows = tokens.reshape(tokens_here, feature_count).astype(jnp.float32)
    normed_one = norm_rows(x_rows, norm1_gain, norm1_shift).astype(jnp.bfloat16)
    qkv_flat = qkv_weight.reshape(feature_count, heads_here * 3 * head_size)
    projected = jnp.dot(normed_one, qkv_flat, preferred_element_type=jnp.float32)
    projected = projected.reshape(tokens_here, heads_here, 3, head_size)
    queries = (projected[:, :, 0] + qv_bias[None, :, :head_size]).astype(jnp.bfloat16)
    key_rows = projected[:, :, 1].astype(jnp.bfloat16)
    value_rows = (projected[:, :, 2] + qv_bias[None, :, head_size:]).astype(jnp.bfloat16)
    doc_ids = jax.vmap(partial(doc_numbers, row_length=row_length))(segment_lens)

    def attend_forward(row_item):
        query_row, key_row, value_row, doc_row = row_item
        scores = masked_scores(query_row, key_row, doc_row, doc_count, score_scale)
        row_max = jnp.max(scores, axis=-1, keepdims=True)
        expo = jnp.exp(scores - row_max)
        row_total = jnp.sum(expo, axis=-1, keepdims=True)
        probs_low = (expo / row_total).astype(jnp.bfloat16)
        context_row = jnp.einsum(
            "hqk,khd->qhd", probs_low, value_row, preferred_element_type=jnp.float32
        )
        return (context_row.astype(jnp.bfloat16), (row_max + jnp.log(row_total))[..., 0])

    context, log_totals = lax.map(
        attend_forward, (shaped(queries), shaped(key_rows), shaped(value_rows), doc_ids)
    )
    context = context.reshape(tokens_here, heads_here * head_size)
    attn_part = jnp.dot(context, out_weight, preferred_element_type=jnp.float32)
    resid = x_rows + lax.psum(attn_part.astype(jnp.bfloat16), "mp").astype(jnp.float32) + out_bias
    normed_two = norm_rows(resid, norm2_gain, norm2_shift).astype(jnp.bfloat16)
    up_pre = jnp.dot(normed_two, up_weight, preferred_element_type=jnp.float32) + up_bias
    hidden = gelu_exact(up_pre).astype(jnp.bfloat16)
    down_part = jnp.dot(hidden, down_weight, preferred_element_type=jnp.float32)
    mixed_rows = (
        resid + lax.psum(down_part.astype(jnp.bfloat16), "mp").astype(jnp.float32) + down_bias
    ).astype(jnp.bfloat16)
    cot_rows = cotangent.reshape(tokens_here, feature_count)
    down_weight_grad = contract_rows(hidden, cot_rows)
    down_bias_grad = jnp.sum(cot_rows.astype(jnp.float32), axis=0)
    hidden_grad = times_transpose(cot_rows, down_weight)
    up_grad = (hidden_grad * gelu_slope(up_pre)).astype(jnp.bfloat16)
    up_weight_grad = contract_rows(normed_two, up_grad)
    up_bias_grad = jnp.sum(up_grad.astype(jnp.float32), axis=0)
    normed_two_grad = lax.psum(
        times_transpose(up_grad, up_weight).astype(jnp.bfloat16), "mp"
    ).astype(jnp.float32)
    _, norm_two_pull = jax.vjp(norm_rows, resid, norm2_gain, norm2_shift)
    resid_norm_grad, norm2_gain_grad, norm2_shift_grad = norm_two_pull(normed_two_grad)
    resid_grad = cot_rows.astype(jnp.float32) + resid_norm_grad
    attention_grad = resid_grad.astype(jnp.bfloat16)
    out_bias_grad = jnp.sum(attention_grad.astype(jnp.float32), axis=0)
    out_weight_grad = contract_rows(context, attention_grad)
    context_grad = times_transpose(attention_grad, out_weight).astype(jnp.bfloat16)

    def attend_backward(row_item):
        query_row, key_row, value_row, doc_row, log_row, context_row_grad = row_item
        scores = masked_scores(query_row, key_row, doc_row, doc_count, score_scale)
        probs = jnp.exp(scores - log_row[..., None])
        probs_grad = jnp.einsum(
            "qhd,khd->hqk", context_row_grad, value_row, preferred_element_type=jnp.float32
        )
        value_grad = jnp.einsum(
            "hqk,qhd->khd",
            probs.astype(jnp.bfloat16),
            context_row_grad,
            preferred_element_type=jnp.float32,
        )
        centre = jnp.sum(probs_grad * probs, axis=-1, keepdims=True)
        score_grad = (probs * (probs_grad - centre)).astype(jnp.bfloat16)
        query_grad = (
            jnp.einsum("hqk,khd->qhd", score_grad, key_row, preferred_element_type=jnp.float32)
            * score_scale
        )
        key_grad = (
            jnp.einsum("hqk,qhd->khd", score_grad, query_row, preferred_element_type=jnp.float32)
            * score_scale
        )
        return (
            query_grad.astype(jnp.bfloat16),
            key_grad.astype(jnp.bfloat16),
            value_grad.astype(jnp.bfloat16),
        )

    query_grad, key_grad, value_grad = lax.map(
        attend_backward,
        (
            shaped(queries),
            shaped(key_rows),
            shaped(value_rows),
            doc_ids,
            log_totals,
            shaped(context_grad),
        ),
    )
    qkv_grad = jnp.stack((query_grad, key_grad, value_grad), axis=3).reshape(
        tokens_here, heads_here * 3 * head_size
    )
    qkv_weight_grad = contract_rows(normed_one, qkv_grad).reshape(
        feature_count, heads_here, 3 * head_size
    )
    qv_bias_grad = jnp.concatenate(
        (
            jnp.sum(query_grad.astype(jnp.float32), axis=(0, 1)),
            jnp.sum(value_grad.astype(jnp.float32), axis=(0, 1)),
        ),
        axis=1,
    )
    normed_one_grad = lax.psum(
        times_transpose(qkv_grad, qkv_flat).astype(jnp.bfloat16), "mp"
    ).astype(jnp.float32)
    _, norm_one_pull = jax.vjp(norm_rows, x_rows, norm1_gain, norm1_shift)
    input_norm_grad, norm1_gain_grad, norm1_shift_grad = norm_one_pull(normed_one_grad)
    tokens_grad = resid_grad + input_norm_grad
    (
        norm1_gain_grad,
        norm1_shift_grad,
        qkv_weight_grad,
        qv_bias_grad,
        out_weight_grad,
        out_bias_grad,
        norm2_gain_grad,
        norm2_shift_grad,
        up_weight_grad,
        up_bias_grad,
        down_weight_grad,
        down_bias_grad,
    ) = (
        lax.psum(norm1_gain_grad.astype(jnp.bfloat16), "dp").astype(jnp.float32),
        lax.psum(norm1_shift_grad.astype(jnp.bfloat16), "dp").astype(jnp.float32),
        lax.psum(qkv_weight_grad.astype(jnp.bfloat16), "dp").astype(jnp.float32),
        lax.psum(qv_bias_grad.astype(jnp.bfloat16), "dp").astype(jnp.float32),
        lax.psum(out_weight_grad.astype(jnp.bfloat16), "dp").astype(jnp.float32),
        lax.psum(out_bias_grad.astype(jnp.bfloat16), "dp").astype(jnp.float32),
        lax.psum(norm2_gain_grad.astype(jnp.bfloat16), "dp").astype(jnp.float32),
        lax.psum(norm2_shift_grad.astype(jnp.bfloat16), "dp").astype(jnp.float32),
        lax.psum(up_weight_grad.astype(jnp.bfloat16), "dp").astype(jnp.float32),
        lax.psum(up_bias_grad.astype(jnp.bfloat16), "dp").astype(jnp.float32),
        lax.psum(down_weight_grad.astype(jnp.bfloat16), "dp").astype(jnp.float32),
        lax.psum(down_bias_grad.astype(jnp.bfloat16), "dp").astype(jnp.float32),
    )
    return (
        mixed_rows.reshape(row_count, row_length, feature_count),
        tokens_grad.reshape(row_count, row_length, feature_count),
        norm1_gain_grad,
        norm1_shift_grad,
        qkv_weight_grad,
        qv_bias_grad,
        out_weight_grad,
        out_bias_grad,
        norm2_gain_grad,
        norm2_shift_grad,
        up_weight_grad,
        up_bias_grad,
        down_weight_grad,
        down_bias_grad,
    )


def solution(mesh):
    placed = (
        P("dp", None, None),
        P("dp", None),
        P(),
        P(),
        P(None, "mp", None),
        P("mp", None),
        P("mp", None),
        P(),
        P(),
        P(),
        P(None, "mp"),
        P("mp"),
        P("mp", None),
        P(),
        P("dp", None, None),
    )
    return jax.shard_map(
        shards,
        mesh=mesh,
        in_specs=placed,
        out_specs=(
            P("dp", None, None),
            P("dp", None, None),
            P(),
            P(),
            P(None, "mp", None),
            P("mp", None),
            P("mp", None),
            P(),
            P(),
            P(),
            P(None, "mp"),
            P("mp"),
            P("mp", None),
            P(),
        ),
        check_vma=False,
    )
```

profile of v0, /device:TPU:0, one launch (start us, length us, event | category | flops | bytes accessed | tf_op | source)
XLA Modules:
  0.0 520.7 jit_solution(690420453418558204)
XLA Ops:
  7.3 1.4 convert_reduce_fusion
  8.8 1.5 fusion.14
  11.3 2.0 fusion.44
  13.4 0.8 fusion.71
  14.6 1.2 copy-done.2
  16.8 1.3 convolution_convert_fusion.6
  18.1 46.2 %all-reduce.8.cloned.1.call-done = bf16[512,768]{1,0:T(8,128)(2,1)} async-done(((bf16[512,768]{1,0:T(8,128)(2,1)}), bf16[512,768]{1,0:T(8,128)(2,1)}) %all-reduce.8.cloned.1.call-update) | async-done | bytes 786448 | tf_op jit(solution)/shard_map/psum | solution.py:114
  64.4 1.5 fusion.32
  67.0 3.1 multiply_convert_fusion.1
  70.1 1.7 fusion.72
  71.8 0.9 copy-done.53
  72.7 1.7 convolution_convert_fusion.3
  75.4 3.2 convolution_convert_fusion.4
  78.6 39.1 %all-reduce.10.cloned.1.call-done = bf16[512,768]{1,0:T(8,128)(2,1)} async-done(((bf16[512,768]{1,0:T(8,128)(2,1)}), bf16[512,768]{1,0:T(8,128)(2,1)}) %all-reduce.10.cloned.1.call-update) | async-done | bytes 786448 | tf_op jit(solution)/shard_map/psum | solution.py:129
  117.8 1.8 fusion.11
  119.6 1.6 fusion.12
  121.3 1.6 fusion.68
  123.5 0.8 multiply_reduce_fusion
  124.3 0.9 multiply_convert_fusion
  125.2 1.0 bitcast_reduce_fusion.1
  126.8 1.3 bitcast_reduce_fusion
  128.3 0.8 copy-done.18
  129.5 1.7 convolution_convert_fusion.5
  131.3 3.0 convolution_convert_fusion
  134.4 2.0 convolution_convert_fusion.1
  136.5 1.0 convolution_convert_fusion.7
  137.5 1.8 convolution_convert_fusion.2
  139.3 0.7 reduce_sum.264
  140.1 1.3 pad_maximum_fusion.1
  141.4 40.7 %all-reduce.14.cloned.1.call-done = (bf16[512,768]{1,0:T(8,128)(2,1)}, bf16[512,768]{1,0:T(8,128)(2,1)}) async-done(((bf16[512,768]{1,0:T(8,128)(2,1)}, bf16[512,768]{1,0:T(8,128)(2,1)}), (bf16[512,768]{1,0:T(8,128)(2,1)}, bf16[512,768]{1,0:T(8,128)(2,1)})) %all-reduce.14.cloned.1.call-update) | async-done | bytes 1572880 | tf_op jit(solution)/shard_map/psum | solution.py:120
  182.1 1.9 reduce_sum.257
  184.1 1.6 fusion.15
  186.9 2.2 fusion.13
  189.2 158.0 %all-reduce = (bf16[768]{0:T(1024)(128)(2,1)}, bf16[768]{0:T(1024)(128)(2,1)}, bf16[3,128]{1,0:T(4,128)(2,1)}, bf16[768]{0:T(1024)(128)(2,1)}, bf16[768]{0:T(102...) all-reduce(bf16[768]{0:T(1024)(128)(2,1)} %get-tuple-element.57, ...), channel_id=1, replica_groups=mesh['dp'=32,'mp'=4] {'dp'}, use_global_device_ids=true, to_apply=%region_18.19 | all-reduce | flops 5760 | bytes 23040 | tf_op jit(solution)/shard_map/psum | solution.py:213
  347.2 1.3 convert_element_type.227
  348.4 1.3 convert_element_type.228
  349.7 1.3 convert_element_type.236
  351.0 1.3 convert_element_type.238
  352.3 1.3 convert_element_type.239
  353.5 1.3 convert_element_type.242
  354.8 1.3 convert_element_type.245
  356.1 1.2 convert_element_type.233
  358.0 3.9 add_bitcast_fusion
  361.9 145.5 %all-reduce.12.cloned.1.call-done = (bf16[768,3,192]{0,2,1:T(8,128)(2,1)}, bf16[192,768]{1,0:T(8,128)(2,1)}, bf16[768,768]{1,0:T(8,128)(2,1)}, bf16[768,768]{1,0:T(8,128)(2,1)}) async-done(((bf16[768,3,192]{0,2,1:T(8,128)(2,1)}, bf16[192,768]{1,0:T(8,128)(2,1)}, bf16[768,768]{1,0:T(8,128)(2,1)}, bf16[768,768]{1,0:T(8,128)(2,1)}), (bf16[768,3,192]{0,2,1:T(8,128)(2,1)}, bf16[192,768]{1,0:T(8,128)(2,1)}, ...) | async-done | bytes 3538960 | tf_op jit(solution)/shard_map/psum | solution.py:215
  507.4 2.9 convert_element_type.241
  510.4 1.6 convert_element_type.244
  511.9 1.4 convert_element_type.230
  513.3 0.9 convert_element_type.235
  (136 shorter events, 8.5 us)
Async XLA Ops:
  7.2 59.8 %copy-start = (bf16[768,768]{1,0:T(8,128)(2,1)S(1)}, bf16[768,768]{1,0:T(8,128)(2,1)}, u32[]{:S(2)}) copy-start(bf16[768,768]{1,0:T(8,128)(2,1)} %param.25) | copy-start | bytes 3538948
  7.2 4.1 copy-start.1
  7.2 3.1 copy-start.52
  7.2 4.0 copy-start.46
  7.2 4.1 copy-start.28
  7.2 4.1 copy-start.50
  7.3 57.1 %all-reduce.8.cloned.1.call-start = ((), (), s32[]{:S(2)}) async-start(), calls=%async_computation | async-start | bytes 1572864 | tf_op jit(solution)/shard_map/psum | solution.py:114
  8.7 4.6 copy-start.26
  10.3 3.1 copy-start.36
  11.3 2.1 copy-start.39
  11.3 3.3 copy-start.44
  14.1 1.7 copy-start.2
  14.2 1.6 copy-start.22
  14.6 1.9 copy-start.30
  16.5 1.6 copy-start.16
  16.5 47.9 %copy-start.21 = (f32[768]{0:T(1024)S(1)}, f32[768]{0:T(1024)}, u32[]{:S(2)}) copy-start(f32[768]{0:T(1024)} %param.22) | copy-start | bytes 9220
  18.1 48.9 %copy-start.23 = (f32[768]{0:T(1024)S(1)}, f32[768]{0:T(1024)}, u32[]{:S(2)}) copy-start(f32[768]{0:T(1024)} %param.23) | copy-start | bytes 9220
  18.1 99.7 %all-reduce.10.cloned.1.call-start = ((), (), s32[]{:S(2)}) async-start(), calls=%async_computation.1 | async-start | bytes 1572864 | tf_op jit(solution)/shard_map/psum | solution.py:129
  64.4 1.5 copy-start.4
  67.0 3.1 copy-start.32
  67.0 3.1 copy-start.7
  67.0 3.1 copy-start.47
  74.4 107.7 %all-reduce.14.cloned.1.call-start = ((), (), s32[]{:S(2)}) async-start(), calls=%async_computation.3 | async-start | bytes 3145728 | tf_op jit(solution)/shard_map/psum | solution.py:120
  117.8 1.8 copy-start.43
  117.8 1.8 copy-start.6
  117.8 1.8 copy-start.24
  117.8 1.8 copy-start.33
  119.6 3.2 copy-start.31
  119.6 3.2 copy-start.14
  121.2 1.6 copy-start.38
  121.2 2.0 copy-start.3
  121.2 2.2 copy-start.11
  121.3 2.2 copy-start.45
  131.2 3.1 copy-start.25
  131.2 376.2 %all-reduce.12.cloned.1.call-start = ((), (), s32[]{:S(2)}) async-start(), calls=%async_computation.2 | async-start | bytes 7077888 | tf_op jit(solution)/shard_map/psum | solution.py:215
  131.3 3.1 copy-start.34
  131.3 3.1 copy-start.49
  131.3 3.1 copy-start.54
  134.4 2.1 copy-start.9
  134.4 2.1 copy-start.17
  134.4 3.1 copy-start.19
  134.4 3.1 copy-start.27
  134.4 3.1 copy-start.29
  134.4 3.1 copy-start.37
  134.4 3.1 copy-start.51
  182.1 4.8 copy-start.5
  507.4 2.9 copy-start.12
  510.3 1.6 copy-start.15
  (11 other events, 11.0 us)
Sparse Core Ops, SparseCore 0:
  18.2 46.1 all-reduce.7
  74.6 43.1 all-reduce.9
  131.3 50.7 all-reduce.13
  185.9 321.4 all-reduce.11
where the time goes:
time: 522 us; the launch traced here: 521 us
  waiting for transfers between devices  272 us (52%)
  blocking collectives  158 us (30%)
  other arithmetic  42.6 us (8%)
  matrix products  28.2 us (5%)
  between operations  14.3 us (3%)
  local copies, waits for them, and re-layouts  5.62 us (1%)
    psum x1, blocking collectives, shards(): lax.psum(norm1_gain_grad.astype(jnp.bfloat16), 'dp').astype(jnp.float32)  158 us
    psum x1, waiting for transfers between devices, shards(): lax.psum(qkv_weight_grad.astype(jnp.bfloat16), 'dp').astype(jnp.float32)  145 us
    psum x1, waiting for transfers between devices, shards(): lax.psum(attn_part.astype(jnp.bfloat16), 'mp').astype(jnp.float32)  46.2 us
    psum x1, waiting for transfers between devices, shards(): lax.psum(down_part.astype(jnp.bfloat16), 'mp').astype(jnp.float32)  40.7 us
    psum x1, waiting for transfers between devices, shards(): lax.psum(times_transpose(up_grad, up_weight).astype(jnp.bfloat16), 'mp')  39.1 us
  transfers between devices with their start and end apart: 4, of which 4 were waited for; matrix products, arithmetic and copies ran while one was open for 7% of the time, Pallas kernels for 0%

commit v1 on v0

v1 whole, which is shorter than its diff:
```python
import jax
import jax.numpy as jnp
from jax import lax
from jax.sharding import Mesh
from jax.sharding import PartitionSpec as P

EPSILON = 1e-05
PLANE = ("z", "x")
DP = ("z", "x", "near")
MP = ("far", "core")
MASKED = -1e30
BF = jnp.bfloat16
F32 = jnp.float32


def norm_parts(values_in):
    center = values_in - jnp.mean(values_in, axis=-1, keepdims=True)
    spread = jnp.mean(center * center, axis=-1, keepdims=True)
    inverse = lax.rsqrt(spread + EPSILON)
    return center * inverse, inverse


def norm_back(grad, xhat, inverse, gain):
    scaled = grad * gain
    centre = jnp.mean(scaled, axis=-1, keepdims=True)
    along = jnp.mean(scaled * xhat, axis=-1, keepdims=True)
    return inverse * (scaled - centre - xhat * along)


def dot(left_side, right_side, left_dim=1, right_dim=0):
    return lax.dot_general(
        left_side, right_side, (((left_dim,), (right_dim,)), ((), ())), preferred_element_type=F32
    )


def shards(
    tokens,
    segment_lens,
    norm1_gain,
    norm1_shift,
    qkv_weight,
    qv_bias,
    out_weight,
    out_bias,
    norm2_gain,
    norm2_shift,
    up_weight,
    up_bias,
    down_weight,
    down_bias,
    cotangent,
):
    row_length, feature_count = tokens.shape[1:]
    heads_here = qkv_weight.shape[1]
    head_size = qkv_weight.shape[2] // 3
    doc_count = segment_lens.shape[1]
    score_scale = head_size ** (-0.5)
    half = row_length // 2
    plane_count = lax.axis_size(PLANE)
    core = lax.axis_index("core")
    mine_at, other_at = core * half, (1 - core) * half

    def core_swap(array_in):
        return lax.ppermute(array_in, "core", [(0, 1), (1, 0)])

    def chip_swap(array_in):
        return lax.ppermute(array_in, "far", [(0, 1), (1, 0)])

    def near_swap(array_in):
        return lax.ppermute(array_in, "near", [(0, 1), (1, 0)])

    def own_first(array_in):
        return jnp.concatenate(
            (
                lax.dynamic_slice_in_dim(array_in, mine_at, half),
                lax.dynamic_slice_in_dim(array_in, other_at, half),
            )
        )

    def in_order(mine, other):
        first = core == 0
        return jnp.concatenate((jnp.where(first, mine, other), jnp.where(first, other, mine)))

    def sum_half(part):
        received = core_swap(part[half:].astype(BF))
        pair = (part[:half] + received.astype(F32)).astype(BF)
        return pair.astype(F32) + chip_swap(pair).astype(F32)

    def both_halves(mine):
        return jnp.concatenate((mine, core_swap(mine)))

    def scatter(grads):
        chunks = [g.astype(BF).reshape(plane_count, -1, feature_count) for g in grads]
        return lax.all_to_all(jnp.concatenate(chunks, axis=1), PLANE, 0, 0, tiled=True)

    def finish(received):
        pair = jnp.sum(received.astype(F32), axis=0).astype(BF)
        return (pair.astype(F32) + near_swap(pair).astype(F32)).astype(BF)

    def gather(chunk):
        copies = jnp.broadcast_to(chunk[None], (plane_count,) + chunk.shape)
        return lax.all_to_all(copies, PLANE, 0, 0, tiled=True)

    x_rows = own_first(tokens[0]).astype(F32)
    cot_rows = own_first(cotangent[0])
    xhat_one, inverse_one = norm_parts(x_rows)
    normed_one = (xhat_one * norm1_gain + norm1_shift).astype(BF)
    qkv_rows = qkv_weight.transpose(1, 2, 0).reshape(heads_here * 3 * head_size, feature_count)
    projected = dot(normed_one, qkv_rows, 1, 1).reshape(row_length, heads_here, 3, head_size)
    queries = (projected[:, :, 0] + qv_bias[None, :, :head_size]).astype(BF)
    key_rows = projected[:, :, 1].astype(BF)
    value_rows = (projected[:, :, 2] + qv_bias[None, :, head_size:]).astype(BF)

    doc_ends = jnp.cumsum(segment_lens[0])
    places = own_first(jnp.arange(row_length, dtype=jnp.int32))
    doc_ids = jnp.sum((places[:, None] >= doc_ends[None, :]).astype(jnp.int32), axis=1)
    same_doc = (doc_ids[:, None] == doc_ids[None, :]) & (doc_ids[:, None] < doc_count)
    allowed = same_doc | (places[:, None] == places[None, :])

    scores = jnp.einsum("qhd,khd->hqk", queries, key_rows, preferred_element_type=F32) * score_scale
    scores = jnp.where(allowed[None], scores, MASKED)
    row_max = jnp.max(scores, axis=-1, keepdims=True)
    expo = jnp.exp(scores - row_max)
    row_total = jnp.sum(expo, axis=-1, keepdims=True)
    probs = expo / row_total
    probs_low = probs.astype(BF)
    context = jnp.einsum("hqk,khd->qhd", probs_low, value_rows, preferred_element_type=F32)
    context = context.astype(BF).reshape(row_length, heads_here * head_size)

    resid = x_rows[:half] + sum_half(dot(context, out_weight)) + out_bias
    xhat_two, inverse_two = norm_parts(resid)
    normed_two = both_halves((xhat_two * norm2_gain + norm2_shift).astype(BF))
    up_pre = dot(normed_two, up_weight) + up_bias
    cumulative = 0.5 * (1.0 + lax.erf(up_pre * 0.7071067811865476))
    hidden = (up_pre * cumulative).astype(BF)
    slope = cumulative + up_pre * (jnp.exp(-0.5 * up_pre * up_pre) * 0.3989422804014327)
    up_grad = (dot(cot_rows, down_weight, 1, 1) * slope).astype(BF)

    normed_two_grad = sum_half(dot(up_grad, up_weight, 1, 1))
    resid_grad = cot_rows[:half].astype(F32) + norm_back(
        normed_two_grad, xhat_two, inverse_two, norm2_gain
    )
    attention_grad_half = resid_grad.astype(BF)
    attention_grad = both_halves(attention_grad_half)

    expert_parts = scatter((dot(hidden, cot_rows, 0, 0), dot(normed_two, up_grad, 0, 0)))

    mixed_half = (resid + sum_half(dot(hidden, down_weight)) + down_bias).astype(BF)
    mixed = in_order(mixed_half, core_swap(mixed_half))

    context_grad = dot(attention_grad, out_weight, 1, 1).astype(BF)
    context_grad = context_grad.reshape(row_length, heads_here, head_size)
    probs_grad = jnp.einsum("qhd,khd->hqk", context_grad, value_rows, preferred_element_type=F32)
    value_grad = jnp.einsum("hqk,qhd->khd", probs_low, context_grad, preferred_element_type=F32)
    centre = jnp.sum(probs_grad * probs, axis=-1, keepdims=True)
    score_grad = (probs * (probs_grad - centre)).astype(BF)
    query_grad = jnp.einsum("hqk,khd->qhd", score_grad, key_rows, preferred_element_type=F32)
    key_grad = jnp.einsum("hqk,qhd->khd", score_grad, queries, preferred_element_type=F32)
    query_grad = (query_grad * score_scale).astype(BF)
    key_grad = (key_grad * score_scale).astype(BF)
    value_grad = value_grad.astype(BF)
    qkv_grad = jnp.stack((query_grad, key_grad, value_grad), axis=2).reshape(row_length, -1)

    normed_one_grad = sum_half(dot(qkv_grad, qkv_rows))
    xhat_half = xhat_one[:half]
    tokens_grad_half = resid_grad + norm_back(
        normed_one_grad, xhat_half, inverse_one[:half], norm1_gain
    )
    tokens_grad = in_order(tokens_grad_half, core_swap(tokens_grad_half))

    attend_parts = scatter(
        (
            dot(qkv_grad, normed_one, 0, 0),
            dot(context, attention_grad, 0, 0),
        )
    )
    expert_sum = finish(expert_parts)
    expert_sum, attend_parts = lax.optimization_barrier((expert_sum, attend_parts))
    expert_grads = gather(expert_sum)
    attend_sum = finish(attend_parts)

    halves = jnp.stack(
        (
            jnp.sum(normed_one_grad * xhat_half, axis=0),
            jnp.sum(normed_one_grad, axis=0),
            jnp.sum(normed_two_grad * xhat_two, axis=0),
            jnp.sum(normed_two_grad, axis=0),
            jnp.sum(attention_grad_half.astype(F32), axis=0),
            jnp.sum(cot_rows[:half].astype(F32), axis=0),
        )
    )
    halves = halves + core_swap(halves)
    qv_sums = jnp.stack((query_grad, value_grad), axis=2).astype(F32).sum(axis=0).reshape(-1)
    whole = jnp.stack(
        (
            jnp.sum(up_grad.astype(F32), axis=0),
            jnp.pad(qv_sums, (0, feature_count - qv_sums.shape[0])),
        )
    )
    vectors = jnp.concatenate((halves, whole))
    vectors = (vectors + near_swap(vectors)).astype(BF)

    expert_grads, attend_sum = lax.optimization_barrier((expert_grads, attend_sum))
    last = gather(jnp.concatenate((attend_sum, vectors)))
    chunk_rows = attend_sum.shape[0]
    expert_grads = expert_grads.astype(F32)
    attend_grads = last[:, :chunk_rows].astype(F32)
    vector_sums = jnp.sum(last[:, chunk_rows:].astype(F32), axis=0)

    def rows_of(grads, first, count):
        return grads[:, first : first + count].reshape(-1, feature_count)

    qkv_chunk = heads_here * 3 * head_size // plane_count
    down_chunk = hidden.shape[1] // plane_count
    qkv_weight_grad = rows_of(attend_grads, 0, qkv_chunk).reshape(
        heads_here, 3 * head_size, feature_count
    )
    return (
        mixed[None],
        tokens_grad[None],
        vector_sums[0],
        vector_sums[1],
        qkv_weight_grad.transpose(2, 0, 1),
        vector_sums[7, : qv_sums.shape[0]].reshape(heads_here, 2 * head_size),
        rows_of(attend_grads, qkv_chunk, chunk_rows - qkv_chunk),
        vector_sums[4],
        vector_sums[2],
        vector_sums[3],
        rows_of(expert_grads, down_chunk, feature_count // plane_count),
        vector_sums[6],
        rows_of(expert_grads, 0, down_chunk),
        vector_sums[5],
    )


def solution(mesh):
    fine = Mesh(mesh.devices.reshape(4, 4, 2, 2, 2), ("z", "x", "near", "far", "core"))
    rows, heads, features = P(DP, None, None), P(MP, None), P(MP)
    placed = (
        rows,
        P(DP, None),
        P(),
        P(),
        P(None, MP, None),
        heads,
        heads,
        P(),
        P(),
        P(),
        P(None, MP),
        features,
        heads,
        P(),
        rows,
    )
    given = (
        rows,
        rows,
        P(),
        P(),
        P(None, MP, None),
        heads,
        heads,
        P(),
        P(),
        P(),
        P(None, MP),
        features,
        heads,
        P(),
    )
    return jax.shard_map(shards, mesh=fine, in_specs=placed, out_specs=given, check_vma=False)
```

time: 522 us -> 207 us (0.40)
  waiting for transfers between devices: 272 us -> 78.3 us
  blocking collectives: 158 us -> 0 us
  starting transfers between devices: 0.34 us -> 35.8 us
  local copies, waits for them, and re-layouts: 5.62 us -> 28.6 us
  between operations: 14.3 us -> 1.4 us
  other arithmetic: 42.6 us -> 33.5 us
    psum x4 -> x0, waiting for transfers between devices: 272 us -> none  [the longest x1 145 us: shards(): lax.psum(qkv_weight_grad.astype(jnp.bfloat16), 'dp').astype(jnp.float32)]
    psum x1 -> x0, blocking collectives: 158 us -> none  [shards(): lax.psum(norm1_gain_grad.astype(jnp.bfloat16), 'dp').astype(jnp.float32)]
    all_to_all x0 -> x4, waiting for transfers between devices: none -> 43.4 us  [the longest x2 27.1 us: scatter(): lax.all_to_all(jnp.concatenate(chunks, axis=1), PLANE, 0, 0, tiled=True)]
    ppermute x0 -> x16, waiting for transfers between devices: none -> 34.9 us  [the longest x4 28.5 us: chip_swap(): return lax.ppermute(array_in, 'far', [(0, 1), (1, 0)])]
    all_to_all x0 -> x4, starting transfers between devices: none -> 20.6 us  [the longest x2 12.3 us: scatter(): lax.all_to_all(jnp.concatenate(chunks, axis=1), PLANE, 0, 0, tiled=True)]
    ppermute x0 -> x16, starting transfers between devices: none -> 15.1 us  [the longest x4 10.3 us: chip_swap(): return lax.ppermute(array_in, 'far', [(0, 1), (1, 0)])]
    convert_element_type x13 -> x11, other arithmetic: 17.7 us -> 7.57 us  [the longest x1 3.41 us: shards(): score_grad = (probs * (probs_grad - centre)).astype(BF)]
    reduce_sum x13, other arithmetic: 16.9 us -> 9.33 us  [the longest x1 2.19 us: shards(): jnp.sum(normed_one_grad * xhat_half, axis=0)]
  transfers between devices with their start and end apart: 4 -> 20, of which waited for: 4 -> 12; matrix products, arithmetic and copies ran while one was open for 7% -> 28% of each run, Pallas kernels for 0% -> 0%
where the time goes in v1:
time: 207 us; the launch traced here: 206 us
  waiting for transfers between devices  78.3 us (38%)
  starting transfers between devices  35.8 us (17%)
  other arithmetic  33.5 us (16%)
  matrix products  28.8 us (14%)
  local copies, waits for them, and re-layouts  28.6 us (14%)
    ppermute x4, waiting for transfers between devices, chip_swap(): return lax.ppermute(array_in, 'far', [(0, 1), (1, 0)])  28.5 us
    all_to_all x2, waiting for transfers between devices, scatter(): lax.all_to_all(jnp.concatenate(chunks, axis=1), PLANE, 0, 0, tiled=True)  27.1 us
    all_to_all x2, waiting for transfers between devices, gather(): return lax.all_to_all(copies, PLANE, 0, 0, tiled=True)  16.3 us
    dot_general x12, matrix products, dot(): lax.dot_general(left_side, right_side, (((left_dim,), (right_dim,)), ((),...  15.5 us
    all_to_all x2, starting transfers between devices, scatter(): lax.all_to_all(jnp.concatenate(chunks, axis=1), PLANE, 0, 0, tiled=True)  12.3 us
    ppermute x4, starting transfers between devices, chip_swap(): return lax.ppermute(array_in, 'far', [(0, 1), (1, 0)])  10.3 us
    all_to_all x2, starting transfers between devices, gather(): return lax.all_to_all(copies, PLANE, 0, 0, tiled=True)  8.33 us
    unnamed x84, local copies, waits for them, and re-layouts  5.48 us
  transfers between devices with their start and end apart: 20, of which 12 were waited for; matrix products, arithmetic and copies ran while one was open for 28% of the time, Pallas kernels for 0%

profile of v1, /device:TPU:0, one launch (start us, length us, event | category | flops | bytes accessed | tf_op | source)
XLA Modules:
  0.0 206.3 jit_solution(9446605198975631256)
XLA Ops:
  3.1 1.2 dynamic-slice_bitcast_fusion.3
  4.9 1.9 fusion.21
  6.8 4.1 %fusion.59 = (f32[3,512]{1,0:T(4,128)S(1)}, f32[3,512,512]{1,2,0:T(8,128)}) fusion(pred[512,512]{0,1:T(8,128)(4,1)S(1)} %compare_or_fusion, f32[512,3,3,64]{0,3,2,1:T(8,128)} %fusion.21, f32[3,64]{1,0:T(4,128)S(1)} %get-tuple-element.53), kind=kOutput, calls=%fused_computation.144 | convolution fusion | flops 104006144 | bytes 4004608 | tf_op jit(solution)/shard_map/sub | solution.py:123
  10.9 2.5 %convolution_convert_fusion.5 = bf16[3,64,512]{2,1,0:T(8,128)(2,1)S(1)} fusion(f32[512,3,3,64]{0,3,2,1:T(8,128)} %fusion.21, f32[3,64]{1,0:T(4,128)S(1)} %get-tuple-element.54, f32[3,512,512]{1,2,0:T(8,128)} %get-tuple-element.56, f32[3,512]{1,0:T(4,128)S(1)} %get-tuple-element.55), kind=kOutput, calls=%fused_computation.38 | convolution fusion | flops 102531072 | bytes 3742464 | tf_op jit(solution)/shard_map/hqk,khd->qhd/dot_general | solution.py:127
  14.6 1.7 collective-permute-done
  16.4 3.3 %collective-permute-start.1 = (bf16[256,768]{1,0:T(8,128)(2,1)S(1)}, bf16[256,768]{1,0:T(8,128)(2,1)S(1)}, u32[]{:S(2)}, u32[]{:S(2)}) collective-permute-start(bf16[256,768]{1,0:T(8,128)(2,1)S(1)} %fusion.19), channel_id=1, source_target_pairs={{0,2},{2,0},{1,3},{3,1},{4,6},{6,4},{5,7},{7,5},{8,10},{10,8},{9,1... | collective-permute-start | bytes 1179656 | tf_op jit(solution)/shard_map/ppermute | solution.py:67
  19.9 9.3 %collective-permute-done.1 = bf16[256,768]{1,0:T(8,128)(2,1)S(1)} collective-permute-done((bf16[256,768]{1,0:T(8,128)(2,1)S(1)}, bf16[256,768]{1,0:T(8,128)(2,1)S(1)}, u32[]{:S(2)}, u32[]{:S(2)}) %collective-permute-start.1) | collective-permute-done | bytes 393248 | tf_op jit(solution)/shard_map/ppermute | solution.py:67
  32.6 1.7 convert_reduce_fusion
  37.1 3.3 %collective-permute-start.7 = (bf16[256,768]{1,0:T(8,128)(2,1)S(1)}, bf16[256,768]{1,0:T(8,128)(2,1)S(1)}, u32[]{:S(2)}, u32[]{:S(2)}) collective-permute-start(bf16[256,768]{1,0:T(8,128)(2,1)S(1)} %fusion.17), channel_id=1, source_target_pairs={{0,2},{2,0},{1,3},{3,1},{4,6},{6,4},{5,7},{7,5},{8,10},{10,8},{9,1... | collective-permute-start | bytes 1179656 | tf_op jit(solution)/shard_map/ppermute | solution.py:67
  41.7 8.9 %collective-permute-done.7 = bf16[256,768]{1,0:T(8,128)(2,1)S(1)} collective-permute-done((bf16[256,768]{1,0:T(8,128)(2,1)S(1)}, bf16[256,768]{1,0:T(8,128)(2,1)S(1)}, u32[]{:S(2)}, u32[]{:S(2)}) %collective-permute-start.7) | collective-permute-done | bytes 393248 | tf_op jit(solution)/shard_map/ppermute | solution.py:67
  51.6 6.6 %collective-permute-done.4 = bf16[256,768]{1,0:T(8,128)(2,1)S(1)} collective-permute-done((bf16[256,768]{1,0:T(8,128)(2,1)S(1)}, bf16[256,768]{1,0:T(8,128)(2,1)S(1)}, u32[]{:S(2)}, u32[]{:S(2)}) %collective-permute-start.4) | collective-permute-done | bytes 393248 | tf_op jit(solution)/shard_map/ppermute | solution.py:67
  58.2 2.1 %convert_reduce_fusion.4 = (f32[768]{0:T(1024)}, bf16[256,768]{1,0:T(8,128)(2,1)S(1)}, f32[256,768]{1,0:T(8,128)}, bf16[256,768]{1,0:T(8,128)(2,1)}) fusion(f32[256]{0:T(256)S(1)} %get-tuple-element.63, f32[256,768]{1,0:T(8,128)S(1)} %get-tuple-element.43, f32[256]{0:T(256)S(1)} %broadcast_multiply_fusion.5, f32[256]{0:T(256)S(1)} %get-tuple-element.64, ...), kind=kLoop, calls=%fused_computation.68 | loop fusion | flops 4128000 | bytes 4338688 | tf_op jit(solution)/shard_map/reduce_sum | solution.py:188
  61.2 1.7 pad_maximum_fusion
  62.8 7.9 %all-to-all-start = ((bf16[16,96,768]{2,1,0:T(8,128)(2,1)}), bf16[16,96,768]{2,1,0:T(8,128)(2,1)S(1)}, u32[]{:S(2)}, u32[]{:S(2)}) async-start(bf16[16,96,768]{2,1,0:T(8,128)(2,1)} %pad_maximum_fusion), calls=%async_computation | async-start | bytes 4718592 | tf_op jit(solution)/shard_map/all_to_all | solution.py:94
  70.8 1.5 convolution_convert_fusion.6
  72.3 5.2 %multiply_reduce_fusion = (f32[3,512]{1,0:T(4,128)}, f32[3,512,512]{1,2,0:T(8,128)}) fusion(f32[3,512,512]{1,2,0:T(8,128)} %get-tuple-element.56, f32[3,512]{1,0:T(4,128)S(1)} %copy-done.28, bf16[512,3,64]{0,2,1:T(8,128)(2,1)S(1)} %bitcast.113, f32[512,3,3,64]{0,3,2,1:T(8,128)} %fusion.21, f32[3,64]{1,0:T(4,128)S(1)} %copy-done.35), kind=kOutput, calls=%fused_computation.2 | convolution fusion | flops 103217664 | bytes 6894336 | tf_op jit(solution)/shard_map/qhd,khd->hqk/dot_general | solution.py:153
  77.5 2.0 convolution_convert_fusion.3
  80.6 3.4 %multiply_convert_fusion = bf16[3,512,512]{1,2,0:T(8,128)(2,1)S(1)} fusion(f32[3,512,512]{1,2,0:T(8,128)} %get-tuple-element.60, f32[3,512]{1,0:T(4,128)} %get-tuple-element.59, f32[3,512,512]{1,2,0:T(8,128)} %get-tuple-element.56, f32[3,512]{1,0:T(4,128)} %copy-done.27), kind=kLoop, calls=%fused_computation.1 | loop fusion | flops 3145728 | bytes 7876608 | tf_op jit(solution)/shard_map/convert_element_type | solution.py:156
  88.2 1.8 convolution_convert_fusion.2
  89.9 2.1 %reshape.244 = bf16[16,36,768]{2,1,0:T(8,128)(2,1)} reshape(bf16[576,768]{1,0:T(8,128)(2,1)} %convolution_convert_fusion.2) | data formatting | bytes 1769472 | tf_op jit(solution)/shard_map/reshape | solution.py:93
  92.0 2.4 %pad_maximum_fusion.1 = bf16[16,48,768]{2,1,0:T(8,128)(2,1)} fusion(bf16[16,12,768]{2,1,0:T(8,128)(2,1)S(1)} %reshape.245, bf16[16,36,768]{2,1,0:T(8,128)(2,1)} %reshape.244), kind=kLoop, calls=%fused_computation.33 | loop fusion | flops 2359296 | bytes 2359296 | tf_op jit(solution)/shard_map/concatenate | solution.py:94
  94.4 14.2 %all-to-all-done = bf16[16,96,768]{2,1,0:T(8,128)(2,1)S(1)} async-done(((bf16[16,96,768]{2,1,0:T(8,128)(2,1)}), bf16[16,96,768]{2,1,0:T(8,128)(2,1)S(1)}, u32[]{:S(2)}, u32[]{:S(2)}) %all-to-all-start) | async-done | bytes 2359328 | tf_op jit(solution)/shard_map/all_to_all | solution.py:94
  108.6 4.4 %all-to-all-start.1 = ((bf16[16,48,768]{2,1,0:T(8,128)(2,1)}), bf16[16,48,768]{2,1,0:T(8,128)(2,1)}, u32[]{:S(2)}, u32[]{:S(2)}) async-start(bf16[16,48,768]{2,1,0:T(8,128)(2,1)} %pad_maximum_fusion.1), calls=%async_computation.1 | async-start | bytes 2359296 | tf_op jit(solution)/shard_map/all_to_all | solution.py:94
  113.3 1.7 collective-permute-start.12
  115.0 2.2 %fusion.71 = f32[512,768]{1,0:T(8,128)S(1)} fusion(bf16[512,576]{0,1:T(8,128)(2,1)} %bitcast.100, bf16[576,768]{1,0:T(8,128)(2,1)} %bitcast.106), kind=kOutput, calls=%fused_computation.148 | convolution fusion | flops 452984832 | bytes 3047424 | tf_op jit(solution)/shard_map/dot_general | solution.py:31
  119.1 12.9 %all-to-all-done.1 = bf16[16,48,768]{2,1,0:T(8,128)(2,1)} async-done(((bf16[16,48,768]{2,1,0:T(8,128)(2,1)}), bf16[16,48,768]{2,1,0:T(8,128)(2,1)}, u32[]{:S(2)}, u32[]{:S(2)}) %all-to-all-start.1) | async-done | bytes 1179680 | tf_op jit(solution)/shard_map/all_to_all | solution.py:94
  132.0 1.6 broadcast_in_dim.24
  133.7 3.7 %all-to-all-start.2 = ((bf16[16,96,768]{2,1,0:T(8,128)(2,1)}), bf16[16,96,768]{2,1,0:T(8,128)(2,1)S(1)}, u32[]{:S(2)}, u32[]{:S(2)}) async-start(bf16[16,96,768]{2,1,0:T(8,128)(2,1)} %broadcast_in_dim.24), calls=%async_computation.2 | async-start | bytes 4718592 | tf_op jit(solution)/shard_map/all_to_all | solution.py:102
  137.4 1.3 fusion.16
  138.8 3.3 %collective-permute-start.10 = (bf16[256,768]{1,0:T(8,128)(2,1)S(1)}, bf16[256,768]{1,0:T(8,128)(2,1)}, u32[]{:S(2)}, u32[]{:S(2)}) collective-permute-start(bf16[256,768]{1,0:T(8,128)(2,1)S(1)} %fusion.16), channel_id=1, source_target_pairs={{0,2},{2,0},{1,3},{3,1},{4,6},{6,4},{5,7},{7,5},{8,10},{10,8},{9,1... | collective-permute-start | bytes 1179656 | tf_op jit(solution)/shard_map/ppermute | solution.py:67
  143.2 1.4 subtract_multiply_fusion
  146.7 3.7 %collective-permute-done.10 = bf16[256,768]{1,0:T(8,128)(2,1)} collective-permute-done((bf16[256,768]{1,0:T(8,128)(2,1)S(1)}, bf16[256,768]{1,0:T(8,128)(2,1)}, u32[]{:S(2)}, u32[]{:S(2)}) %collective-permute-start.10) | collective-permute-done | bytes 393248 | tf_op jit(solution)/shard_map/ppermute | solution.py:67
  150.4 2.2 %multiply_reduce_fusion.3 = (f32[768]{0:T(1024)S(1)}, f32[256]{0:T(256)}, f32[256]{0:T(256)}, f32[768]{0:T(1024)S(1)}) fusion(bf16[256,768]{1,0:T(8,128)(2,1)} %collective-permute-done.10, bf16[256,768]{1,0:T(8,128)(2,1)S(1)} %fusion.16, f32[512,768]{1,0:T(8,128)} %subtract_multiply_fusion, f32[768]{0:T(1024)S(1)} %copy-done.18), kind=kLoop, calls=%fused_computation.70 | loop fusion | flops 1964032 | bytes 1584128 | tf_op jit(solution)/shard_map/reduce_sum | solution.py:184
  153.7 1.4 stack.54
  158.5 1.6 collective-permute-start.15
  160.1 2.4 %multiply_add_fusion = f32[256,768]{1,0:T(8,128)} fusion(f32[256,768]{1,0:T(8,128)S(1)} %copy-done.4, f32[512,768]{1,0:T(8,128)} %subtract_multiply_fusion, bf16[256,768]{1,0:T(8,128)(2,1)} %collective-permute-done.10, bf16[256,768]{1,0:T(8,128)(2,1)S(1)} %fusion.16, f32[256]{0:T(256)S(1)} %broadcast_multiply_fusion.1, f32[256]{0:T(256)S(1)} %broadcast_multiply_fusion.2, ...), kind=kLoop, calls=%fused_computation.71 | loop fusion | flops 1769472 | bytes 3151872 | tf_op jit(solution)/shard_map/add | solution.py:166
  162.6 1.4 reduce_sum.216
  165.4 3.3 %collective-permute-done.13 = bf16[48,768]{1,0:T(8,128)(2,1)S(1)} collective-permute-done((bf16[48,768]{1,0:T(8,128)(2,1)S(1)}, bf16[48,768]{1,0:T(8,128)(2,1)S(1)}, u32[]{:S(2)}, u32[]{:S(2)}) %collective-permute-start.13) | collective-permute-done | bytes 73760 | tf_op jit(solution)/shard_map/ppermute | solution.py:70
  168.7 2.4 %all-to-all-done.2 = bf16[16,96,768]{2,1,0:T(8,128)(2,1)S(1)} async-done(((bf16[16,96,768]{2,1,0:T(8,128)(2,1)}), bf16[16,96,768]{2,1,0:T(8,128)(2,1)S(1)}, u32[]{:S(2)}, u32[]{:S(2)}) %all-to-all-start.2) | async-done | bytes 2359328 | tf_op jit(solution)/shard_map/all_to_all | solution.py:102
  172.2 4.6 %all-to-all-start.3 = ((bf16[16,56,768]{2,1,0:T(8,128)(2,1)}), bf16[16,56,768]{2,1,0:T(8,128)(2,1)}, u32[]{:S(2)}, u32[]{:S(2)}) async-start(bf16[16,56,768]{2,1,0:T(8,128)(2,1)} %broadcast_in_dim.25), calls=%async_computation.3 | async-start | bytes 2752512 | tf_op jit(solution)/shard_map/all_to_all | solution.py:102
  176.9 1.2 broadcast_select_fusion.3
  179.0 1.2 broadcast_select_fusion.1
  180.2 1.2 maximum_bitcast_fusion
  181.5 2.8 %fusion.57 = (f32[16,48,768]{2,1,0:T(8,128)}, f32[16,48,768]{2,1,0:T(8,128)}) fusion(bf16[16,96,768]{2,1,0:T(8,128)(2,1)S(1)} %all-to-all-done.2), kind=kLoop, calls=%fused_computation.142 | loop fusion | bytes 9437184 | tf_op jit(solution)/shard_map/slice | solution.py:211
  184.2 13.9 %all-to-all-done.3 = bf16[16,56,768]{2,1,0:T(8,128)(2,1)} async-done(((bf16[16,56,768]{2,1,0:T(8,128)(2,1)}), bf16[16,56,768]{2,1,0:T(8,128)(2,1)}, u32[]{:S(2)}, u32[]{:S(2)}) %all-to-all-start.3) | async-done | bytes 1376288 | tf_op jit(solution)/shard_map/all_to_all | solution.py:102
  200.3 1.5 slice_convert_fusion
  202.9 1.4 reshape_reshape.3
  204.3 2.0 reshape.247
  (177 shorter events, 35.5 us)
Async XLA Ops:
  0.6 31.1 %copy-start = (bf16[768,768]{1,0:T(8,128)(2,1)S(1)}, bf16[768,768]{1,0:T(8,128)(2,1)}, u32[]{:S(2)}) copy-start(bf16[768,768]{1,0:T(8,128)(2,1)} %param.25) | copy-start | bytes 3538948
  2.7 4.1 %copy-start.25 = (f32[3,64]{1,0:T(4,128)}, f32[3,64]{1,0:T(4,128)S(1)}, u32[]{:S(2)}) copy-start(f32[3,64]{1,0:T(4,128)S(1)} %get-tuple-element.53) | copy-start | bytes 2308
  2.7 8.2 %copy-start.34 = (f32[3,64]{1,0:T(4,128)}, f32[3,64]{1,0:T(4,128)S(1)}, u32[]{:S(2)}) copy-start(f32[3,64]{1,0:T(4,128)S(1)} %get-tuple-element.54) | copy-start | bytes 2308
  3.0 1.9 copy-start.8
  4.9 1.9 copy-start.21
  10.9 2.5 %copy-start.27 = (f32[3,512]{1,0:T(4,128)}, f32[3,512]{1,0:T(4,128)S(1)}, u32[]{:S(2)}) copy-start(f32[3,512]{1,0:T(4,128)S(1)} %get-tuple-element.55) | copy-start | bytes 18436
  10.9 3.2 %copy-start.13 = (bf16[192,768]{1,0:T(8,128)(2,1)S(1)}, bf16[192,768]{1,0:T(8,128)(2,1)}, u32[]{:S(2)}) copy-start(bf16[192,768]{1,0:T(8,128)(2,1)} %param.21) | copy-start | bytes 884740
  14.5 1.8 collective-permute-start
  16.4 12.8 %copy-start.30 = (f32[768]{0:T(1024)S(1)}, f32[768]{0:T(1024)}, u32[]{:S(2)}) copy-start(f32[768]{0:T(1024)} %param.22) | copy-start | bytes 9220
  16.4 12.8 %collective-permute-start.1 = (bf16[256,768]{1,0:T(8,128)(2,1)S(1)}, bf16[256,768]{1,0:T(8,128)(2,1)S(1)}, u32[]{:S(2)}, u32[]{:S(2)}) collective-permute-start(bf16[256,768]{1,0:T(8,128)(2,1)S(1)} %fusion.19), channel_id=1, source_target_pairs={{0,2},{2,0},{1,3},{3,1},{4,6},{6,4},{5,7},{7,5},{8,10},{10,8},{9,1... | collective-permute-start | bytes 1179656 | tf_op jit(solution)/shard_map/ppermute | solution.py:67
  19.9 9.8 %copy-start.17 = (f32[768]{0:T(1024)S(1)}, f32[768]{0:T(1024)}, u32[]{:S(2)}) copy-start(f32[768]{0:T(1024)} %param.23) | copy-start | bytes 9220
  19.9 9.8 %copy-start.31 = (f32[768]{0:T(1024)S(1)}, f32[768]{0:T(1024)}, u32[]{:S(2)}) copy-start(f32[768]{0:T(1024)} %param.24) | copy-start | bytes 9220
  29.7 2.1 copy-start.37
  29.9 1.8 collective-permute-start.2
  30.7 1.9 copy-start.36
  35.2 1.8 collective-permute-start.6
  36.2 5.0 %collective-permute-start.3 = (bf16[256,768]{1,0:T(8,128)(2,1)S(1)}, bf16[256,768]{1,0:T(8,128)(2,1)S(1)}, u32[]{:S(2)}, u32[]{:S(2)}) collective-permute-start(bf16[256,768]{1,0:T(8,128)(2,1)S(1)} %slice.207), channel_id=1, source_target_pairs={{0,1},{1,0},{2,3},{3,2},{4,5},{5,4},{6,7},{7,6},{8,9},{9,8},{10,11... | collective-permute-start | bytes 1179656 | tf_op jit(solution)/shard_map/ppermute | solution.py:64
  37.1 13.5 %collective-permute-start.7 = (bf16[256,768]{1,0:T(8,128)(2,1)S(1)}, bf16[256,768]{1,0:T(8,128)(2,1)S(1)}, u32[]{:S(2)}, u32[]{:S(2)}) collective-permute-start(bf16[256,768]{1,0:T(8,128)(2,1)S(1)} %fusion.17), channel_id=1, source_target_pairs={{0,2},{2,0},{1,3},{3,1},{4,6},{6,4},{5,7},{7,5},{8,10},{10,8},{9,1... | collective-permute-start | bytes 1179656 | tf_op jit(solution)/shard_map/ppermute | solution.py:67
  41.2 17.0 %copy-start.33 = (f32[768]{0:T(1024)S(1)}, f32[768]{0:T(1024)}, u32[]{:S(2)}) copy-start(f32[768]{0:T(1024)} %param.28) | copy-start | bytes 9220
  41.3 16.9 %collective-permute-start.4 = (bf16[256,768]{1,0:T(8,128)(2,1)S(1)}, bf16[256,768]{1,0:T(8,128)(2,1)S(1)}, u32[]{:S(2)}, u32[]{:S(2)}) collective-permute-start(bf16[256,768]{1,0:T(8,128)(2,1)S(1)} %fusion.18), channel_id=1, source_target_pairs={{0,2},{2,0},{1,3},{3,1},{4,6},{6,4},{5,7},{7,5},{8,10},{10,8},{9,1... | collective-permute-start | bytes 1179656 | tf_op jit(solution)/shard_map/ppermute | solution.py:67
  60.4 10.4 %collective-permute-start.8 = (bf16[256,768]{1,0:T(8,128)(2,1)S(1)}, bf16[256,768]{1,0:T(8,128)(2,1)}, u32[]{:S(2)}, u32[]{:S(2)}) collective-permute-start(bf16[256,768]{1,0:T(8,128)(2,1)S(1)} %get-tuple-element.40), channel_id=1, source_target_pairs={{0,1},{1,0},{2,3},{3,2},{4,5},{5,4},{6,7},{7,6},{8,9},{9,8},{10,11... | collective-permute-start | bytes 1179656 | tf_op jit(solution)/shard_map/ppermute | solution.py:64
  62.8 45.7 %all-to-all-start = ((bf16[16,96,768]{2,1,0:T(8,128)(2,1)}), bf16[16,96,768]{2,1,0:T(8,128)(2,1)S(1)}, u32[]{:S(2)}, u32[]{:S(2)}) async-start(bf16[16,96,768]{2,1,0:T(8,128)(2,1)} %pad_maximum_fusion), calls=%async_computation | async-start | bytes 4718592 | tf_op jit(solution)/shard_map/all_to_all | solution.py:94
  72.3 5.2 %copy-start.40 = (bf16[512,192]{0,1:T(8,128)(2,1)}, bf16[512,192]{0,1:T(8,128)(2,1)S(1)}, u32[]{:S(2)}) copy-start(bf16[512,192]{0,1:T(8,128)(2,1)S(1)} %convolution_convert_fusion.6) | copy-start | bytes 589828
  72.3 5.2 %copy-start.16 = (bf16[3,64,512]{2,1,0:T(8,128)(2,1)S(1)}, bf16[3,64,512]{2,1,0:T(8,128)(2,1)}, u32[]{:S(2)}) copy-start(bf16[3,64,512]{2,1,0:T(8,128)(2,1)} %copy-done.15) | copy-start | bytes 589828
  80.6 3.4 %copy-start.12 = (f32[512,3,3,64]{0,3,2,1:T(8,128)S(1)}, f32[512,3,3,64]{0,3,2,1:T(8,128)}, u32[]{:S(2)}) copy-start(f32[512,3,3,64]{0,3,2,1:T(8,128)} %fusion.21) | copy-start | bytes 3538948
  80.6 3.8 %copy-start.26 = (f32[3,64]{1,0:T(4,128)S(1)}, f32[3,64]{1,0:T(4,128)}, u32[]{:S(2)}) copy-start(f32[3,64]{1,0:T(4,128)} %copy-done.25) | copy-start | bytes 2308
  84.0 2.0 copy-start.3
  84.5 2.2 %copy-start.6 = (bf16[512,3,1,64]{0,3,1,2:T(8,128)(2,1)}, bf16[512,3,1,64]{0,3,1,2:T(8,128)(2,1)S(1)}, u32[]{:S(2)}) copy-start(bf16[512,3,1,64]{0,3,1,2:T(8,128)(2,1)S(1)} %fusion.15) | copy-start | bytes 589828
  108.6 23.5 %all-to-all-start.1 = ((bf16[16,48,768]{2,1,0:T(8,128)(2,1)}), bf16[16,48,768]{2,1,0:T(8,128)(2,1)}, u32[]{:S(2)}, u32[]{:S(2)}) async-start(bf16[16,48,768]{2,1,0:T(8,128)(2,1)} %pad_maximum_fusion.1), calls=%async_computation.1 | async-start | bytes 2359296 | tf_op jit(solution)/shard_map/all_to_all | solution.py:94
  113.3 5.8 %collective-permute-start.12 = (bf16[96,768]{1,0:T(8,128)(2,1)S(1)}, bf16[96,768]{1,0:T(8,128)(2,1)S(1)}, u32[]{:S(2)}, u32[]{:S(2)}) collective-permute-start(bf16[96,768]{1,0:T(8,128)(2,1)S(1)} %reduce_sum.215), channel_id=1, source_target_pairs={{0,4},{4,0},{1,5},{5,1},{2,6},{6,2},{3,7},{7,3},{8,12},{12,8},{9,1... | collective-permute-start | bytes 442376 | tf_op jit(solution)/shard_map/ppermute | solution.py:70
  119.1 18.4 %collective-permute-start.9 = (bf16[256,768]{1,0:T(8,128)(2,1)}, bf16[256,768]{1,0:T(8,128)(2,1)}, u32[]{:S(2)}, u32[]{:S(2)}) collective-permute-start(bf16[256,768]{1,0:T(8,128)(2,1)} %slice.205), channel_id=1, source_target_pairs={{0,1},{1,0},{2,3},{3,2},{4,5},{5,4},{6,7},{7,6},{8,9},{9,8},{10,11... | collective-permute-start | bytes 1179656 | tf_op jit(solution)/shard_map/ppermute | solution.py:64
  133.7 37.4 %all-to-all-start.2 = ((bf16[16,96,768]{2,1,0:T(8,128)(2,1)}), bf16[16,96,768]{2,1,0:T(8,128)(2,1)S(1)}, u32[]{:S(2)}, u32[]{:S(2)}) async-start(bf16[16,96,768]{2,1,0:T(8,128)(2,1)} %broadcast_in_dim.24), calls=%async_computation.2 | async-start | bytes 4718592 | tf_op jit(solution)/shard_map/all_to_all | solution.py:102
  137.4 4.7 %copy-start.23 = (f32[512]{0:T(512)S(1)}, f32[512]{0:T(512)}, u32[]{:S(2)}) copy-start(f32[512]{0:T(512)} %copy-done.21) | copy-start | bytes 6148
  138.7 5.9 %copy-start.32 = (f32[768]{0:T(1024)S(1)}, f32[768]{0:T(1024)}, u32[]{:S(2)}) copy-start(f32[768]{0:T(1024)} %get-tuple-element.61) | copy-start | bytes 9220
  138.8 5.9 %copy-start.19 = (f32[768]{0:T(1024)S(1)}, f32[768]{0:T(1024)}, u32[]{:S(2)}) copy-start(f32[768]{0:T(1024)} %get-tuple-element.24) | copy-start | bytes 9220
  138.8 7.1 %copy-start.20 = (f32[768]{0:T(1024)S(1)}, f32[768]{0:T(1024)}, u32[]{:S(2)}) copy-start(f32[768]{0:T(1024)} %get-tuple-element.39) | copy-start | bytes 9220
  138.8 7.6 %copy-start.7 = (bf16[512,3,1,64]{0,3,1,2:T(8,128)(2,1)S(1)}, bf16[512,3,1,64]{0,3,1,2:T(8,128)(2,1)}, u32[]{:S(2)}) copy-start(bf16[512,3,1,64]{0,3,1,2:T(8,128)(2,1)} %copy-done.6) | copy-start | bytes 589828
  138.8 7.6 %copy-start.10 = (bf16[512,3,1,64]{0,3,1,2:T(8,128)(2,1)S(1)}, bf16[512,3,1,64]{0,3,1,2:T(8,128)(2,1)}, u32[]{:S(2)}) copy-start(bf16[512,3,1,64]{0,3,1,2:T(8,128)(2,1)} %copy-done.9) | copy-start | bytes 589828
  138.8 11.6 %collective-permute-start.10 = (bf16[256,768]{1,0:T(8,128)(2,1)S(1)}, bf16[256,768]{1,0:T(8,128)(2,1)}, u32[]{:S(2)}, u32[]{:S(2)}) collective-permute-start(bf16[256,768]{1,0:T(8,128)(2,1)S(1)} %fusion.16), channel_id=1, source_target_pairs={{0,2},{2,0},{1,3},{3,1},{4,6},{6,4},{5,7},{7,5},{8,10},{10,8},{9,1... | collective-permute-start | bytes 1179656 | tf_op jit(solution)/shard_map/ppermute | solution.py:67
  144.6 15.4 %copy-start.4 = (f32[256,768]{1,0:T(8,128)S(1)}, f32[256,768]{1,0:T(8,128)}, u32[]{:S(2)}) copy-start(f32[256,768]{1,0:T(8,128)} %get-tuple-element.41) | copy-start | bytes 2359300
  146.4 30.5 %collective-permute-start.5 = (bf16[256,768]{1,0:T(8,128)(2,1)}, bf16[256,768]{1,0:T(8,128)(2,1)}, u32[]{:S(2)}, u32[]{:S(2)}) collective-permute-start(bf16[256,768]{1,0:T(8,128)(2,1)} %get-tuple-element.48), channel_id=1, source_target_pairs={{0,1},{1,0},{2,3},{3,2},{4,5},{5,4},{6,7},{7,6},{8,9},{9,8},{10,11... | collective-permute-start | bytes 1179656 | tf_op jit(solution)/shard_map/ppermute | solution.py:64
  146.6 7.1 %copy-start.24 = (f32[1,768]{1,0:T(1,128)S(1)}, f32[1,768]{1,0:T(1,128)}, u32[]{:S(2)}) copy-start(f32[1,768]{1,0:T(1,128)} %stack.50) | copy-start | bytes 9220
  155.1 1.4 collective-permute-start.14
  158.5 6.1 %collective-permute-start.15 = (f32[8,768]{1,0:T(8,128)}, f32[8,768]{1,0:T(8,128)}, u32[]{:S(2)}, u32[]{:S(2)}) collective-permute-start(f32[8,768]{1,0:T(8,128)} %pad_maximum_fusion.14), channel_id=1, source_target_pairs={{0,4},{4,0},{1,5},{5,1},{2,6},{6,2},{3,7},{7,3},{8,12},{12,8},{9,1... | collective-permute-start | bytes 73736 | tf_op jit(solution)/shard_map/ppermute | solution.py:70
  162.5 16.5 %collective-permute-start.11 = (f32[256,768]{1,0:T(8,128)}, f32[256,768]{1,0:T(8,128)S(1)}, u32[]{:S(2)}, u32[]{:S(2)}) collective-permute-start(f32[256,768]{1,0:T(8,128)} %multiply_add_fusion), channel_id=1, source_target_pairs={{0,1},{1,0},{2,3},{3,2},{4,5},{5,4},{6,7},{7,6},{8,9},{9,8},{10,11... | collective-permute-start | bytes 2359304 | tf_op jit(solution)/shard_map/ppermute | solution.py:64
  164.1 4.6 %collective-permute-start.13 = (bf16[48,768]{1,0:T(8,128)(2,1)S(1)}, bf16[48,768]{1,0:T(8,128)(2,1)S(1)}, u32[]{:S(2)}, u32[]{:S(2)}) collective-permute-start(bf16[48,768]{1,0:T(8,128)(2,1)S(1)} %reduce_sum.216), channel_id=1, source_target_pairs={{0,4},{4,0},{1,5},{5,1},{2,6},{6,2},{3,7},{7,3},{8,12},{12,8},{9,1... | collective-permute-start | bytes 221192 | tf_op jit(solution)/shard_map/ppermute | solution.py:70
  172.2 25.9 %all-to-all-start.3 = ((bf16[16,56,768]{2,1,0:T(8,128)(2,1)}), bf16[16,56,768]{2,1,0:T(8,128)(2,1)}, u32[]{:S(2)}, u32[]{:S(2)}) async-start(bf16[16,56,768]{2,1,0:T(8,128)(2,1)} %broadcast_in_dim.25), calls=%async_computation.3 | async-start | bytes 2752512 | tf_op jit(solution)/shard_map/all_to_all | solution.py:102
  202.9 3.4 %copy-start.1 = (bf16[768,768]{1,0:T(8,128)(2,1)S(1)}, bf16[768,768]{1,0:T(8,128)(2,1)}, u32[]{:S(2)}) copy-start(bf16[768,768]{1,0:T(8,128)(2,1)} %param.25) | copy-start | bytes 3538948
  (14 other events, 18.0 us)

commit v2 on v1

v2 whole, which is shorter than its diff:
```python
import jax
import jax.numpy as jnp
from jax import lax
from jax.experimental import pallas as pl
from jax.experimental.pallas import tpu as pltpu
from jax.sharding import Mesh
from jax.sharding import PartitionSpec as P

EPSILON = 1e-05
MASKED = -1e30
BF = jnp.bfloat16
F32 = jnp.float32
PLANE = ("z", "x")
DP = ("z", "x", "near")
MP = ("far", "core")
SMEM = pltpu.SMEM


def dot(left_side, right_side, left_dim=1, right_dim=0):
    return lax.dot_general(
        left_side, right_side, (((left_dim,), (right_dim,)), ((), ())), preferred_element_type=F32
    )


def call(body, outs, scratch=(), place=pltpu.VMEM, limit=12 << 20, cost=1000):
    def run(*arrays):
        space = pl.BlockSpec() if place is None else pl.BlockSpec(memory_space=place)
        return pl.pallas_call(
            body,
            out_shape=[jax.ShapeDtypeStruct(s, d) for s, d in outs],
            in_specs=[space] * len(arrays),
            out_specs=[space] * len(outs),
            scratch_shapes=[pltpu.VMEM(*s) if isinstance(s, tuple) else s for s in scratch],
            cost_estimate=pl.CostEstimate(flops=cost, bytes_accessed=1000, transcendentals=0),
            compiler_params=pltpu.CompilerParams(vmem_limit_bytes=limit),
            name=body.__name__,
        )(*arrays)

    return run


def line(ref):
    return ref[...].reshape(1, -1)


def norm_parts(values_in):
    center = values_in - jnp.mean(values_in, axis=-1, keepdims=True)
    spread = jnp.mean(center * center, axis=-1, keepdims=True)
    inverse = lax.rsqrt(spread + EPSILON)
    return center * inverse, inverse


def norm_back(grad, xhat, inverse, gain):
    scaled = grad * gain
    centre = jnp.mean(scaled, axis=-1, keepdims=True)
    along = jnp.mean(scaled * xhat, axis=-1, keepdims=True)
    return inverse * (scaled - centre - xhat * along)


def half_at(which, half):
    core = lax.axis_index("core")
    return pl.multiple_of((core if which == 0 else 1 - core) * half, half)


def fold(rows):
    return jnp.sum(rows, axis=0, keepdims=True)


def attend_kernel(
    lens_ref,
    tok_ref,
    gain_ref,
    shift_ref,
    w_ref,
    bias_ref,
    out_ref,
    normed_out,
    qkv_out,
    probs_out,
    ctx_out,
    own_out,
    other_out,
    normed_ref,
    qkv_ref,
    probs_ref,
    ctx_ref,
    own_ref,
    other_ref,
    lens_at,
    tok_at,
    gain_at,
    shift_at,
    w_at,
    bias_at,
    out_at,
    semaphores,
):
    length, features = tok_ref.shape
    half = length // 2
    heads = bias_ref.shape[0]
    size = bias_ref.shape[1] // 2
    copies = []

    def fetch(source, target):
        copies.append(pltpu.make_async_copy(source, target, semaphores.at[len(copies)]))
        copies[-1].start()
        return copies[-1]

    piece = half // 2
    pieces = []
    for which in range(2):
        for part in range(2):
            start = half_at(which, half) + part * piece
            at = which * half + part * piece
            pieces.append(fetch(tok_ref.at[pl.ds(start, piece)], tok_at.at[pl.ds(at, piece)]))
    norms = [fetch(gain_ref, gain_at), fetch(shift_ref, shift_at)]
    weights = []
    for head in range(heads):
        rows = pl.ds(head * 3 * size, 3 * size)
        weights.append(fetch(w_ref.at[rows], w_at.at[rows]))
    bias_copy, lens_copy = fetch(bias_ref, bias_at), fetch(lens_ref, lens_at)
    out_copy = fetch(out_ref, out_at)
    for copy in norms:
        copy.wait()
    step = 64
    for index, copy in enumerate(pieces):
        copy.wait()
        for first in range(index * piece, (index + 1) * piece, step):
            xhat, _ = norm_parts(tok_at[first : first + step, :].astype(F32))
            normed_ref[first : first + step, :] = (xhat * line(gain_at) + line(shift_at)).astype(BF)
    leaving = [fetch(normed_ref, normed_out)]
    bias_copy.wait()
    lens_copy.wait()
    lens_ref, bias_ref, w_ref = lens_at, bias_at, w_at

    diagonal = lax.broadcasted_iota(jnp.int32, (2 * size, 2 * size), 0) == (
        lax.broadcasted_iota(jnp.int32, (2 * size, 2 * size), 1)
    )
    for head in range(heads):
        base = head * 3 * size
        column = jnp.sum(
            jnp.where(diagonal, bias_ref[head : head + 1, :], 0.0), axis=1, keepdims=True
        )
        weights[head].wait()
        projected = dot(w_ref[base : base + 3 * size, :], normed_ref[...], 1, 1)
        qkv_ref[base : base + size, :] = (projected[:size] + column[:size]).astype(BF)
        qkv_ref[base + size : base + 2 * size, :] = projected[size : 2 * size].astype(BF)
        qkv_ref[base + 2 * size : base + 3 * size, :] = (
            projected[2 * size :] + column[size:]
        ).astype(BF)
    leaving.append(fetch(qkv_ref, qkv_out))

    docs = lens_ref.shape[1]
    ends = [lens_ref[0, 0]]
    for doc in range(1, docs):
        ends.append(ends[-1] + lens_ref[0, doc])

    def numbers(shape, dim, first):
        place = lax.broadcasted_iota(jnp.int32, shape, dim) + first + lax.axis_index("core") * half
        place = jnp.where(place >= length, place - length, place)
        number = jnp.zeros(shape, jnp.int32)
        for end in ends:
            number += (place >= end).astype(jnp.int32)
        return jnp.where(number >= docs, docs + place, number)

    key_docs = numbers((1, length), 1, 0)
    block = 128
    query_docs = [numbers((block, 1), 0, first) for first in range(0, length, block)]
    scale = size ** (-0.5)
    for head in range(heads):
        base = head * 3 * size
        keys = qkv_ref[base + size : base + 2 * size, :]
        for index in range(length // block):
            rows = slice(index * block, (index + 1) * block)
            scores = dot(qkv_ref[base : base + size, rows], keys, 0, 0) * scale
            scores = jnp.where(query_docs[index] == key_docs, scores, MASKED)
            expo = jnp.exp(scores - jnp.max(scores, axis=-1, keepdims=True))
            probs = expo * (1.0 / jnp.sum(expo, axis=-1, keepdims=True))
            probs_ref[head, rows, :] = probs.astype(BF)
        leaving.append(fetch(probs_ref.at[head], probs_out.at[head]))
        values = qkv_ref[base + 2 * size : base + 3 * size, :]
        ctx_ref[head * size : (head + 1) * size, :] = dot(values, probs_ref[head], 1, 1).astype(BF)
    leaving.append(fetch(ctx_ref, ctx_out))
    out_copy.wait()
    other_ref[...] = dot(ctx_ref[:, half:], out_at[...], 0, 0).astype(BF)
    leaving.append(fetch(other_ref, other_out))
    own_ref[...] = dot(ctx_ref[:, :half], out_at[...], 0, 0)
    leaving.append(fetch(own_ref, own_out))
    for copy in leaving:
        copy.wait()


def resid_kernel(tok_ref, pair_ref, come_ref, bias_ref, gain_ref, shift_ref, normed_ref, resid_ref):
    half = pair_ref.shape[0]
    start = half_at(0, half)
    step = 64
    for first in range(0, half, step):
        rows = slice(first, first + step)
        resid = (
            tok_ref[pl.ds(start + first, step), :].astype(F32)
            + (pair_ref[rows, :].astype(F32) + come_ref[rows, :].astype(F32))
            + line(bias_ref)
        )
        resid_ref[rows, :] = resid
        xhat, _ = norm_parts(resid)
        normed_ref[rows, :] = (xhat * line(gain_ref) + line(shift_ref)).astype(BF)


def expert_kernel(
    mine_ref,
    theirs_ref,
    up_ref,
    bias_ref,
    down_ref,
    cot_ref,
    hidden_ref,
    grad_ref,
    own_ref,
    other_ref,
    sum_ref,
):
    half = mine_ref.shape[0]
    step = 128
    total = jnp.zeros((1, up_ref.shape[1]), F32)
    for which in (1, 0):
        start = half_at(which, half)
        for first in range(0, half, step):
            rows = slice(first, first + step)
            normed = (theirs_ref if which else mine_ref)[rows, :]
            pre = dot(normed, up_ref[...]) + line(bias_ref)
            back = dot(cot_ref[pl.ds(start + first, step), :], down_ref[...], 1, 1)
            cumulative = 0.5 * (1.0 + lax.erf(pre * 0.7071067811865476))
            at = slice(which * half + first, which * half + first + step)
            hidden_ref[at, :] = (pre * cumulative).astype(BF)
            slope = cumulative + pre * (jnp.exp(-0.5 * pre * pre) * 0.3989422804014327)
            grad = (back * slope).astype(BF)
            grad_ref[at, :] = grad
            total += fold(grad.astype(F32))
            part = dot(grad, up_ref[...], 1, 1)
            if which:
                other_ref[rows, :] = part.astype(BF)
            else:
                own_ref[rows, :] = part
    sum_ref[...] = total


def expert_weights_kernel(hidden_ref, cot_ref, mine_ref, theirs_ref, grad_ref, chunk_ref):
    half = mine_ref.shape[0]
    count, pair, _ = chunk_ref.shape
    each = pair // 2
    cot_mine = cot_ref[pl.ds(half_at(0, half), half), :]
    cot_theirs = cot_ref[pl.ds(half_at(1, half), half), :]
    some = 4
    for first in range(0, count, some):
        columns = slice(first * each, (first + some) * each)
        down = dot(hidden_ref[:half, columns], cot_mine, 0, 0)
        down += dot(hidden_ref[half:, columns], cot_theirs, 0, 0)
        chunk_ref[first : first + some, :each, :] = down.astype(BF).reshape(some, each, -1)
        up = dot(mine_ref[:, columns], grad_ref[:half, :], 0, 0)
        up += dot(theirs_ref[:, columns], grad_ref[half:, :], 0, 0)
        chunk_ref[first : first + some, each:, :] = up.astype(BF).reshape(some, each, -1)


def second_norm_kernel(
    pair_ref, come_ref, resid_ref, gain_ref, cot_ref, low_ref, grad_ref, rows_ref
):
    half = resid_ref.shape[0]
    start = half_at(0, half)
    step = 64
    gains, shifts, outs, downs = 0.0, 0.0, 0.0, 0.0
    for first in range(0, half, step):
        rows = slice(first, first + step)
        xhat, inverse = norm_parts(resid_ref[rows, :])
        grad = pair_ref[rows, :].astype(F32) + come_ref[rows, :].astype(F32)
        cot = cot_ref[pl.ds(start + first, step), :].astype(F32)
        back = cot + norm_back(grad, xhat, inverse, line(gain_ref))
        grad_ref[rows, :] = back
        low = back.astype(BF)
        low_ref[rows, :] = low
        gains += fold(grad * xhat)
        shifts += fold(grad)
        outs += fold(low.astype(F32))
        downs += fold(cot)
    rows_ref[...] = jnp.zeros_like(rows_ref)
    for index, value in ((2, gains), (3, shifts), (4, outs), (5, downs)):
        rows_ref[index : index + 1, :] = value


def attend_back_kernel(
    mine_ref,
    theirs_ref,
    out_ref,
    probs_ref,
    qkv_ref,
    ctx_ref,
    normed_ref,
    grads_ref,
    chunk_ref,
    sums_ref,
    back_ref,
    score_ref,
):
    heads, length, _ = probs_ref.shape
    half = length // 2
    size = ctx_ref.shape[0] // heads
    scale = size ** (-0.5)
    back_ref[:, :half] = dot(out_ref[...], mine_ref[...], 1, 1).astype(BF)
    back_ref[:, half:] = dot(out_ref[...], theirs_ref[...], 1, 1).astype(BF)
    block = 128
    for head in range(heads):
        base = head * 3 * size
        own = slice(head * size, (head + 1) * size)
        queries = qkv_ref[base : base + size, :]
        keys = qkv_ref[base + size : base + 2 * size, :]
        values = qkv_ref[base + 2 * size : base + 3 * size, :]
        for first in range(0, length, block):
            rows = slice(first, first + block)
            probs = probs_ref[head, rows, :].astype(F32)
            probs_grad = dot(back_ref[own, rows], values, 0, 0)
            centre = jnp.sum(probs_grad * probs, axis=-1, keepdims=True)
            score_ref[rows, :] = (probs * (probs_grad - centre)).astype(BF)
        score_grad = score_ref[...]
        grads_ref[base : base + size, :] = (dot(keys, score_grad, 1, 1) * scale).astype(BF)
        grads_ref[base + size : base + 2 * size, :] = (dot(queries, score_grad) * scale).astype(BF)
        grads_ref[base + 2 * size : base + 3 * size, :] = dot(
            back_ref[own, :], probs_ref[head]
        ).astype(BF)
    width = grads_ref.shape[0]
    each = chunk_ref.shape[1]
    some = 4
    for first in range(0, width, some * each):
        grad = dot(grads_ref[first : first + some * each, :], normed_ref[...]).astype(BF)
        at = first // each
        chunk_ref[at : at + some] = grad.reshape(some, each, -1)
    outs = dot(ctx_ref[:, :half], mine_ref[...]) + dot(ctx_ref[:, half:], theirs_ref[...])
    chunk_ref[width // each :] = outs.astype(BF).reshape(-1, each, outs.shape[1])
    sums_ref[...] = dot(jnp.ones((8, length), BF), grads_ref[...], 1, 1)


def parts_kernel(grads_ref, w_ref, hidden_ref, down_ref, own_ref, other_ref):
    half = own_ref.shape[0] // 2
    other_ref[:half, :] = dot(grads_ref[:, half:], w_ref[...], 0, 0).astype(BF)
    other_ref[half:, :] = dot(hidden_ref[half:, :], down_ref[...]).astype(BF)
    own_ref[:half, :] = dot(grads_ref[:, :half], w_ref[...], 0, 0)
    own_ref[half:, :] = dot(hidden_ref[:half, :], down_ref[...])


def first_norm_kernel(
    tok_ref, pair_ref, come_ref, gain_ref, bias_ref, back_ref, resid_ref, rows_ref, grad_ref, mixed_ref
):
    half = mixed_ref.shape[0]
    start = half_at(0, half)
    step = 64
    gains, shifts = 0.0, 0.0
    for first in range(0, half, step):
        rows = slice(first, first + step)
        below = slice(half + first, half + first + step)
        xhat, inverse = norm_parts(tok_ref[pl.ds(start + first, step), :].astype(F32))
        grad = pair_ref[rows, :].astype(F32) + come_ref[rows, :].astype(F32)
        grad_ref[rows, :] = back_ref[rows, :] + norm_back(grad, xhat, inverse, line(gain_ref))
        out = pair_ref[below, :].astype(F32) + come_ref[below, :].astype(F32)
        mixed_ref[rows, :] = (resid_ref[rows, :] + out + line(bias_ref)).astype(BF)
        gains += fold(grad * xhat)
        shifts += fold(grad)
    grad_ref[half:, :] = rows_ref[...]
    grad_ref[half : half + 1, :] = gains
    grad_ref[half + 1 : half + 2, :] = shifts


def mixed_order_kernel(mine_ref, theirs_ref, row_ref):
    half = mine_ref.shape[0]
    row_ref[pl.ds(half_at(0, half), half), :] = mine_ref[...]
    row_ref[pl.ds(half_at(1, half), half), :] = theirs_ref[...]


def token_order_kernel(mine_ref, theirs_ref, up_ref, qkv_ref, row_ref, whole_ref):
    half = row_ref.shape[0] // 2
    row_ref[pl.ds(half_at(0, half), half), :] = mine_ref[:half, :]
    row_ref[pl.ds(half_at(1, half), half), :] = theirs_ref[:half, :]
    whole_ref[...] = mine_ref[half:, :] + theirs_ref[half:, :]
    whole_ref[6:7, :] = up_ref[...]
    whole_ref[7:8, : qkv_ref.shape[1]] = qkv_ref[0:1, :]


def pair_kernel(own_ref, come_ref, pair_ref):
    pair_ref[...] = (own_ref[...] + come_ref[...].astype(F32)).astype(BF)


def expert_finish_kernel(pair_ref, come_ref, a_ref, b_ref):
    split = a_ref.shape[0]
    a_ref[...] = pair_ref[:split, :] + come_ref[:split, :]
    b_ref[...] = pair_ref[split:, :] + come_ref[split:, :]


def total_kernel(parts_ref, total_ref):
    step = 16
    for first in range(0, total_ref.shape[0], step):
        rows = slice(first, first + step)
        total = parts_ref[0, rows, :].astype(F32)
        for part in range(1, parts_ref.shape[0]):
            total += parts_ref[part, rows, :].astype(F32)
        total_ref[rows, :] = total.astype(BF)


def attend_total_kernel(parts_ref, whole_ref, pair_ref):
    count = parts_ref.shape[1]
    total_kernel(parts_ref, pair_ref.at[:count])
    vectors = whole_ref[...]
    pair_ref[count:, :] = jnp.concatenate((vectors, jnp.zeros_like(vectors))).astype(BF)


def attend_finish_kernel(pair_ref, come_ref, total_ref):
    total_ref[...] = pair_ref[...] + come_ref[...]


def place(axis, blocks, store):
    count = len(blocks)
    for shift, block in enumerate(blocks):
        store(lax.rem(lax.axis_index(axis) + count - shift, count), block)


def expert_small_kernel(*refs):
    a_blocks, b_blocks, (a_ref, b_ref) = refs[:4], refs[4:8], refs[8:]
    each = a_blocks[0].shape[0]

    def store_a(source, block):
        for copy in range(a_ref.shape[0]):
            a_ref[copy, pl.ds(pl.multiple_of(source * each, each), each), :] = block[...]

    def store_b(source, block):
        b_ref[pl.ds(pl.multiple_of(source * each, each), each), :] = block[...]

    place("z", a_blocks, store_a)
    place("x", b_blocks, store_b)


def expert_last_kernel(parts_ref, *refs):
    blocks, (down_ref, up_ref) = refs[:4], refs[4:]
    planes = parts_ref.shape[0]
    rows = blocks[0].shape[0]
    each = rows // planes
    for x in range(planes):
        for z in range(planes):
            at = (z * planes + x) * each
            down_ref[at : at + each, :] = parts_ref[x, z * each : (z + 1) * each, :].astype(F32)

    def store(source, block):
        up_ref[pl.ds(pl.multiple_of(source * rows, rows), rows), :] = block[...].astype(F32)

    place("z", blocks, store)


def attend_small_kernel(*refs):
    blocks, (copies_ref, keep_ref) = refs[:4], refs[4:]
    each = blocks[0].shape[0] - keep_ref.shape[1]
    planes = keep_ref.shape[0]

    def store(source, block):
        keep_ref[source] = block[each:, :].astype(F32)
        for copy in range(planes):
            copies_ref[copy, pl.ds(pl.multiple_of(source * each, each), each), :] = block[:each, :]

    place("z", blocks, store)
    total = keep_ref[0]
    for source in range(1, planes):
        total += keep_ref[source]
    for copy in range(planes):
        copies_ref[copy, planes * each :, :] = total.astype(BF)


def attend_last_kernel(parts_ref, qkv_ref, out_ref, qv_ref, *vector_refs):
    planes = parts_ref.shape[0]
    each = (parts_ref.shape[1] - 16) // planes
    width = qkv_ref.shape[0]
    for x in range(planes):
        for z in range(planes):
            rows = parts_ref[x, z * each : (z + 1) * each, :].astype(F32)
            at = (z * planes + x) * each
            if at < width:
                qkv_ref[at : at + each, :] = rows
            else:
                out_ref[at - width : at - width + each, :] = rows
    total = parts_ref[0, planes * each :, :].astype(F32)
    for x in range(1, planes):
        total += parts_ref[x, planes * each :, :].astype(F32)
    for index, vector_ref in enumerate(vector_refs):
        vector_ref[...] = total[index]
    heads, double = qv_ref.shape
    size = double // 2
    for head in range(heads):
        base = 3 * head * size
        qv_ref[head : head + 1, :size] = total[7:8, base : base + size]
        qv_ref[head : head + 1, size:] = total[7:8, base + 2 * size : base + 3 * size]


def shards(
    tokens,
    segment_lens,
    norm1_gain,
    norm1_shift,
    qkv_weight,
    qv_bias,
    out_weight,
    out_bias,
    norm2_gain,
    norm2_shift,
    up_weight,
    up_bias,
    down_weight,
    down_bias,
    cotangent,
):
    length, features = tokens.shape[1:]
    heads = qkv_weight.shape[1]
    size = qkv_weight.shape[2] // 3
    width = heads * 3 * size
    units = up_weight.shape[1]
    half = length // 2
    plane = lax.axis_size(PLANE)
    side = lax.axis_size("x")
    tok, cot = tokens[0], cotangent[0]
    qkv_rows = qkv_weight.transpose(1, 2, 0).reshape(width, features)

    def core_swap(array_in):
        return lax.ppermute(array_in, "core", [(0, 1), (1, 0)])

    def chip_swap(array_in):
        return lax.ppermute(array_in, "far", [(0, 1), (1, 0)])

    def near_swap(array_in):
        return lax.ppermute(array_in, "near", [(0, 1), (1, 0)])

    def add_pair(own, other):
        return call(pair_kernel, ((other.shape, BF),))(own, core_swap(other))[0]

    def scatter(chunks):
        return lax.all_to_all(chunks, PLANE, 0, 0, tiled=True)

    def plane_sum(received):
        return call(total_kernel, ((received.shape[1:], BF),))(received)[0]

    def along(block, axis):
        moves = [[(i, (i + shift) % side) for i in range(side)] for shift in range(1, side)]
        far, near, back = (lax.ppermute(block, axis, moves[i]) for i in (1, 0, 2))
        return (block, near, far, back)

    def spread(copies):
        return lax.all_to_all(copies, "x", 0, 0, tiled=True)

    half_low, half_full = ((half, features), BF), ((half, features), F32)
    row_low, row_full = ((length, features), BF), ((length, features), F32)
    rows_full = ((8, features), F32)
    count = heads * size

    outs = (
        row_low,
        ((width, length), BF),
        ((heads, length, length), BF),
        ((count, length), BF),
        half_full,
        half_low,
    )
    staged = (
        pltpu.SMEM(segment_lens.shape, segment_lens.dtype),
        row_low,
        ((features,), F32),
        ((features,), F32),
        ((width, features), BF),
        (qv_bias.shape, F32),
        (out_weight.shape, BF),
        pltpu.SemaphoreType.DMA((14 + 2 * heads,)),
    )
    normed_one, qkv, probs, context, own, other = call(
        attend_kernel, outs, outs + staged, pltpu.HBM, 60 << 20
    )(segment_lens, tok, norm1_gain, norm1_shift, qkv_rows, qv_bias, out_weight)
    pair = add_pair(own, other)
    normed_mine, resid = call(resid_kernel, (half_low, half_full))(
        tok, pair, chip_swap(pair), out_bias, norm2_gain, norm2_shift
    )
    normed_theirs = core_swap(normed_mine)

    hidden, up_grad, own, other, up_sums = call(
        expert_kernel,
        (((length, units), BF), ((length, units), BF), half_full, half_low, ((1, units), F32)),
    )(normed_mine, normed_theirs, up_weight, up_bias, down_weight, cot)
    pair = add_pair(own, other)
    pair, hidden = lax.optimization_barrier((pair, hidden))
    (chunks,) = call(
        expert_weights_kernel,
        (((plane, (units + features) // plane, features), BF),),
        cost=20_000_000_000,
    )(hidden, cot, normed_mine, normed_theirs, up_grad)
    come = chip_swap(pair)
    expert_parts = scatter(chunks)
    low_mine, resid_grad, sums = call(second_norm_kernel, (half_low, half_full, rows_full))(
        pair, come, resid, norm2_gain, cot
    )
    low_theirs = core_swap(low_mine)

    qkv_grad, chunks, qkv_sums = call(
        attend_back_kernel,
        (((width, length), BF), ((plane, (width + count) // plane, features), BF), ((8, width), F32)),
        (((count, length), BF), ((length, length), BF)),
    )(low_mine, low_theirs, out_weight, probs, qkv, context, normed_one)
    attend_parts = scatter(chunks)
    own, other = call(parts_kernel, (row_full, row_low))(qkv_grad, qkv_rows, hidden, down_weight)
    parts_pair = add_pair(own, other)

    pair = plane_sum(expert_parts)
    each = pair.shape[0] // 2
    come = near_swap(pair)
    come, parts_pair = lax.optimization_barrier((come, parts_pair))
    blocks = call(expert_finish_kernel, (((each, features), BF),) * 2)(pair, come)
    copies, block = call(
        expert_small_kernel,
        (((side, side * each, features), BF), ((side * each, features), BF)),
    )(*along(blocks[0], "z"), *along(blocks[1], "x"))
    copies, attend_parts = lax.optimization_barrier((copies, attend_parts))
    come, _ = lax.optimization_barrier((chip_swap(parts_pair), block))
    gathered = spread(copies)
    expert_blocks = along(block, "z")

    token_grad, mixed = call(first_norm_kernel, (((half + 8, features), F32), half_low))(
        tok, parts_pair, come, norm1_gain, down_bias, resid_grad, resid, sums
    )
    tokens_grad, whole = call(token_order_kernel, (row_full, rows_full))(
        token_grad, core_swap(token_grad), up_sums, qkv_sums
    )
    (mixed,) = call(mixed_order_kernel, (row_low,))(mixed, core_swap(mixed))

    rows = attend_parts.shape[1] + 16
    (pair,) = call(attend_total_kernel, (((rows, features), BF),))(attend_parts, whole)
    (block,) = call(attend_finish_kernel, (((rows, features), BF),))(pair, near_swap(pair))
    blocks, expert_blocks = lax.optimization_barrier((along(block, "z"), expert_blocks))
    (copies,) = call(
        attend_small_kernel,
        (((side, side * (rows - 16) + 16, features), BF),),
        (((side, 16, features), F32),),
    )(*blocks)
    copies, gathered = lax.optimization_barrier((copies, gathered))
    down_grad, up_weight_grad = call(
        expert_last_kernel,
        (((units, features), F32), ((features, units), F32)),
        place=None,
        limit=60 << 20,
    )(gathered, *expert_blocks)
    qkv_grads, out_weight_grad, qv_bias_grad, *vectors = call(
        attend_last_kernel,
        (((width, features), F32), ((count, features), F32), (qv_bias.shape, F32))
        + (((features,), F32),) * 7,
    )(spread(copies))
    return (
        mixed[None],
        tokens_grad[None],
        vectors[0],
        vectors[1],
        qkv_grads.reshape(heads, 3 * size, features).transpose(2, 0, 1),
        qv_bias_grad,
        out_weight_grad,
        vectors[4],
        vectors[2],
        vectors[3],
        up_weight_grad,
        vectors[6],
        down_grad,
        vectors[5],
    )


def solution(mesh):
    fine = Mesh(mesh.devices.reshape(4, 4, 2, 2, 2), ("z", "x", "near", "far", "core"))
    rows, first, features = P(DP, None, None), P(MP, None), P(MP)
    weights = (
        P(),
        P(),
        P(None, MP, None),
        first,
        first,
        P(),
        P(),
        P(),
        P(None, MP),
        features,
        first,
        P(),
    )
    return jax.shard_map(
        shards,
        mesh=fine,
        in_specs=(rows, P(DP, None)) + weights + (rows,),
        out_specs=(rows, rows) + weights,
        check_vma=False,
    )
```

time: 207 us -> 163 us (0.79)
  other arithmetic: 33.5 us -> 0 us
  Pallas kernels: 0 us -> 33.3 us
  matrix products: 28.8 us -> 0 us
  starting transfers between devices: 35.8 us -> 53.2 us
  local copies, waits for them, and re-layouts: 28.6 us -> 12.6 us
  waiting for transfers between devices: 78.3 us -> 62.5 us
    pallas_call x0 -> x21, Pallas kernels: none -> 33.3 us  [run(): pl.pallas_call(body, out_shape=[jax.ShapeDtypeStruct(s, d) for s, d in ou...]
    all_to_all x4, waiting for transfers between devices: 43.4 us -> 18.4 us  [the longest x2 9.8 us: spread(): return lax.all_to_all(copies, 'x', 0, 0, tiled=True)]
    dot_general x17 -> x0, matrix products: 24.8 us -> none  [the longest x12 15.5 us: dot(): lax.dot_general(left_side, right_side, (((left_dim,), (right_dim,)), ((),...]
    ppermute x0 -> x12, starting transfers between devices: none -> 19 us  [along(): far, near, back = (lax.ppermute(block, axis, moves[i]) for i in (1, 0, 2))]
    ppermute x0 -> x12, waiting for transfers between devices: none -> 11.3 us  [along(): far, near, back = (lax.ppermute(block, axis, moves[i]) for i in (1, 0, 2))]
    ppermute x4 -> x3, waiting for transfers between devices: 28.5 us -> 18.6 us  [chip_swap(): return lax.ppermute(array_in, 'far', [(0, 1), (1, 0)])]
    reduce_sum x13 -> x0, other arithmetic: 9.33 us -> none  [the longest x1 2.19 us: shards(): jnp.sum(normed_one_grad * xhat_half, axis=0)]
    convert_element_type x11 -> x0, other arithmetic: 7.57 us -> none  [the longest x1 3.41 us: shards(): score_grad = (probs * (probs_grad - centre)).astype(BF)]
  transfers between devices with their start and end apart: 20 -> 28, of which waited for: 12 -> 17; matrix products, arithmetic and copies ran while one was open for 28% -> 0% of each run, Pallas kernels for 0% -> 12%
where the time goes in v2:
time: 163 us
  waiting for transfers between devices  62.5 us (38%)
  starting transfers between devices  53.2 us (33%)
  Pallas kernels  33.3 us (20%)
  local copies, waits for them, and re-layouts  12.6 us (8%)
    pallas_call x21, Pallas kernels, run(): pl.pallas_call(body, out_shape=[jax.ShapeDtypeStruct(s, d) for s, d in ou...  33.3 us
    ppermute x12, starting transfers between devices, along(): far, near, back = (lax.ppermute(block, axis, moves[i]) for i in (1, 0, 2))  19 us
    ppermute x3, waiting for transfers between devices, chip_swap(): return lax.ppermute(array_in, 'far', [(0, 1), (1, 0)])  18.6 us
    unnamed x74, local copies, waits for them, and re-layouts  12.6 us
    all_to_all x2, starting transfers between devices, scatter(): return lax.all_to_all(chunks, PLANE, 0, 0, tiled=True)  12.3 us
    ppermute x12, waiting for transfers between devices, along(): far, near, back = (lax.ppermute(block, axis, moves[i]) for i in (1, 0, 2))  11.3 us
    ppermute x3, starting transfers between devices, chip_swap(): return lax.ppermute(array_in, 'far', [(0, 1), (1, 0)])  9.82 us
    all_to_all x2, waiting for transfers between devices, spread(): return lax.all_to_all(copies, 'x', 0, 0, tiled=True)  9.8 us
  transfers between devices with their start and end apart: 28, of which 17 were waited for; matrix products, arithmetic and copies ran while one was open for 0% of the time, Pallas kernels for 12%

profile of v2, /device:TPU:0, one launch (start us, length us, event | category | flops | bytes accessed | tf_op | source)
XLA Modules:
  0.0 162.7 jit_solution(8575528250160026817)
XLA Ops:
  0.7 7.0 %attend_kernel.1 = (bf16[512,768]{1,0:T(8,128)(2,1)}, bf16[576,512]{1,0:T(8,128)(2,1)}, bf16[3,512,512]{2,1,0:T(8,128)(2,1)}, bf16[192,512]{1,0:T(8,128)(2,1)}, ...) custom-call(s32[1,8]{1,0:T(1,128)} %lens_ref.1, bf16[512,768]{1,0:T(8,128)(2,1)} %bitcast.10, f32[768]{0:T(1024)} %gain_ref.7, ...), custom_call_target="tpu_custom_call" | custom-call | flops 1000 | bytes 1000 | tf_op jit(solution)/shard_map/attend_kernel/pallas_call | solution.py:28
  7.8 1.9 %collective-permute-done.come_ref = bf16[256,768]{1,0:T(8,128)(2,1)S(1)} collective-permute-done((bf16[256,768]{1,0:T(8,128)(2,1)}, bf16[256,768]{1,0:T(8,128)(2,1)S(1)}, u32[]{:S(2)}, u32[]{:S(2)}) %collective-permute-start) | collective-permute-done | bytes 393248 | tf_op jit(solution)/shard_map/ppermute | solution.py:525
  9.7 1.1 copy-done.18
  10.9 3.4 %collective-permute-start.1 = (bf16[256,768]{1,0:T(8,128)(2,1)S(1)}, bf16[256,768]{1,0:T(8,128)(2,1)S(1)}, u32[]{:S(2)}, u32[]{:S(2)}) collective-permute-start(bf16[256,768]{1,0:T(8,128)(2,1)S(1)} %pair_kernel.3.pair_ref), channel_id=1, source_target_pairs={{0,2},{2,0},{1,3},{3,1},{4,6},{6,4},{5,7},{7,5},{8,10},{10,8},{9,1... | collective-permute-start | bytes 1179656 | tf_op jit(solution)/shard_map/ppermute | solution.py:528
  14.3 9.4 %collective-permute-done.1.come_ref = bf16[256,768]{1,0:T(8,128)(2,1)S(1)} collective-permute-done((bf16[256,768]{1,0:T(8,128)(2,1)S(1)}, bf16[256,768]{1,0:T(8,128)(2,1)S(1)}, u32[]{:S(2)}, u32[]{:S(2)}) %collective-permute-start.1) | collective-permute-done | bytes 393248 | tf_op jit(solution)/shard_map/ppermute | solution.py:528
  25.0 1.7 %collective-permute-done.2.theirs_ref = bf16[256,768]{1,0:T(8,128)(2,1)S(1)} collective-permute-done((bf16[256,768]{1,0:T(8,128)(2,1)S(1)}, bf16[256,768]{1,0:T(8,128)(2,1)S(1)}, u32[]{:S(2)}, u32[]{:S(2)}) %collective-permute-start.2) | collective-permute-done | bytes 393248 | tf_op jit(solution)/shard_map/ppermute | solution.py:525
  26.7 3.7 %expert_kernel.1 = (bf16[512,768]{1,0:T(8,128)(2,1)S(1)}, bf16[512,768]{1,0:T(8,128)(2,1)S(1)}, f32[256,768]{1,0:T(8,128)S(1)}, bf16[256,768]{1,0:T(8,128)(2,1)S(1)}, f32[1,768]{1,0:T(1,128)S(1)}) custom-call(bf16[256,768]{1,0:T(8,128)(2,1)S(1)} %get-tuple-element.74.mine_ref, bf16[256,768]{1,0:T(8,128)(2,1)S(1)} %collective-permute-done.2.theirs_ref, ...), custom_call_target="tpu_custom_call" | custom-call | flops 1000 | bytes 1000 | tf_op jit(solution)/shard_map/expert_kernel/pallas_call | solution.py:28
  30.6 1.6 collective-permute-done.3.come_ref
  32.3 1.5 expert_weights_kernel.1
  33.8 1.4 copy-done.9
  35.2 7.9 %all-to-all-start = ((bf16[16,96,768]{2,1,0:T(8,128)(2,1)}), bf16[16,96,768]{2,1,0:T(8,128)(2,1)S(1)}, u32[]{:S(2)}, u32[]{:S(2)}) async-start(bf16[16,96,768]{2,1,0:T(8,128)(2,1)} %copy-done.9), calls=%async_computation | async-start | bytes 4718592 | tf_op jit(solution)/shard_map/all_to_all | solution.py:537
  43.1 3.3 %collective-permute-start.5 = (bf16[256,768]{1,0:T(8,128)(2,1)S(1)}, bf16[256,768]{1,0:T(8,128)(2,1)S(1)}, u32[]{:S(2)}, u32[]{:S(2)}) collective-permute-start(bf16[256,768]{1,0:T(8,128)(2,1)S(1)} %pair_kernel.4.pair_ref), channel_id=1, source_target_pairs={{0,2},{2,0},{1,3},{3,1},{4,6},{6,4},{5,7},{7,5},{8,10},{10,8},{9,1... | collective-permute-start | bytes 1179656 | tf_op jit(solution)/shard_map/ppermute | solution.py:528
  46.4 9.2 %collective-permute-done.5.come_ref = bf16[256,768]{1,0:T(8,128)(2,1)S(1)} collective-permute-done((bf16[256,768]{1,0:T(8,128)(2,1)S(1)}, bf16[256,768]{1,0:T(8,128)(2,1)S(1)}, u32[]{:S(2)}, u32[]{:S(2)}) %collective-permute-start.5) | collective-permute-done | bytes 393248 | tf_op jit(solution)/shard_map/ppermute | solution.py:528
  55.6 1.1 copy-done.5
  60.2 1.7 %collective-permute-done.6.theirs_ref = bf16[256,768]{1,0:T(8,128)(2,1)S(1)} collective-permute-done((bf16[256,768]{1,0:T(8,128)(2,1)S(1)}, bf16[256,768]{1,0:T(8,128)(2,1)S(1)}, u32[]{:S(2)}, u32[]{:S(2)}) %collective-permute-start.6) | collective-permute-done | bytes 393248 | tf_op jit(solution)/shard_map/ppermute | solution.py:525
  64.1 3.3 %attend_back_kernel.1 = (bf16[576,512]{1,0:T(8,128)(2,1)S(1)}, bf16[16,48,768]{2,1,0:T(8,128)(2,1)S(1)}, f32[8,576]{1,0:T(8,128)S(1)}) custom-call(bf16[256,768]{1,0:T(8,128)(2,1)S(1)} %get-tuple-element.82.mine_ref, bf16[256,768]{1,0:T(8,128)(2,1)S(1)} %collective-permute-done.6.theirs_ref, bf16[192,768]{1,0:T(8,128)(2,1)S(1)} %copy-done.13, ...), custom_call_target="tpu_custom_call" | custom-call | flops 1000 | bytes 1000 | tf_op jit(solution)/shard_map/attend_back_kernel/pallas_call | solution.py:28
  68.4 1.7 %parts_kernel.1 = (f32[512,768]{1,0:T(8,128)S(1)}, bf16[512,768]{1,0:T(8,128)(2,1)}) custom-call(bf16[576,512]{1,0:T(8,128)(2,1)S(1)} %get-tuple-element.87.grads_ref, bf16[576,768]{1,0:T(8,128)(2,1)S(1)} %bitcast.14, bf16[512,768]{1,0:T(8,128)(2,1)S(1)} %copy-done.20, bf16[768,768]{1,0:T(8,128)(2,1)S(1)} %copy-done.2), custom_call_target="tpu_custom_call" | custom-call | flops 1000 | bytes 1000 | tf_op jit(solution)/shard_map/parts_kernel/pallas_call | solution.py:28
  70.1 1.1 copy-done.11
  71.4 8.6 %all-to-all-done.parts_ref = bf16[16,96,768]{2,1,0:T(8,128)(2,1)S(1)} async-done(((bf16[16,96,768]{2,1,0:T(8,128)(2,1)}), bf16[16,96,768]{2,1,0:T(8,128)(2,1)S(1)}, u32[]{:S(2)}, u32[]{:S(2)}) %all-to-all-start) | async-done | bytes 2359328 | tf_op jit(solution)/shard_map/all_to_all | solution.py:537
  80.0 4.4 %all-to-all-start.1 = ((bf16[16,48,768]{2,1,0:T(8,128)(2,1)}), bf16[16,48,768]{2,1,0:T(8,128)(2,1)}, u32[]{:S(2)}, u32[]{:S(2)}) async-start(bf16[16,48,768]{2,1,0:T(8,128)(2,1)} %copy-done.15), calls=%async_computation.1 | async-start | bytes 2359296 | tf_op jit(solution)/shard_map/all_to_all | solution.py:537
  84.7 1.7 %collective-permute-start.4 = (bf16[96,768]{1,0:T(8,128)(2,1)S(1)}, bf16[96,768]{1,0:T(8,128)(2,1)S(1)}, u32[]{:S(2)}, u32[]{:S(2)}) collective-permute-start(bf16[96,768]{1,0:T(8,128)(2,1)S(1)} %total_kernel.1.pair_ref), channel_id=1, source_target_pairs={{0,4},{4,0},{1,5},{5,1},{2,6},{6,2},{3,7},{7,3},{8,12},{12,8},{9,1... | collective-permute-start | bytes 442376 | tf_op jit(solution)/shard_map/ppermute | solution.py:531
  86.4 1.4 pair_kernel.5.pair_ref
  87.8 2.1 %collective-permute-done.4.come_ref = bf16[96,768]{1,0:T(8,128)(2,1)S(1)} collective-permute-done((bf16[96,768]{1,0:T(8,128)(2,1)S(1)}, bf16[96,768]{1,0:T(8,128)(2,1)S(1)}, u32[]{:S(2)}, u32[]{:S(2)}) %collective-permute-start.4) | collective-permute-done | bytes 147488 | tf_op jit(solution)/shard_map/ppermute | solution.py:531
  89.9 3.2 %collective-permute-start.8 = (bf16[512,768]{1,0:T(8,128)(2,1)S(1)}, bf16[512,768]{1,0:T(8,128)(2,1)S(1)}, u32[]{:S(2)}, u32[]{:S(2)}) collective-permute-start(bf16[512,768]{1,0:T(8,128)(2,1)S(1)} %pair_kernel.5.pair_ref), channel_id=1, source_target_pairs={{0,2},{2,0},{1,3},{3,1},{4,6},{6,4},{5,7},{7,5},{8,10},{10,8},{9,1... | collective-permute-start | bytes 2359304 | tf_op jit(solution)/shard_map/ppermute | solution.py:528
  93.1 3.4 %collective-permute-start.10 = (bf16[48,768]{1,0:T(8,128)(2,1)S(1)}, bf16[48,768]{1,0:T(8,128)(2,1)S(1)}, u32[]{:S(2)}, u32[]{:S(2)}) collective-permute-start(bf16[48,768]{1,0:T(8,128)(2,1)S(1)} %get-tuple-element.92.refs_0_), channel_id=1, source_target_pairs={{0,64},{32,96},{64,0},{96,32},{1,65},{33,97},{65,1},{97,33},{2,66}... | collective-permute-start | bytes 221192 | tf_op jit(solution)/shard_map/ppermute | solution.py:544
  96.5 1.1 collective-permute-start.11
  97.7 1.5 collective-permute-start.12
  99.1 2.7 %collective-permute-start.13 = (bf16[48,768]{1,0:T(8,128)(2,1)S(1)}, bf16[48,768]{1,0:T(8,128)(2,1)S(1)}, u32[]{:S(2)}, u32[]{:S(2)}) collective-permute-start(bf16[48,768]{1,0:T(8,128)(2,1)S(1)} %get-tuple-element.93.refs_4_), channel_id=1, source_target_pairs={{0,16},{8,24},{16,0},{24,8},{1,17},{9,25},{17,1},{25,9},{2,18},{10... | collective-permute-start | bytes 221192 | tf_op jit(solution)/shard_map/ppermute | solution.py:544
  101.8 2.6 %collective-permute-start.14 = (bf16[48,768]{1,0:T(8,128)(2,1)S(1)}, bf16[48,768]{1,0:T(8,128)(2,1)S(1)}, u32[]{:S(2)}, u32[]{:S(2)}) collective-permute-start(bf16[48,768]{1,0:T(8,128)(2,1)S(1)} %get-tuple-element.93.refs_4_), channel_id=1, source_target_pairs={{0,24},{8,0},{16,8},{24,16},{1,25},{9,1},{17,9},{25,17},{2,26},{10... | collective-permute-start | bytes 221192 | tf_op jit(solution)/shard_map/ppermute | solution.py:544
  104.4 1.2 collective-permute-start.9
  106.4 3.6 %collective-permute-done.9.refs_1_ = bf16[48,768]{1,0:T(8,128)(2,1)S(1)} collective-permute-done((bf16[48,768]{1,0:T(8,128)(2,1)S(1)}, bf16[48,768]{1,0:T(8,128)(2,1)S(1)}, u32[]{:S(2)}, u32[]{:S(2)}) %collective-permute-start.9) | collective-permute-done | bytes 73760 | tf_op jit(solution)/shard_map/ppermute | solution.py:544
  111.1 1.6 first_norm_kernel.1
  112.8 4.3 %all-to-all-start.2 = ((bf16[4,192,768]{2,1,0:T(8,128)(2,1)}), bf16[4,192,768]{2,1,0:T(8,128)(2,1)}, u32[]{:S(2)}, u32[]{:S(2)}) async-start(bf16[4,192,768]{2,1,0:T(8,128)(2,1)} %copy-done.16), calls=%async_computation.2 | async-start | bytes 2359296 | tf_op jit(solution)/shard_map/all_to_all | solution.py:548
  117.2 2.6 %collective-permute-start.22 = (bf16[192,768]{1,0:T(8,128)(2,1)S(1)}, bf16[192,768]{1,0:T(8,128)(2,1)S(1)}, u32[]{:S(2)}, u32[]{:S(2)}) collective-permute-start(bf16[192,768]{1,0:T(8,128)(2,1)S(1)} %get-tuple-element.122.refs_0_), channel_id=1, source_target_pairs={{0,64},{32,96},{64,0},{96,32},{1,65},{33,97},{65,1},{97,33},{2,66}... | collective-permute-start | bytes 884744 | tf_op jit(solution)/shard_map/ppermute | solution.py:544
  119.7 1.4 collective-permute-start.23
  121.2 2.4 %token_order_kernel.1 = (f32[512,768]{1,0:T(8,128)}, f32[8,768]{1,0:T(8,128)S(1)}) custom-call(f32[264,768]{1,0:T(8,128)} %get-tuple-element.99.mine_ref, f32[264,768]{1,0:T(8,128)S(1)} %collective-permute-done.16.theirs_ref, f32[1,768]{1,0:T(1,128)S(1)} %get-tuple-element.100.up_ref, f32[8,576]{1,0:T(8,128)S(1)} %get-tuple-element.101.qkv_ref), custom_call_target="tpu_custom_call" | custom-call | flops 1000 | bytes 1000 | tf_op jit(solution)/shard_map/token_order_kernel/pallas_call | solution.py:28
  123.6 1.4 attend_total_kernel.1.pair_ref
  125.0 1.3 collective-permute-start.17
  126.3 3.4 %collective-permute-done.17.come_ref = bf16[64,768]{1,0:T(8,128)(2,1)S(1)} collective-permute-done((bf16[64,768]{1,0:T(8,128)(2,1)S(1)}, bf16[64,768]{1,0:T(8,128)(2,1)S(1)}, u32[]{:S(2)}, u32[]{:S(2)}) %collective-permute-start.17) | collective-permute-done | bytes 98336 | tf_op jit(solution)/shard_map/ppermute | solution.py:531
  130.4 1.6 collective-permute-start.19
  132.0 2.5 %collective-permute-done.21.refs_1_ = bf16[192,768]{1,0:T(8,128)(2,1)S(1)} collective-permute-done((bf16[192,768]{1,0:T(8,128)(2,1)S(1)}, bf16[192,768]{1,0:T(8,128)(2,1)S(1)}, u32[]{:S(2)}, u32[]{:S(2)}) %collective-permute-start.21) | collective-permute-done | bytes 294944 | tf_op jit(solution)/shard_map/ppermute | solution.py:544
  135.4 2.9 %collective-permute-done.18.refs_1_ = bf16[64,768]{1,0:T(8,128)(2,1)S(1)} collective-permute-done((bf16[64,768]{1,0:T(8,128)(2,1)S(1)}, bf16[64,768]{1,0:T(8,128)(2,1)S(1)}, u32[]{:S(2)}, u32[]{:S(2)}) %collective-permute-start.18) | collective-permute-done | bytes 98336 | tf_op jit(solution)/shard_map/ppermute | solution.py:544
  139.1 1.2 attend_small_kernel.1
  140.2 4.5 %all-to-all-start.3 = ((bf16[4,208,768]{2,1,0:T(8,128)(2,1)}), bf16[4,208,768]{2,1,0:T(8,128)(2,1)S(1)}, u32[]{:S(2)}, u32[]{:S(2)}) async-start(bf16[4,208,768]{2,1,0:T(8,128)(2,1)} %attend_small_kernel.1), calls=%async_computation.3 | async-start | bytes 2555904 | tf_op jit(solution)/shard_map/all_to_all | solution.py:548
  144.7 1.7 %collective-permute-done.15.theirs_ref = bf16[256,768]{1,0:T(8,128)(2,1)S(1)} collective-permute-done((bf16[256,768]{1,0:T(8,128)(2,1)S(1)}, bf16[256,768]{1,0:T(8,128)(2,1)S(1)}, u32[]{:S(2)}, u32[]{:S(2)}) %collective-permute-start.15) | collective-permute-done | bytes 393248 | tf_op jit(solution)/shard_map/ppermute | solution.py:525
  147.4 4.0 %expert_last_kernel.1 = (f32[768,768]{1,0:T(8,128)}, f32[768,768]{1,0:T(8,128)}) custom-call(bf16[4,192,768]{2,1,0:T(8,128)(2,1)} %all-to-all-done.2.parts_ref, bf16[192,768]{1,0:T(8,128)(2,1)} %copy-done.24, bf16[192,768]{1,0:T(8,128)(2,1)} %copy-done.34, bf16[192,768]{1,0:T(8,128)(2,1)} %copy-done.35, bf16[192,768]{1,0:T(8,128)(2,1)} %copy-done.36), custom_call_target="tpu_custom_call" | custom-call | flops 1000 | bytes 1000 | tf_op jit(solution)/shard_map/expert_last_kernel/pallas_call | solution.py:28
  151.4 9.8 %all-to-all-done.3.parts_ref = bf16[4,208,768]{2,1,0:T(8,128)(2,1)S(1)} async-done(((bf16[4,208,768]{2,1,0:T(8,128)(2,1)}), bf16[4,208,768]{2,1,0:T(8,128)(2,1)S(1)}, u32[]{:S(2)}, u32[]{:S(2)}) %all-to-all-start.3) | async-done | bytes 1277984 | tf_op jit(solution)/shard_map/all_to_all | solution.py:548
  161.2 1.5 attend_last_kernel.1
  (103 shorter events, 14.2 us)
Async XLA Ops:
  0.6 23.0 %copy-start = (bf16[1,512,768]{2,1,0:T(8,128)(2,1)S(1)}, bf16[1,512,768]{2,1,0:T(8,128)(2,1)}, u32[]{:S(2)}) copy-start(bf16[1,512,768]{2,1,0:T(8,128)(2,1)} %param.15) | copy-start | bytes 2359300
  0.7 23.0 %copy-start.28 = (f32[768]{0:T(1024)S(1)}, f32[768]{0:T(1024)}, u32[]{:S(2)}) copy-start(f32[768]{0:T(1024)} %gain_ref.6) | copy-start | bytes 9220
  0.7 23.0 %copy-start.30 = (f32[768]{0:T(1024)S(1)}, f32[768]{0:T(1024)}, u32[]{:S(2)}) copy-start(f32[768]{0:T(1024)} %bias_ref.5) | copy-start | bytes 9220
  0.7 23.0 %copy-start.31 = (f32[768]{0:T(1024)S(1)}, f32[768]{0:T(1024)}, u32[]{:S(2)}) copy-start(f32[768]{0:T(1024)} %shift_ref.3) | copy-start | bytes 9220
  7.7 2.0 %collective-permute-start = (bf16[256,768]{1,0:T(8,128)(2,1)}, bf16[256,768]{1,0:T(8,128)(2,1)S(1)}, u32[]{:S(2)}, u32[]{:S(2)}) collective-permute-start(bf16[256,768]{1,0:T(8,128)(2,1)} %get-tuple-element.73), channel_id=1, source_target_pairs={{0,1},{1,0},{2,3},{3,2},{4,5},{5,4},{6,7},{7,6},{8,9},{9,8},{10,11... | collective-permute-start | bytes 1179656 | tf_op jit(solution)/shard_map/ppermute | solution.py:525
  10.8 15.9 %copy-start.1 = (bf16[768,768]{1,0:T(8,128)(2,1)S(1)}, bf16[768,768]{1,0:T(8,128)(2,1)}, u32[]{:S(2)}) copy-start(bf16[768,768]{1,0:T(8,128)(2,1)} %down_ref.3) | copy-start | bytes 3538948
  10.8 15.9 %copy-start.4 = (bf16[1,512,768]{2,1,0:T(8,128)(2,1)S(1)}, bf16[1,512,768]{2,1,0:T(8,128)(2,1)}, u32[]{:S(2)}) copy-start(bf16[1,512,768]{2,1,0:T(8,128)(2,1)} %param.29) | copy-start | bytes 2359300
  10.8 15.9 %copy-start.14 = (bf16[768,768]{1,0:T(8,128)(2,1)S(1)}, bf16[768,768]{1,0:T(8,128)(2,1)}, u32[]{:S(2)}) copy-start(bf16[768,768]{1,0:T(8,128)(2,1)} %up_ref.1) | copy-start | bytes 3538948
  10.8 15.9 %copy-start.32 = (f32[768]{0:T(1024)S(1)}, f32[768]{0:T(1024)}, u32[]{:S(2)}) copy-start(f32[768]{0:T(1024)} %bias_ref.6) | copy-start | bytes 9220
  10.9 12.8 %collective-permute-start.1 = (bf16[256,768]{1,0:T(8,128)(2,1)S(1)}, bf16[256,768]{1,0:T(8,128)(2,1)S(1)}, u32[]{:S(2)}, u32[]{:S(2)}) collective-permute-start(bf16[256,768]{1,0:T(8,128)(2,1)S(1)} %pair_kernel.3.pair_ref), channel_id=1, source_target_pairs={{0,2},{2,0},{1,3},{3,1},{4,6},{6,4},{5,7},{7,5},{8,10},{10,8},{9,1... | collective-permute-start | bytes 1179656 | tf_op jit(solution)/shard_map/ppermute | solution.py:528
  25.0 1.7 %collective-permute-start.2 = (bf16[256,768]{1,0:T(8,128)(2,1)S(1)}, bf16[256,768]{1,0:T(8,128)(2,1)S(1)}, u32[]{:S(2)}, u32[]{:S(2)}) collective-permute-start(bf16[256,768]{1,0:T(8,128)(2,1)S(1)} %get-tuple-element.74.mine_ref), channel_id=1, source_target_pairs={{0,1},{1,0},{2,3},{3,2},{4,5},{5,4},{6,7},{7,6},{8,9},{9,8},{10,11... | collective-permute-start | bytes 1179656 | tf_op jit(solution)/shard_map/ppermute | solution.py:525
  30.4 1.8 %collective-permute-start.3 = (bf16[256,768]{1,0:T(8,128)(2,1)S(1)}, bf16[256,768]{1,0:T(8,128)(2,1)S(1)}, u32[]{:S(2)}, u32[]{:S(2)}) collective-permute-start(bf16[256,768]{1,0:T(8,128)(2,1)S(1)} %get-tuple-element.76), channel_id=1, source_target_pairs={{0,1},{1,0},{2,3},{3,2},{4,5},{5,4},{6,7},{7,6},{8,9},{9,8},{10,11... | collective-permute-start | bytes 1179656 | tf_op jit(solution)/shard_map/ppermute | solution.py:525
  35.2 44.8 %all-to-all-start = ((bf16[16,96,768]{2,1,0:T(8,128)(2,1)}), bf16[16,96,768]{2,1,0:T(8,128)(2,1)S(1)}, u32[]{:S(2)}, u32[]{:S(2)}) async-start(bf16[16,96,768]{2,1,0:T(8,128)(2,1)} %copy-done.9), calls=%async_computation | async-start | bytes 4718592 | tf_op jit(solution)/shard_map/all_to_all | solution.py:537
  43.1 12.5 %collective-permute-start.5 = (bf16[256,768]{1,0:T(8,128)(2,1)S(1)}, bf16[256,768]{1,0:T(8,128)(2,1)S(1)}, u32[]{:S(2)}, u32[]{:S(2)}) collective-permute-start(bf16[256,768]{1,0:T(8,128)(2,1)S(1)} %pair_kernel.4.pair_ref), channel_id=1, source_target_pairs={{0,2},{2,0},{1,3},{3,1},{4,6},{6,4},{5,7},{7,5},{8,10},{10,8},{9,1... | collective-permute-start | bytes 1179656 | tf_op jit(solution)/shard_map/ppermute | solution.py:528
  57.9 4.1 %copy-start.25 = (bf16[192,512]{1,0:T(8,128)(2,1)S(1)}, bf16[192,512]{1,0:T(8,128)(2,1)}, u32[]{:S(2)}) copy-start(bf16[192,512]{1,0:T(8,128)(2,1)} %get-tuple-element.85.ctx_ref) | copy-start | bytes 589828
  60.2 1.7 %collective-permute-start.6 = (bf16[256,768]{1,0:T(8,128)(2,1)S(1)}, bf16[256,768]{1,0:T(8,128)(2,1)S(1)}, u32[]{:S(2)}, u32[]{:S(2)}) collective-permute-start(bf16[256,768]{1,0:T(8,128)(2,1)S(1)} %get-tuple-element.82.mine_ref), channel_id=1, source_target_pairs={{0,1},{1,0},{2,3},{3,2},{4,5},{5,4},{6,7},{7,6},{8,9},{9,8},{10,11... | collective-permute-start | bytes 1179656 | tf_op jit(solution)/shard_map/ppermute | solution.py:525
  64.1 4.3 %copy-start.2 = (bf16[768,768]{1,0:T(8,128)(2,1)S(1)}, bf16[768,768]{1,0:T(8,128)(2,1)}, u32[]{:S(2)}) copy-start(bf16[768,768]{1,0:T(8,128)(2,1)} %down_ref.3) | copy-start | bytes 3538948
  64.1 4.3 %copy-start.3 = (bf16[768,3,192]{0,2,1:T(8,128)(2,1)S(1)}, bf16[768,3,192]{0,2,1:T(8,128)(2,1)}, u32[]{:S(2)}) copy-start(bf16[768,3,192]{0,2,1:T(8,128)(2,1)} %param.19) | copy-start | bytes 2654212
  64.1 4.3 %copy-start.20 = (bf16[512,768]{1,0:T(8,128)(2,1)S(1)}, bf16[512,768]{1,0:T(8,128)(2,1)}, u32[]{:S(2)}) copy-start(bf16[512,768]{1,0:T(8,128)(2,1)} %copy-done.19) | copy-start | bytes 2359300
  71.3 15.1 %collective-permute-start.7 = (bf16[512,768]{1,0:T(8,128)(2,1)}, bf16[512,768]{1,0:T(8,128)(2,1)}, u32[]{:S(2)}, u32[]{:S(2)}) collective-permute-start(bf16[512,768]{1,0:T(8,128)(2,1)} %get-tuple-element.89), channel_id=1, source_target_pairs={{0,1},{1,0},{2,3},{3,2},{4,5},{5,4},{6,7},{7,6},{8,9},{9,8},{10,11... | collective-permute-start | bytes 2359304 | tf_op jit(solution)/shard_map/ppermute | solution.py:525
  80.0 32.8 %all-to-all-start.1 = ((bf16[16,48,768]{2,1,0:T(8,128)(2,1)}), bf16[16,48,768]{2,1,0:T(8,128)(2,1)}, u32[]{:S(2)}, u32[]{:S(2)}) async-start(bf16[16,48,768]{2,1,0:T(8,128)(2,1)} %copy-done.15), calls=%async_computation.1 | async-start | bytes 2359296 | tf_op jit(solution)/shard_map/all_to_all | solution.py:537
  84.7 5.2 %collective-permute-start.4 = (bf16[96,768]{1,0:T(8,128)(2,1)S(1)}, bf16[96,768]{1,0:T(8,128)(2,1)S(1)}, u32[]{:S(2)}, u32[]{:S(2)}) collective-permute-start(bf16[96,768]{1,0:T(8,128)(2,1)S(1)} %total_kernel.1.pair_ref), channel_id=1, source_target_pairs={{0,4},{4,0},{1,5},{5,1},{2,6},{6,2},{3,7},{7,3},{8,12},{12,8},{9,1... | collective-permute-start | bytes 442376 | tf_op jit(solution)/shard_map/ppermute | solution.py:531
  86.4 24.7 %copy-start.8 = (f32[256,768]{1,0:T(8,128)S(1)}, f32[256,768]{1,0:T(8,128)}, u32[]{:S(2)}) copy-start(f32[256,768]{1,0:T(8,128)} %copy-done.6) | copy-start | bytes 2359300
  86.4 24.7 %copy-start.22 = (f32[256,768]{1,0:T(8,128)S(1)}, f32[256,768]{1,0:T(8,128)}, u32[]{:S(2)}) copy-start(f32[256,768]{1,0:T(8,128)} %copy-done.21) | copy-start | bytes 2359300
  86.4 24.7 %copy-start.27 = (f32[8,768]{1,0:T(8,128)S(1)}, f32[8,768]{1,0:T(8,128)}, u32[]{:S(2)}) copy-start(f32[8,768]{1,0:T(8,128)} %copy-done.26) | copy-start | bytes 73732
  86.4 24.7 %copy-start.29 = (f32[768]{0:T(1024)S(1)}, f32[768]{0:T(1024)}, u32[]{:S(2)}) copy-start(f32[768]{0:T(1024)} %gain_ref.7) | copy-start | bytes 9220
  86.4 24.7 %copy-start.33 = (f32[768]{0:T(1024)S(1)}, f32[768]{0:T(1024)}, u32[]{:S(2)}) copy-start(f32[768]{0:T(1024)} %bias_ref.7) | copy-start | bytes 9220
  89.9 21.2 %collective-permute-start.8 = (bf16[512,768]{1,0:T(8,128)(2,1)S(1)}, bf16[512,768]{1,0:T(8,128)(2,1)S(1)}, u32[]{:S(2)}, u32[]{:S(2)}) collective-permute-start(bf16[512,768]{1,0:T(8,128)(2,1)S(1)} %pair_kernel.5.pair_ref), channel_id=1, source_target_pairs={{0,2},{2,0},{1,3},{3,1},{4,6},{6,4},{5,7},{7,5},{8,10},{10,8},{9,1... | collective-permute-start | bytes 2359304 | tf_op jit(solution)/shard_map/ppermute | solution.py:528
  93.1 8.7 %collective-permute-start.10 = (bf16[48,768]{1,0:T(8,128)(2,1)S(1)}, bf16[48,768]{1,0:T(8,128)(2,1)S(1)}, u32[]{:S(2)}, u32[]{:S(2)}) collective-permute-start(bf16[48,768]{1,0:T(8,128)(2,1)S(1)} %get-tuple-element.92.refs_0_), channel_id=1, source_target_pairs={{0,64},{32,96},{64,0},{96,32},{1,65},{33,97},{65,1},{97,33},{2,66}... | collective-permute-start | bytes 221192 | tf_op jit(solution)/shard_map/ppermute | solution.py:544
  96.5 7.9 %collective-permute-start.11 = (bf16[48,768]{1,0:T(8,128)(2,1)S(1)}, bf16[48,768]{1,0:T(8,128)(2,1)S(1)}, u32[]{:S(2)}, u32[]{:S(2)}) collective-permute-start(bf16[48,768]{1,0:T(8,128)(2,1)S(1)} %get-tuple-element.92.refs_0_), channel_id=1, source_target_pairs={{0,96},{32,0},{64,32},{96,64},{1,97},{33,1},{65,33},{97,65},{2,98}... | collective-permute-start | bytes 221192 | tf_op jit(solution)/shard_map/ppermute | solution.py:544
  97.7 8.0 %collective-permute-start.12 = (bf16[48,768]{1,0:T(8,128)(2,1)S(1)}, bf16[48,768]{1,0:T(8,128)(2,1)S(1)}, u32[]{:S(2)}, u32[]{:S(2)}) collective-permute-start(bf16[48,768]{1,0:T(8,128)(2,1)S(1)} %get-tuple-element.93.refs_4_), channel_id=1, source_target_pairs={{0,8},{8,16},{16,24},{24,0},{1,9},{9,17},{17,25},{25,1},{2,10},{10... | collective-permute-start | bytes 221192 | tf_op jit(solution)/shard_map/ppermute | solution.py:544
  99.1 6.5 %collective-permute-start.13 = (bf16[48,768]{1,0:T(8,128)(2,1)S(1)}, bf16[48,768]{1,0:T(8,128)(2,1)S(1)}, u32[]{:S(2)}, u32[]{:S(2)}) collective-permute-start(bf16[48,768]{1,0:T(8,128)(2,1)S(1)} %get-tuple-element.93.refs_4_), channel_id=1, source_target_pairs={{0,16},{8,24},{16,0},{24,8},{1,17},{9,25},{17,1},{25,9},{2,18},{10... | collective-permute-start | bytes 221192 | tf_op jit(solution)/shard_map/ppermute | solution.py:544
  101.8 4.6 %collective-permute-start.14 = (bf16[48,768]{1,0:T(8,128)(2,1)S(1)}, bf16[48,768]{1,0:T(8,128)(2,1)S(1)}, u32[]{:S(2)}, u32[]{:S(2)}) collective-permute-start(bf16[48,768]{1,0:T(8,128)(2,1)S(1)} %get-tuple-element.93.refs_4_), channel_id=1, source_target_pairs={{0,24},{8,0},{16,8},{24,16},{1,25},{9,1},{17,9},{25,17},{2,26},{10... | collective-permute-start | bytes 221192 | tf_op jit(solution)/shard_map/ppermute | solution.py:544
  104.4 5.6 %collective-permute-start.9 = (bf16[48,768]{1,0:T(8,128)(2,1)S(1)}, bf16[48,768]{1,0:T(8,128)(2,1)S(1)}, u32[]{:S(2)}, u32[]{:S(2)}) collective-permute-start(bf16[48,768]{1,0:T(8,128)(2,1)S(1)} %get-tuple-element.92.refs_0_), channel_id=1, source_target_pairs={{0,32},{32,64},{64,96},{96,0},{1,33},{33,65},{65,97},{97,1},{2,34}... | collective-permute-start | bytes 221192 | tf_op jit(solution)/shard_map/ppermute | solution.py:544
  111.1 8.7 %copy-start.24 = (bf16[192,768]{1,0:T(8,128)(2,1)}, bf16[192,768]{1,0:T(8,128)(2,1)S(1)}, u32[]{:S(2)}) copy-start(bf16[192,768]{1,0:T(8,128)(2,1)S(1)} %get-tuple-element.122.refs_0_) | copy-start | bytes 884740
  112.8 8.4 %collective-permute-start.16 = (f32[264,768]{1,0:T(8,128)}, f32[264,768]{1,0:T(8,128)S(1)}, u32[]{:S(2)}, u32[]{:S(2)}) collective-permute-start(f32[264,768]{1,0:T(8,128)} %get-tuple-element.99.mine_ref), channel_id=1, source_target_pairs={{0,1},{1,0},{2,3},{3,2},{4,5},{5,4},{6,7},{7,6},{8,9},{9,8},{10,11... | collective-permute-start | bytes 2433032 | tf_op jit(solution)/shard_map/ppermute | solution.py:525
  112.8 27.5 %all-to-all-start.2 = ((bf16[4,192,768]{2,1,0:T(8,128)(2,1)}), bf16[4,192,768]{2,1,0:T(8,128)(2,1)}, u32[]{:S(2)}, u32[]{:S(2)}) async-start(bf16[4,192,768]{2,1,0:T(8,128)(2,1)} %copy-done.16), calls=%async_computation.2 | async-start | bytes 2359296 | tf_op jit(solution)/shard_map/all_to_all | solution.py:548
  117.0 17.4 %collective-permute-start.21 = (bf16[192,768]{1,0:T(8,128)(2,1)S(1)}, bf16[192,768]{1,0:T(8,128)(2,1)S(1)}, u32[]{:S(2)}, u32[]{:S(2)}) collective-permute-start(bf16[192,768]{1,0:T(8,128)(2,1)S(1)} %get-tuple-element.122.refs_0_), channel_id=1, source_target_pairs={{0,32},{32,64},{64,96},{96,0},{1,33},{33,65},{65,97},{97,1},{2,34}... | collective-permute-start | bytes 884744 | tf_op jit(solution)/shard_map/ppermute | solution.py:544
  117.2 17.4 %collective-permute-start.22 = (bf16[192,768]{1,0:T(8,128)(2,1)S(1)}, bf16[192,768]{1,0:T(8,128)(2,1)S(1)}, u32[]{:S(2)}, u32[]{:S(2)}) collective-permute-start(bf16[192,768]{1,0:T(8,128)(2,1)S(1)} %get-tuple-element.122.refs_0_), channel_id=1, source_target_pairs={{0,64},{32,96},{64,0},{96,32},{1,65},{33,97},{65,1},{97,33},{2,66}... | collective-permute-start | bytes 884744 | tf_op jit(solution)/shard_map/ppermute | solution.py:544
  119.7 15.7 %collective-permute-start.23 = (bf16[192,768]{1,0:T(8,128)(2,1)S(1)}, bf16[192,768]{1,0:T(8,128)(2,1)S(1)}, u32[]{:S(2)}, u32[]{:S(2)}) collective-permute-start(bf16[192,768]{1,0:T(8,128)(2,1)S(1)} %get-tuple-element.122.refs_0_), channel_id=1, source_target_pairs={{0,96},{32,0},{64,32},{96,64},{1,97},{33,1},{65,33},{97,65},{2,98}... | collective-permute-start | bytes 884744 | tf_op jit(solution)/shard_map/ppermute | solution.py:544
  125.0 4.7 %collective-permute-start.17 = (bf16[64,768]{1,0:T(8,128)(2,1)S(1)}, bf16[64,768]{1,0:T(8,128)(2,1)S(1)}, u32[]{:S(2)}, u32[]{:S(2)}) collective-permute-start(bf16[64,768]{1,0:T(8,128)(2,1)S(1)} %attend_total_kernel.1.pair_ref), channel_id=1, source_target_pairs={{0,4},{4,0},{1,5},{5,1},{2,6},{6,2},{3,7},{7,3},{8,12},{12,8},{9,1... | collective-permute-start | bytes 294920 | tf_op jit(solution)/shard_map/ppermute | solution.py:531
  129.7 8.6 %collective-permute-start.18 = (bf16[64,768]{1,0:T(8,128)(2,1)S(1)}, bf16[64,768]{1,0:T(8,128)(2,1)S(1)}, u32[]{:S(2)}, u32[]{:S(2)}) collective-permute-start(bf16[64,768]{1,0:T(8,128)(2,1)S(1)} %attend_finish_kernel.1.refs_0_), channel_id=1, source_target_pairs={{0,32},{32,64},{64,96},{96,0},{1,33},{33,65},{65,97},{97,1},{2,34}... | collective-permute-start | bytes 294920 | tf_op jit(solution)/shard_map/ppermute | solution.py:544
  130.4 7.9 %collective-permute-start.19 = (bf16[64,768]{1,0:T(8,128)(2,1)S(1)}, bf16[64,768]{1,0:T(8,128)(2,1)S(1)}, u32[]{:S(2)}, u32[]{:S(2)}) collective-permute-start(bf16[64,768]{1,0:T(8,128)(2,1)S(1)} %attend_finish_kernel.1.refs_0_), channel_id=1, source_target_pairs={{0,64},{32,96},{64,0},{96,32},{1,65},{33,97},{65,1},{97,33},{2,66}... | collective-permute-start | bytes 294920 | tf_op jit(solution)/shard_map/ppermute | solution.py:544
  134.4 4.6 %copy-start.34 = (bf16[192,768]{1,0:T(8,128)(2,1)}, bf16[192,768]{1,0:T(8,128)(2,1)S(1)}, u32[]{:S(2)}) copy-start(bf16[192,768]{1,0:T(8,128)(2,1)S(1)} %collective-permute-done.21.refs_1_) | copy-start | bytes 884740
  134.4 4.6 %collective-permute-start.20 = (bf16[64,768]{1,0:T(8,128)(2,1)S(1)}, bf16[64,768]{1,0:T(8,128)(2,1)S(1)}, u32[]{:S(2)}, u32[]{:S(2)}) collective-permute-start(bf16[64,768]{1,0:T(8,128)(2,1)S(1)} %attend_finish_kernel.1.refs_0_), channel_id=1, source_target_pairs={{0,96},{32,0},{64,32},{96,64},{1,97},{33,1},{65,33},{97,65},{2,98}... | collective-permute-start | bytes 294920 | tf_op jit(solution)/shard_map/ppermute | solution.py:544
  134.5 4.5 %copy-start.35 = (bf16[192,768]{1,0:T(8,128)(2,1)}, bf16[192,768]{1,0:T(8,128)(2,1)S(1)}, u32[]{:S(2)}) copy-start(bf16[192,768]{1,0:T(8,128)(2,1)S(1)} %collective-permute-done.22.refs_2_) | copy-start | bytes 884740
  140.2 21.0 %all-to-all-start.3 = ((bf16[4,208,768]{2,1,0:T(8,128)(2,1)}), bf16[4,208,768]{2,1,0:T(8,128)(2,1)S(1)}, u32[]{:S(2)}, u32[]{:S(2)}) async-start(bf16[4,208,768]{2,1,0:T(8,128)(2,1)} %attend_small_kernel.1), calls=%async_computation.3 | async-start | bytes 2555904 | tf_op jit(solution)/shard_map/all_to_all | solution.py:548
  144.7 1.7 %collective-permute-start.15 = (bf16[256,768]{1,0:T(8,128)(2,1)S(1)}, bf16[256,768]{1,0:T(8,128)(2,1)S(1)}, u32[]{:S(2)}, u32[]{:S(2)}) collective-permute-start(bf16[256,768]{1,0:T(8,128)(2,1)S(1)} %get-tuple-element.98.mine_ref), channel_id=1, source_target_pairs={{0,1},{1,0},{2,3},{3,2},{4,5},{5,4},{6,7},{7,6},{8,9},{9,8},{10,11... | collective-permute-start | bytes 1179656 | tf_op jit(solution)/shard_map/ppermute | solution.py:525
  (17 other events, 28.2 us)

commit v3 on v2

--- a/solution.py
+++ b/solution.py
@@ -22,17 +22,20 @@
     )
 
 
-def call(body, outs, scratch=(), place=pltpu.VMEM, limit=12 << 20, cost=1000):
+def call(body, outs, scratch=(), place=pltpu.VMEM, limit=12 << 20, cost=1000, aliases=(), far=()):
     def run(*arrays):
         space = pl.BlockSpec() if place is None else pl.BlockSpec(memory_space=place)
+        apart = pl.BlockSpec(memory_space=pltpu.HBM)
+        count = len(arrays)
         return pl.pallas_call(
             body,
             out_shape=[jax.ShapeDtypeStruct(s, d) for s, d in outs],
-            in_specs=[space] * len(arrays),
-            out_specs=[space] * len(outs),
+            in_specs=[apart if i in far else space for i in range(count)],
+            out_specs=[apart if count + i in far else space for i in range(len(outs))],
             scratch_shapes=[pltpu.VMEM(*s) if isinstance(s, tuple) else s for s in scratch],
             cost_estimate=pl.CostEstimate(flops=cost, bytes_accessed=1000, transcendentals=0),
             compiler_params=pltpu.CompilerParams(vmem_limit_bytes=limit),
+            input_output_aliases=dict(aliases),
             name=body.__name__,
         )(*arrays)
 
@@ -184,7 +187,7 @@
     out_copy.wait()
     other_ref[...] = dot(ctx_ref[:, half:], out_at[...], 0, 0).astype(BF)
     leaving.append(fetch(other_ref, other_out))
-    own_ref[...] = dot(ctx_ref[:, :half], out_at[...], 0, 0)
+    own_ref[...] = dot(ctx_ref[:, :half], out_at[...], 0, 0).astype(BF)
     leaving.append(fetch(own_ref, own_out))
     for copy in leaving:
         copy.wait()
@@ -237,10 +240,7 @@
             grad_ref[at, :] = grad
             total += fold(grad.astype(F32))
             part = dot(grad, up_ref[...], 1, 1)
-            if which:
-                other_ref[rows, :] = part.astype(BF)
-            else:
-                own_ref[rows, :] = part
+            (other_ref if which else own_ref)[rows, :] = part.astype(BF)
     sum_ref[...] = total
 
 
@@ -337,29 +337,33 @@
     sums_ref[...] = dot(jnp.ones((8, length), BF), grads_ref[...], 1, 1)
 
 
-def parts_kernel(grads_ref, w_ref, hidden_ref, down_ref, own_ref, other_ref):
-    half = own_ref.shape[0] // 2
-    other_ref[:half, :] = dot(grads_ref[:, half:], w_ref[...], 0, 0).astype(BF)
-    other_ref[half:, :] = dot(hidden_ref[half:, :], down_ref[...]).astype(BF)
-    own_ref[:half, :] = dot(grads_ref[:, :half], w_ref[...], 0, 0)
-    own_ref[half:, :] = dot(hidden_ref[:half, :], down_ref[...])
-
-
-def first_norm_kernel(
-    tok_ref, pair_ref, come_ref, gain_ref, bias_ref, back_ref, resid_ref, rows_ref, grad_ref, mixed_ref
-):
-    half = mixed_ref.shape[0]
+def attend_in_kernel(grads_ref, w_ref, own_ref, other_ref):
+    half = own_ref.shape[0]
+    other_ref[...] = dot(grads_ref[:, half:], w_ref[...], 0, 0).astype(BF)
+    own_ref[...] = dot(grads_ref[:, :half], w_ref[...], 0, 0).astype(BF)
+
+
+def expert_out_kernel(hidden_ref, down_ref, own_ref, other_ref):
+    half = own_ref.shape[0]
+    other_ref[...] = dot(hidden_ref[half:, :], down_ref[...]).astype(BF)
+    own_ref[...] = dot(hidden_ref[:half, :], down_ref[...]).astype(BF)
+
+
+def mixed_kernel(resid_ref, pair_ref, come_ref, bias_ref, mixed_ref):
+    total = pair_ref[...].astype(F32) + come_ref[...].astype(F32)
+    mixed_ref[...] = (resid_ref[...] + total + line(bias_ref)).astype(BF)
+
+
+def first_norm_kernel(tok_ref, pair_ref, come_ref, gain_ref, back_ref, rows_ref, grad_ref):
+    half = pair_ref.shape[0]
     start = half_at(0, half)
     step = 64
     gains, shifts = 0.0, 0.0
     for first in range(0, half, step):
         rows = slice(first, first + step)
-        below = slice(half + first, half + first + step)
         xhat, inverse = norm_parts(tok_ref[pl.ds(start + first, step), :].astype(F32))
         grad = pair_ref[rows, :].astype(F32) + come_ref[rows, :].astype(F32)
         grad_ref[rows, :] = back_ref[rows, :] + norm_back(grad, xhat, inverse, line(gain_ref))
-        out = pair_ref[below, :].astype(F32) + come_ref[below, :].astype(F32)
-        mixed_ref[rows, :] = (resid_ref[rows, :] + out + line(bias_ref)).astype(BF)
         gains += fold(grad * xhat)
         shifts += fold(grad)
     grad_ref[half:, :] = rows_ref[...]
@@ -383,7 +387,7 @@
 
 
 def pair_kernel(own_ref, come_ref, pair_ref):
-    pair_ref[...] = (own_ref[...] + come_ref[...].astype(F32)).astype(BF)
+    pair_ref[...] = own_ref[...] + come_ref[...]
 
 
 def expert_finish_kernel(pair_ref, come_ref, a_ref, b_ref):
@@ -405,12 +409,7 @@
 def attend_total_kernel(parts_ref, whole_ref, pair_ref):
     count = parts_ref.shape[1]
     total_kernel(parts_ref, pair_ref.at[:count])
-    vectors = whole_ref[...]
-    pair_ref[count:, :] = jnp.concatenate((vectors, jnp.zeros_like(vectors))).astype(BF)
-
-
-def attend_finish_kernel(pair_ref, come_ref, total_ref):
-    total_ref[...] = pair_ref[...] + come_ref[...]
+    pair_ref[count:, :] = whole_ref[...].astype(BF)
 
 
 def place(axis, blocks, store):
@@ -419,70 +418,79 @@
         store(lax.rem(lax.axis_index(axis) + count - shift, count), block)
 
 
-def expert_small_kernel(*refs):
-    a_blocks, b_blocks, (a_ref, b_ref) = refs[:4], refs[4:8], refs[8:]
-    each = a_blocks[0].shape[0]
-
-    def store_a(source, block):
-        for copy in range(a_ref.shape[0]):
-            a_ref[copy, pl.ds(pl.multiple_of(source * each, each), each), :] = block[...]
-
-    def store_b(source, block):
-        b_ref[pl.ds(pl.multiple_of(source * each, each), each), :] = block[...]
-
-    place("z", a_blocks, store_a)
-    place("x", b_blocks, store_b)
-
-
-def expert_last_kernel(parts_ref, *refs):
-    blocks, (down_ref, up_ref) = refs[:4], refs[4:]
+def join(axis, bit, own_ref, come_ref, store):
+    place = (lax.axis_index(axis) >> bit) & 1
+    store(place, own_ref)
+    store(1 - place, come_ref)
+
+
+def join_kernel(axes, bit, *refs):
+    count = len(axes)
+    for index, axis in enumerate(axes):
+        own_ref, come_ref, row_ref = refs[index], refs[count + index], refs[2 * count + index]
+        each = own_ref.shape[0]
+
+        def store(place, block, row_ref=row_ref, each=each):
+            row_ref[pl.ds(pl.multiple_of(place * each, each), each), :] = block[...]
+
+        join(axis, bit, own_ref, come_ref, store)
+
+
+def expert_most_kernel(*refs):
+    a_blocks, b_blocks, (down_ref, up_ref) = refs[:3], refs[3:6], refs[6:]
+    rows = a_blocks[0].shape[0]
+    planes = down_ref.shape[0] // rows
+    each = rows // planes
+    for shift, a_block, b_block in zip((0, 1, 3), a_blocks, b_blocks):
+        source = lax.rem(lax.axis_index("x") + planes - shift, planes)
+        for z in range(planes):
+            at = pl.multiple_of(z * rows + source * each, each)
+            down_ref[pl.ds(at, each), :] = a_block[z * each : (z + 1) * each, :].astype(F32)
+        source = lax.rem(lax.axis_index("z") + planes - shift, planes)
+        up_ref[pl.ds(pl.multiple_of(source * rows, rows), rows), :] = b_block[...].astype(F32)
+
+
+def attend_finish_kernel(pair_ref, come_ref, copies_ref):
+    total = pair_ref[...] + come_ref[...]
+    for copy in range(copies_ref.shape[0]):
+        copies_ref[copy] = total
+
+
+def last_kernel(parts_ref, a_ref, b_ref, down_in, up_in, down_ref, up_ref, qkv_ref, out_ref, qv_ref, *refs):
+    *vector_refs, a_full, b_full, semaphores = refs
+    rows = a_ref.shape[0]
+    side = down_ref.shape[0] // rows
+    a_full[...] = a_ref[...].astype(F32)
+    leaving = []
+    source = lax.rem(lax.axis_index("x") + 2, side)
+    for z in range(side):
+        at = pl.multiple_of((z * side + source) * (rows // side), rows // side)
+        leaving.append(
+            pltpu.make_async_copy(
+                a_full.at[pl.ds(z * (rows // side), rows // side)],
+                down_ref.at[pl.ds(at, rows // side)],
+                semaphores.at[z],
+            )
+        )
+        leaving[-1].start()
+    b_full[...] = b_ref[...].astype(F32)
+    at = pl.multiple_of(lax.rem(lax.axis_index("z") + 2, side) * rows, rows)
+    leaving.append(
+        pltpu.make_async_copy(b_full, up_ref.at[pl.ds(at, rows)], semaphores.at[side])
+    )
+    leaving[-1].start()
     planes = parts_ref.shape[0]
-    rows = blocks[0].shape[0]
-    each = rows // planes
-    for x in range(planes):
-        for z in range(planes):
-            at = (z * planes + x) * each
-            down_ref[at : at + each, :] = parts_ref[x, z * each : (z + 1) * each, :].astype(F32)
-
-    def store(source, block):
-        up_ref[pl.ds(pl.multiple_of(source * rows, rows), rows), :] = block[...].astype(F32)
-
-    place("z", blocks, store)
-
-
-def attend_small_kernel(*refs):
-    blocks, (copies_ref, keep_ref) = refs[:4], refs[4:]
-    each = blocks[0].shape[0] - keep_ref.shape[1]
-    planes = keep_ref.shape[0]
-
-    def store(source, block):
-        keep_ref[source] = block[each:, :].astype(F32)
-        for copy in range(planes):
-            copies_ref[copy, pl.ds(pl.multiple_of(source * each, each), each), :] = block[:each, :]
-
-    place("z", blocks, store)
-    total = keep_ref[0]
-    for source in range(1, planes):
-        total += keep_ref[source]
-    for copy in range(planes):
-        copies_ref[copy, planes * each :, :] = total.astype(BF)
-
-
-def attend_last_kernel(parts_ref, qkv_ref, out_ref, qv_ref, *vector_refs):
-    planes = parts_ref.shape[0]
-    each = (parts_ref.shape[1] - 16) // planes
+    each = parts_ref.shape[1] - len(vector_refs) - 1
     width = qkv_ref.shape[0]
-    for x in range(planes):
-        for z in range(planes):
-            rows = parts_ref[x, z * each : (z + 1) * each, :].astype(F32)
-            at = (z * planes + x) * each
-            if at < width:
-                qkv_ref[at : at + each, :] = rows
-            else:
-                out_ref[at - width : at - width + each, :] = rows
-    total = parts_ref[0, planes * each :, :].astype(F32)
-    for x in range(1, planes):
-        total += parts_ref[x, planes * each :, :].astype(F32)
+    total = jnp.zeros(parts_ref.shape[2:], F32)
+    for part in range(planes):
+        rows = parts_ref[part, :each, :].astype(F32)
+        at = part * each
+        if at < width:
+            qkv_ref[at : at + each, :] = rows
+        else:
+            out_ref[at - width : at - width + each, :] = rows
+        total = total + parts_ref[part, each:, :].astype(F32)
     for index, vector_ref in enumerate(vector_refs):
         vector_ref[...] = total[index]
     heads, double = qv_ref.shape
@@ -491,6 +499,8 @@
         base = 3 * head * size
         qv_ref[head : head + 1, :size] = total[7:8, base : base + size]
         qv_ref[head : head + 1, size:] = total[7:8, base + 2 * size : base + 3 * size]
+    for copy in leaving:
+        copy.wait()
 
 
 def shards(
@@ -539,13 +549,21 @@
     def plane_sum(received):
         return call(total_kernel, ((received.shape[1:], BF),))(received)[0]
 
+    def exchange(block, axis, bit):
+        partner = (lambda i: i ^ 1) if bit == 0 else (lambda i: side - 1 - i)
+        return lax.ppermute(block, axis, [(i, partner(i)) for i in range(side)])
+
+    def joiner(axes, bit):
+        def kernel(*refs):
+            join_kernel(axes, bit, *refs)
+
+        kernel.__name__ = "join_kernel"
+        return kernel
+
     def along(block, axis):
         moves = [[(i, (i + shift) % side) for i in range(side)] for shift in range(1, side)]
         far, near, back = (lax.ppermute(block, axis, moves[i]) for i in (1, 0, 2))
         return (block, near, far, back)
-
-    def spread(copies):
-        return lax.all_to_all(copies, "x", 0, 0, tiled=True)
 
     half_low, half_full = ((half, features), BF), ((half, features), F32)
     row_low, row_full = ((length, features), BF), ((length, features), F32)
@@ -557,7 +575,7 @@
         ((width, length), BF),
         ((heads, length, length), BF),
         ((count, length), BF),
-        half_full,
+        half_low,
         half_low,
     )
     staged = (
@@ -581,7 +599,7 @@
 
     hidden, up_grad, own, other, up_sums = call(
         expert_kernel,
-        (((length, units), BF), ((length, units), BF), half_full, half_low, ((1, units), F32)),
+        (((length, units), BF), ((length, units), BF), half_low, half_low, ((1, units), F32)),
     )(normed_mine, normed_theirs, up_weight, up_bias, down_weight, cot)
     pair = add_pair(own, other)
     pair, hidden = lax.optimization_barrier((pair, hidden))
@@ -592,6 +610,10 @@
     )(hidden, cot, normed_mine, normed_theirs, up_grad)
     come = chip_swap(pair)
     expert_parts = scatter(chunks)
+    own, other = call(expert_out_kernel, (half_low, half_low))(hidden, down_weight)
+    other, _ = lax.optimization_barrier((other, come))
+    mixed_pair = add_pair(own, other)
+    mixed_come = chip_swap(mixed_pair)
     low_mine, resid_grad, sums = call(second_norm_kernel, (half_low, half_full, rows_full))(
         pair, come, resid, norm2_gain, cot
     )
@@ -603,52 +625,58 @@
         (((count, length), BF), ((length, length), BF)),
     )(low_mine, low_theirs, out_weight, probs, qkv, context, normed_one)
     attend_parts = scatter(chunks)
-    own, other = call(parts_kernel, (row_full, row_low))(qkv_grad, qkv_rows, hidden, down_weight)
+    qkv_grad, mixed_come = lax.optimization_barrier((qkv_grad, mixed_come))
+    own, other = call(attend_in_kernel, (half_low, half_low))(qkv_grad, qkv_rows)
     parts_pair = add_pair(own, other)
 
+    come = chip_swap(parts_pair)
     pair = plane_sum(expert_parts)
     each = pair.shape[0] // 2
-    come = near_swap(pair)
-    come, parts_pair = lax.optimization_barrier((come, parts_pair))
-    blocks = call(expert_finish_kernel, (((each, features), BF),) * 2)(pair, come)
-    copies, block = call(
-        expert_small_kernel,
-        (((side, side * each, features), BF), ((side * each, features), BF)),
-    )(*along(blocks[0], "z"), *along(blocks[1], "x"))
-    copies, attend_parts = lax.optimization_barrier((copies, attend_parts))
-    come, _ = lax.optimization_barrier((chip_swap(parts_pair), block))
-    gathered = spread(copies)
-    expert_blocks = along(block, "z")
-
-    token_grad, mixed = call(first_norm_kernel, (((half + 8, features), F32), half_low))(
-        tok, parts_pair, come, norm1_gain, down_bias, resid_grad, resid, sums
+    near_pair, come = lax.optimization_barrier((near_swap(pair), come))
+    blocks = call(expert_finish_kernel, (((each, features), BF),) * 2)(pair, near_pair)
+    (token_grad,) = call(first_norm_kernel, (((half + 8, features), F32),))(
+        tok, parts_pair, come, norm1_gain, resid_grad, sums
     )
     tokens_grad, whole = call(token_order_kernel, (row_full, rows_full))(
         token_grad, core_swap(token_grad), up_sums, qkv_sums
     )
+    step = (exchange(blocks[0], "z", 0), exchange(blocks[1], "x", 0))
+    blocks = call(joiner(("z", "x"), 0), (((2 * each, features), BF),) * 2)(*blocks, *step)
+    rows = attend_parts.shape[1] + whole.shape[0]
+    blocks, whole = lax.optimization_barrier((blocks, whole))
+    (pair,) = call(attend_total_kernel, (((rows, features), BF),))(attend_parts, whole)
+    blocks, pair = lax.optimization_barrier((blocks, pair))
+    step = (exchange(blocks[0], "z", 1), exchange(blocks[1], "x", 1))
+    blocks = call(joiner(("z", "x"), 1), (((4 * each, features), BF),) * 2)(*blocks, *step)
+    down_blocks, up_blocks = along(blocks[0], "x"), along(blocks[1], "z")
+    (mixed,) = call(mixed_kernel, (half_low,))(resid, mixed_pair, mixed_come, down_bias)
     (mixed,) = call(mixed_order_kernel, (row_low,))(mixed, core_swap(mixed))
 
-    rows = attend_parts.shape[1] + 16
-    (pair,) = call(attend_total_kernel, (((rows, features), BF),))(attend_parts, whole)
-    (block,) = call(attend_finish_kernel, (((rows, features), BF),))(pair, near_swap(pair))
-    blocks, expert_blocks = lax.optimization_barrier((along(block, "z"), expert_blocks))
-    (copies,) = call(
-        attend_small_kernel,
-        (((side, side * (rows - 16) + 16, features), BF),),
-        (((side, 16, features), F32),),
-    )(*blocks)
-    copies, gathered = lax.optimization_barrier((copies, gathered))
+    rows = pair.shape[0]
+    come = near_swap(pair)
+    down_own, down_near, down_far, down_back = down_blocks
+    up_own, up_near, up_far, up_back = up_blocks
+    come, down_near, down_back, up_near, up_back = lax.optimization_barrier(
+        (come, down_near, down_back, up_near, up_back)
+    )
+    (copies,) = call(attend_finish_kernel, (((plane, rows, features), BF),))(pair, come)
+    gathered = scatter(copies)
     down_grad, up_weight_grad = call(
-        expert_last_kernel,
+        expert_most_kernel,
         (((units, features), F32), ((features, units), F32)),
         place=None,
         limit=60 << 20,
-    )(gathered, *expert_blocks)
-    qkv_grads, out_weight_grad, qv_bias_grad, *vectors = call(
-        attend_last_kernel,
-        (((width, features), F32), ((count, features), F32), (qv_bias.shape, F32))
+    )(down_own, down_near, down_back, up_own, up_near, up_back)
+    block = down_far.shape
+    down_grad, up_weight_grad, qkv_grads, out_weight_grad, qv_bias_grad, *vectors = call(
+        last_kernel,
+        (((units, features), F32), ((features, units), F32))
+        + (((width, features), F32), ((count, features), F32), (qv_bias.shape, F32))
         + (((features,), F32),) * 7,
-    )(spread(copies))
+        ((block, F32), (block, F32), pltpu.SemaphoreType.DMA((1 + side,))),
+        aliases=((3, 0), (4, 1)),
+        far=(3, 4, 5, 6),
+    )(gathered, down_far, up_far, down_grad, up_weight_grad)
     return (
         mixed[None],
         tokens_grad[None],

time: 163 us -> 159 us (0.975)
  local copies, waits for them, and re-layouts: 12.6 us -> 7.95 us
  waiting for transfers between devices: 62.5 us -> 64.2 us
    ppermute x0 -> x4, waiting for transfers between devices: none -> 9.82 us  [exchange(): return lax.ppermute(block, axis, [(i, partner(i)) for i in range(side)])]
    all_to_all x2 -> x0, waiting for transfers between devices: 9.8 us -> none  [spread(): return lax.all_to_all(copies, 'x', 0, 0, tiled=True)]
    all_to_all x2 -> x0, starting transfers between devices: 8.75 us -> none  [spread(): return lax.all_to_all(copies, 'x', 0, 0, tiled=True)]
    ppermute x12 -> x6, starting transfers between devices: 19 us -> 10.7 us  [along(): far, near, back = (lax.ppermute(block, axis, moves[i]) for i in (1, 0, 2))]
    ppermute x0 -> x4, starting transfers between devices: none -> 6.53 us  [exchange(): return lax.ppermute(block, axis, [(i, partner(i)) for i in range(side)])]
    all_to_all x2 -> x3, starting transfers between devices: 12.3 us -> 17.1 us  [scatter(): return lax.all_to_all(chunks, PLANE, 0, 0, tiled=True)]
    unnamed x74 -> x82, local copies, waits for them, and re-layouts: 12.6 us -> 7.95 us
    all_to_all x2 -> x3, waiting for transfers between devices: 8.58 us -> 5.12 us  [scatter(): return lax.all_to_all(chunks, PLANE, 0, 0, tiled=True)]
  transfers between devices with their start and end apart: 28 -> 27, of which waited for: 17 -> 18; matrix products, arithmetic and copies ran while one was open for 0% -> 0% of each run, Pallas kernels for 12% -> 9%
where the time goes in v3:
time: 159 us; the launch traced here: 158 us
  waiting for transfers between devices  64.2 us (40%)
  starting transfers between devices  52.1 us (33%)
  Pallas kernels  32.4 us (20%)
  local copies, waits for them, and re-layouts  7.95 us (5%)
    pallas_call x24, Pallas kernels, run(): pl.pallas_call(body, out_shape=[jax.ShapeDtypeStruct(s, d) for s, d in ou...  32.4 us
    ppermute x4, waiting for transfers between devices, chip_swap(): return lax.ppermute(array_in, 'far', [(0, 1), (1, 0)])  21.5 us
    all_to_all x3, starting transfers between devices, scatter(): return lax.all_to_all(chunks, PLANE, 0, 0, tiled=True)  17.1 us
    ppermute x6, waiting for transfers between devices, along(): far, near, back = (lax.ppermute(block, axis, moves[i]) for i in (1, 0, 2))  14.3 us
    ppermute x4, starting transfers between devices, chip_swap(): return lax.ppermute(array_in, 'far', [(0, 1), (1, 0)])  13.2 us
    ppermute x6, starting transfers between devices, along(): far, near, back = (lax.ppermute(block, axis, moves[i]) for i in (1, 0, 2))  10.7 us
    ppermute x4, waiting for transfers between devices, exchange(): return lax.ppermute(block, axis, [(i, partner(i)) for i in range(side)])  9.82 us
    unnamed x82, local copies, waits for them, and re-layouts  7.95 us
  transfers between devices with their start and end apart: 27, of which 18 were waited for; matrix products, arithmetic and copies ran while one was open for 0% of the time, Pallas kernels for 9%

profile of v3, /device:TPU:0, one launch (start us, length us, event | category | flops | bytes accessed | tf_op | source)
XLA Modules:
  0.0 158.0 jit_solution(1114165263089648615)
XLA Ops:
  0.7 6.9 %attend_kernel.1 = (bf16[512,768]{1,0:T(8,128)(2,1)}, bf16[576,512]{1,0:T(8,128)(2,1)}, bf16[3,512,512]{2,1,0:T(8,128)(2,1)}, bf16[192,512]{1,0:T(8,128)(2,1)}, ...) custom-call(s32[1,8]{1,0:T(1,128)} %lens_ref.1, bf16[512,768]{1,0:T(8,128)(2,1)} %bitcast.10, f32[768]{0:T(1024)} %gain_ref.7, ...), custom_call_target="tpu_custom_call" | custom-call | flops 1000 | bytes 1000 | tf_op jit(solution)/shard_map/attend_kernel/pallas_call | solution.py:30
  7.7 1.9 %collective-permute-done.come_ref = bf16[256,768]{1,0:T(8,128)(2,1)S(1)} collective-permute-done((bf16[256,768]{1,0:T(8,128)(2,1)}, bf16[256,768]{1,0:T(8,128)(2,1)S(1)}, u32[]{:S(2)}, u32[]{:S(2)}) %collective-permute-start) | collective-permute-done | bytes 393248 | tf_op jit(solution)/shard_map/ppermute | solution.py:535
  9.6 1.0 copy-done.22
  10.7 3.4 %collective-permute-start.1 = (bf16[256,768]{1,0:T(8,128)(2,1)S(1)}, bf16[256,768]{1,0:T(8,128)(2,1)S(1)}, u32[]{:S(2)}, u32[]{:S(2)}) collective-permute-start(bf16[256,768]{1,0:T(8,128)(2,1)S(1)} %pair_kernel.4.pair_ref), channel_id=1, source_target_pairs={{0,2},{2,0},{1,3},{3,1},{4,6},{6,4},{5,7},{7,5},{8,10},{10,8},{9,1... | collective-permute-start | bytes 1179656 | tf_op jit(solution)/shard_map/ppermute | solution.py:538
  14.0 9.4 %collective-permute-done.1.come_ref = bf16[256,768]{1,0:T(8,128)(2,1)S(1)} collective-permute-done((bf16[256,768]{1,0:T(8,128)(2,1)S(1)}, bf16[256,768]{1,0:T(8,128)(2,1)S(1)}, u32[]{:S(2)}, u32[]{:S(2)}) %collective-permute-start.1) | collective-permute-done | bytes 393248 | tf_op jit(solution)/shard_map/ppermute | solution.py:538
  25.4 1.7 %collective-permute-done.2.theirs_ref = bf16[256,768]{1,0:T(8,128)(2,1)S(1)} collective-permute-done((bf16[256,768]{1,0:T(8,128)(2,1)S(1)}, bf16[256,768]{1,0:T(8,128)(2,1)S(1)}, u32[]{:S(2)}, u32[]{:S(2)}) %collective-permute-start.2) | collective-permute-done | bytes 393248 | tf_op jit(solution)/shard_map/ppermute | solution.py:535
  27.2 3.7 %expert_kernel.1 = (bf16[512,768]{1,0:T(8,128)(2,1)S(1)}, bf16[512,768]{1,0:T(8,128)(2,1)S(1)}, bf16[256,768]{1,0:T(8,128)(2,1)S(1)}, bf16[256,768]{1,0:T(8,128)(2,1)S(1)}, f32[1,768]{1,0:T(1,128)S(1)}) custom-call(bf16[256,768]{1,0:T(8,128)(2,1)S(1)} %get-tuple-element.80.mine_ref, bf16[256,768]{1,0:T(8,128)(2,1)S(1)} %collective-permute-done.2.theirs_ref, ...), custom_call_target="tpu_custom_call" | custom-call | flops 1000 | bytes 1000 | tf_op jit(solution)/shard_map/expert_kernel/pallas_call | solution.py:30
  31.1 1.6 %collective-permute-done.3.come_ref = bf16[256,768]{1,0:T(8,128)(2,1)S(1)} collective-permute-done((bf16[256,768]{1,0:T(8,128)(2,1)S(1)}, bf16[256,768]{1,0:T(8,128)(2,1)S(1)}, u32[]{:S(2)}, u32[]{:S(2)}) %collective-permute-start.3) | collective-permute-done | bytes 393248 | tf_op jit(solution)/shard_map/ppermute | solution.py:535
  32.7 1.5 expert_weights_kernel.1
  34.2 1.4 copy-done.9
  35.6 7.9 %all-to-all-start = ((bf16[16,96,768]{2,1,0:T(8,128)(2,1)}), bf16[16,96,768]{2,1,0:T(8,128)(2,1)S(1)}, u32[]{:S(2)}, u32[]{:S(2)}) async-start(bf16[16,96,768]{2,1,0:T(8,128)(2,1)} %copy-done.9), calls=%async_computation | async-start | bytes 4718592 | tf_op jit(solution)/shard_map/all_to_all | solution.py:547
  43.5 3.3 %collective-permute-start.4 = (bf16[256,768]{1,0:T(8,128)(2,1)S(1)}, bf16[256,768]{1,0:T(8,128)(2,1)S(1)}, u32[]{:S(2)}, u32[]{:S(2)}) collective-permute-start(bf16[256,768]{1,0:T(8,128)(2,1)S(1)} %pair_kernel.5.pair_ref), channel_id=1, source_target_pairs={{0,2},{2,0},{1,3},{3,1},{4,6},{6,4},{5,7},{7,5},{8,10},{10,8},{9,1... | collective-permute-start | bytes 1179656 | tf_op jit(solution)/shard_map/ppermute | solution.py:538
  46.8 1.3 copy-done.2
  48.1 1.1 copy-done.20
  50.0 6.0 %collective-permute-done.4.come_ref = bf16[256,768]{1,0:T(8,128)(2,1)S(1)} collective-permute-done((bf16[256,768]{1,0:T(8,128)(2,1)S(1)}, bf16[256,768]{1,0:T(8,128)(2,1)S(1)}, u32[]{:S(2)}, u32[]{:S(2)}) %collective-permute-start.4) | collective-permute-done | bytes 393248 | tf_op jit(solution)/shard_map/ppermute | solution.py:538
  57.8 3.3 %collective-permute-start.7 = (bf16[256,768]{1,0:T(8,128)(2,1)S(1)}, bf16[256,768]{1,0:T(8,128)(2,1)S(1)}, u32[]{:S(2)}, u32[]{:S(2)}) collective-permute-start(bf16[256,768]{1,0:T(8,128)(2,1)S(1)} %pair_kernel.6.pair_ref), channel_id=1, source_target_pairs={{0,2},{2,0},{1,3},{3,1},{4,6},{6,4},{5,7},{7,5},{8,10},{10,8},{9,1... | collective-permute-start | bytes 1179656 | tf_op jit(solution)/shard_map/ppermute | solution.py:538
  61.1 3.3 %attend_back_kernel.1 = (bf16[576,512]{1,0:T(8,128)(2,1)S(1)}, bf16[16,48,768]{2,1,0:T(8,128)(2,1)S(1)}, f32[8,576]{1,0:T(8,128)S(1)}) custom-call(bf16[256,768]{1,0:T(8,128)(2,1)S(1)} %get-tuple-element.89.mine_ref, bf16[256,768]{1,0:T(8,128)(2,1)S(1)} %collective-permute-done.6.theirs_ref, bf16[192,768]{1,0:T(8,128)(2,1)S(1)} %copy-done.13, ...), custom_call_target="tpu_custom_call" | custom-call | flops 1000 | bytes 1000 | tf_op jit(solution)/shard_map/attend_back_kernel/pallas_call | solution.py:30
  64.4 6.1 %collective-permute-done.7.come_ref = bf16[256,768]{1,0:T(8,128)(2,1)S(1)} collective-permute-done((bf16[256,768]{1,0:T(8,128)(2,1)S(1)}, bf16[256,768]{1,0:T(8,128)(2,1)S(1)}, u32[]{:S(2)}, u32[]{:S(2)}) %collective-permute-start.7) | collective-permute-done | bytes 393248 | tf_op jit(solution)/shard_map/ppermute | solution.py:538
  71.4 1.7 %collective-permute-done.9.come_ref = bf16[256,768]{1,0:T(8,128)(2,1)S(1)} collective-permute-done((bf16[256,768]{1,0:T(8,128)(2,1)S(1)}, bf16[256,768]{1,0:T(8,128)(2,1)S(1)}, u32[]{:S(2)}, u32[]{:S(2)}) %collective-permute-start.9) | collective-permute-done | bytes 393248 | tf_op jit(solution)/shard_map/ppermute | solution.py:535
  73.2 3.3 %collective-permute-start.11 = (bf16[256,768]{1,0:T(8,128)(2,1)S(1)}, bf16[256,768]{1,0:T(8,128)(2,1)}, u32[]{:S(2)}, u32[]{:S(2)}) collective-permute-start(bf16[256,768]{1,0:T(8,128)(2,1)S(1)} %pair_kernel.7.pair_ref), channel_id=1, source_target_pairs={{0,2},{2,0},{1,3},{3,1},{4,6},{6,4},{5,7},{7,5},{8,10},{10,8},{9,1... | collective-permute-start | bytes 1179656 | tf_op jit(solution)/shard_map/ppermute | solution.py:538
  76.5 3.9 %all-to-all-done.parts_ref = bf16[16,96,768]{2,1,0:T(8,128)(2,1)S(1)} async-done(((bf16[16,96,768]{2,1,0:T(8,128)(2,1)}), bf16[16,96,768]{2,1,0:T(8,128)(2,1)S(1)}, u32[]{:S(2)}, u32[]{:S(2)}) %all-to-all-start) | async-done | bytes 2359328 | tf_op jit(solution)/shard_map/all_to_all | solution.py:547
  80.4 4.4 %all-to-all-start.1 = ((bf16[16,48,768]{2,1,0:T(8,128)(2,1)}), bf16[16,48,768]{2,1,0:T(8,128)(2,1)}, u32[]{:S(2)}, u32[]{:S(2)}) async-start(bf16[16,48,768]{2,1,0:T(8,128)(2,1)} %copy-done.15), calls=%async_computation.1 | async-start | bytes 2359296 | tf_op jit(solution)/shard_map/all_to_all | solution.py:547
  85.1 1.7 %collective-permute-start.10 = (bf16[96,768]{1,0:T(8,128)(2,1)S(1)}, bf16[96,768]{1,0:T(8,128)(2,1)S(1)}, u32[]{:S(2)}, u32[]{:S(2)}) collective-permute-start(bf16[96,768]{1,0:T(8,128)(2,1)S(1)} %total_kernel.1.pair_ref), channel_id=1, source_target_pairs={{0,4},{4,0},{1,5},{5,1},{2,6},{6,2},{3,7},{7,3},{8,12},{12,8},{9,1... | collective-permute-start | bytes 442376 | tf_op jit(solution)/shard_map/ppermute | solution.py:541
  86.8 3.6 %collective-permute-done.10.come_ref = bf16[96,768]{1,0:T(8,128)(2,1)S(1)} collective-permute-done((bf16[96,768]{1,0:T(8,128)(2,1)S(1)}, bf16[96,768]{1,0:T(8,128)(2,1)S(1)}, u32[]{:S(2)}, u32[]{:S(2)}) %collective-permute-start.10) | collective-permute-done | bytes 147488 | tf_op jit(solution)/shard_map/ppermute | solution.py:541
  90.3 1.7 %first_norm_kernel.1.mine_ref = f32[264,768]{1,0:T(8,128)S(1)} custom-call(bf16[512,768]{1,0:T(8,128)(2,1)S(1)} %bitcast.12, bf16[256,768]{1,0:T(8,128)(2,1)S(1)} %pair_kernel.7.pair_ref, bf16[256,768]{1,0:T(8,128)(2,1)} %collective-permute-done.11.come_ref, f32[768]{0:T(1024)S(1)} %copy-done.33, f32[256,768]{1,0:T(8,128)S(1)} %copy-done.18, ...), custom_call_target="tpu_custom_call" | custom-call | flops 1000 | bytes 1000 | tf_op jit(solution)/shard_map/first_norm_kernel/pallas_call | solution.py:30
  92.2 1.8 %collective-permute-start.13 = (bf16[48,768]{1,0:T(8,128)(2,1)S(1)}, bf16[48,768]{1,0:T(8,128)(2,1)S(1)}, u32[]{:S(2)}, u32[]{:S(2)}) collective-permute-start(bf16[48,768]{1,0:T(8,128)(2,1)S(1)} %get-tuple-element.107.refs_0_), channel_id=1, source_target_pairs={{0,32},{32,0},{64,96},{96,64},{1,33},{33,1},{65,97},{97,65},{2,34}... | collective-permute-start | bytes 221192 | tf_op jit(solution)/shard_map/ppermute | solution.py:554
  94.0 1.5 collective-permute-start.14
  95.5 5.5 %collective-permute-done.13.refs_2_ = bf16[48,768]{1,0:T(8,128)(2,1)S(1)} collective-permute-done((bf16[48,768]{1,0:T(8,128)(2,1)S(1)}, bf16[48,768]{1,0:T(8,128)(2,1)S(1)}, u32[]{:S(2)}, u32[]{:S(2)}) %collective-permute-start.13) | collective-permute-done | bytes 73760 | tf_op jit(solution)/shard_map/ppermute | solution.py:554
  101.1 1.3 token_order_kernel.1
  102.4 1.2 all-to-all-done.1.parts_ref
  103.6 1.4 attend_total_kernel.1.pair_ref
  105.0 1.1 collective-permute-start.16
  106.2 2.1 %collective-permute-start.17 = (bf16[96,768]{1,0:T(8,128)(2,1)S(1)}, bf16[96,768]{1,0:T(8,128)(2,1)S(1)}, u32[]{:S(2)}, u32[]{:S(2)}) collective-permute-start(bf16[96,768]{1,0:T(8,128)(2,1)S(1)} %get-tuple-element.118.refs_1_), channel_id=1, source_target_pairs={{0,24},{8,16},{16,8},{24,0},{1,25},{9,17},{17,9},{25,1},{2,26},{10... | collective-permute-start | bytes 442376 | tf_op jit(solution)/shard_map/ppermute | solution.py:554
  108.2 3.2 %collective-permute-done.16.refs_2_ = bf16[96,768]{1,0:T(8,128)(2,1)S(1)} collective-permute-done((bf16[96,768]{1,0:T(8,128)(2,1)S(1)}, bf16[96,768]{1,0:T(8,128)(2,1)S(1)}, u32[]{:S(2)}, u32[]{:S(2)}) %collective-permute-start.16) | collective-permute-done | bytes 147488 | tf_op jit(solution)/shard_map/ppermute | solution.py:554
  111.5 1.1 collective-permute-done.17.refs_3_
  113.3 2.1 %collective-permute-start.19 = (bf16[192,768]{1,0:T(8,128)(2,1)}, bf16[192,768]{1,0:T(8,128)(2,1)S(1)}, u32[]{:S(2)}, u32[]{:S(2)}) collective-permute-start(bf16[192,768]{1,0:T(8,128)(2,1)} %get-tuple-element.119.refs_0_), channel_id=1, source_target_pairs={{0,24},{8,0},{16,8},{24,16},{1,25},{9,1},{17,9},{25,17},{2,26},{10... | collective-permute-start | bytes 884744 | tf_op jit(solution)/shard_map/ppermute | solution.py:565
  115.4 2.2 %collective-permute-start.21 = (bf16[192,768]{1,0:T(8,128)(2,1)S(1)}, bf16[192,768]{1,0:T(8,128)(2,1)S(1)}, u32[]{:S(2)}, u32[]{:S(2)}) collective-permute-start(bf16[192,768]{1,0:T(8,128)(2,1)S(1)} %get-tuple-element.120.refs_3_), channel_id=1, source_target_pairs={{0,96},{32,0},{64,32},{96,64},{1,97},{33,1},{65,33},{97,65},{2,98}... | collective-permute-start | bytes 884744 | tf_op jit(solution)/shard_map/ppermute | solution.py:565
  117.5 1.6 collective-permute-start.15
  119.1 2.9 %collective-permute-done.15.come_ref = bf16[56,768]{1,0:T(8,128)(2,1)S(1)} collective-permute-done((bf16[56,768]{1,0:T(8,128)(2,1)S(1)}, bf16[56,768]{1,0:T(8,128)(2,1)S(1)}, u32[]{:S(2)}, u32[]{:S(2)}) %collective-permute-start.15) | collective-permute-done | bytes 86048 | tf_op jit(solution)/shard_map/ppermute | solution.py:541
  122.0 2.0 %collective-permute-done.18.refs_1_ = bf16[192,768]{1,0:T(8,128)(2,1)S(1)} collective-permute-done((bf16[192,768]{1,0:T(8,128)(2,1)}, bf16[192,768]{1,0:T(8,128)(2,1)S(1)}, u32[]{:S(2)}, u32[]{:S(2)}) %collective-permute-start.18) | collective-permute-done | bytes 294944 | tf_op jit(solution)/shard_map/ppermute | solution.py:565
  126.2 1.2 attend_finish_kernel.1
  127.4 4.8 %all-to-all-start.2 = ((bf16[16,56,768]{2,1,0:T(8,128)(2,1)}), bf16[16,56,768]{2,1,0:T(8,128)(2,1)S(1)}, u32[]{:S(2)}, u32[]{:S(2)}) async-start(bf16[16,56,768]{2,1,0:T(8,128)(2,1)} %attend_finish_kernel.1), calls=%async_computation.2 | async-start | bytes 2752512 | tf_op jit(solution)/shard_map/all_to_all | solution.py:547
  132.5 3.5 %collective-permute-start.22 = (bf16[192,768]{1,0:T(8,128)(2,1)}, bf16[192,768]{1,0:T(8,128)(2,1)S(1)}, u32[]{:S(2)}, u32[]{:S(2)}) collective-permute-start(bf16[192,768]{1,0:T(8,128)(2,1)} %get-tuple-element.119.refs_0_), channel_id=1, source_target_pairs={{0,16},{8,24},{16,0},{24,8},{1,17},{9,25},{17,1},{25,9},{2,18},{10... | collective-permute-start | bytes 884744 | tf_op jit(solution)/shard_map/ppermute | solution.py:565
  136.0 3.0 %collective-permute-start.23 = (bf16[192,768]{1,0:T(8,128)(2,1)S(1)}, bf16[192,768]{1,0:T(8,128)(2,1)S(1)}, u32[]{:S(2)}, u32[]{:S(2)}) collective-permute-start(bf16[192,768]{1,0:T(8,128)(2,1)S(1)} %copy-done.26), channel_id=1, source_target_pairs={{0,64},{32,96},{64,0},{96,32},{1,65},{33,97},{65,1},{97,33},{2,66}... | collective-permute-start | bytes 884744 | tf_op jit(solution)/shard_map/ppermute | solution.py:565
  139.0 0.9 mixed_order_kernel.1
  140.0 3.8 %expert_most_kernel.1 = (f32[768,768]{1,0:T(8,128)}, f32[768,768]{1,0:T(8,128)}) custom-call(bf16[192,768]{1,0:T(8,128)(2,1)} %get-tuple-element.119.refs_0_, bf16[192,768]{1,0:T(8,128)(2,1)} %copy-done.39, bf16[192,768]{1,0:T(8,128)(2,1)} %copy-done.38, bf16[192,768]{1,0:T(8,128)(2,1)} %copy-done.25, bf16[192,768]{1,0:T(8,128)(2,1)} %collective-permute-done.20.refs_4_, ...), custom_call_target="tpu_custom_call" | custom-call | flops 1000 | bytes 1000 | tf_op jit(solution)/shard_map/expert_most_kernel/pallas_call | solution.py:30
  143.7 11.1 %collective-permute-done.22.a_ref = bf16[192,768]{1,0:T(8,128)(2,1)S(1)} collective-permute-done((bf16[192,768]{1,0:T(8,128)(2,1)}, bf16[192,768]{1,0:T(8,128)(2,1)S(1)}, u32[]{:S(2)}, u32[]{:S(2)}) %collective-permute-start.22) | collective-permute-done | bytes 294944 | tf_op jit(solution)/shard_map/ppermute | solution.py:565
  155.3 2.5 %last_kernel.1 = (f32[768,768]{1,0:T(8,128)}, f32[768,768]{1,0:T(8,128)}, f32[576,768]{1,0:T(8,128)}, f32[192,768]{1,0:T(8,128)}, f32[3,128]{1,0:T(4,128)}, /*in...) custom-call(bf16[16,56,768]{2,1,0:T(8,128)(2,1)S(1)} %all-to-all-don, ...), custom_call_target="tpu_custom_call", output_to_operand_aliasing={{0}: (3, {}), {1}: (4, {})} | custom-call | flops 1000 | bytes 1000 | tf_op jit(solution)/shard_map/last_kernel/pallas_call | solution.py:30
  (112 shorter events, 10.1 us)
Async XLA Ops:
  0.6 26.5 %copy-start.36 = (f32[768]{0:T(1024)S(1)}, f32[768]{0:T(1024)}, u32[]{:S(2)}) copy-start(f32[768]{0:T(1024)} %bias_ref.6) | copy-start | bytes 9220
  0.7 22.8 %copy-start = (bf16[1,512,768]{2,1,0:T(8,128)(2,1)S(1)}, bf16[1,512,768]{2,1,0:T(8,128)(2,1)}, u32[]{:S(2)}) copy-start(bf16[1,512,768]{2,1,0:T(8,128)(2,1)} %param.15) | copy-start | bytes 2359300
  0.7 22.8 %copy-start.32 = (f32[768]{0:T(1024)S(1)}, f32[768]{0:T(1024)}, u32[]{:S(2)}) copy-start(f32[768]{0:T(1024)} %gain_ref.6) | copy-start | bytes 9220
  0.7 22.8 %copy-start.34 = (f32[768]{0:T(1024)S(1)}, f32[768]{0:T(1024)}, u32[]{:S(2)}) copy-start(f32[768]{0:T(1024)} %bias_ref.5) | copy-start | bytes 9220
  0.7 26.5 %copy-start.14 = (bf16[768,768]{1,0:T(8,128)(2,1)S(1)}, bf16[768,768]{1,0:T(8,128)(2,1)}, u32[]{:S(2)}) copy-start(bf16[768,768]{1,0:T(8,128)(2,1)} %up_ref.1) | copy-start | bytes 3538948
  7.6 19.6 %copy-start.1 = (bf16[768,768]{1,0:T(8,128)(2,1)S(1)}, bf16[768,768]{1,0:T(8,128)(2,1)}, u32[]{:S(2)}) copy-start(bf16[768,768]{1,0:T(8,128)(2,1)} %down_ref.3) | copy-start | bytes 3538948
  7.6 19.6 %copy-start.4 = (bf16[1,512,768]{2,1,0:T(8,128)(2,1)S(1)}, bf16[1,512,768]{2,1,0:T(8,128)(2,1)}, u32[]{:S(2)}) copy-start(bf16[1,512,768]{2,1,0:T(8,128)(2,1)} %param.29) | copy-start | bytes 2359300
  7.6 2.0 %collective-permute-start = (bf16[256,768]{1,0:T(8,128)(2,1)}, bf16[256,768]{1,0:T(8,128)(2,1)S(1)}, u32[]{:S(2)}, u32[]{:S(2)}) collective-permute-start(bf16[256,768]{1,0:T(8,128)(2,1)} %get-tuple-element.78), channel_id=1, source_target_pairs={{0,1},{1,0},{2,3},{3,2},{4,5},{5,4},{6,7},{7,6},{8,9},{9,8},{10,11... | collective-permute-start | bytes 1179656 | tf_op jit(solution)/shard_map/ppermute | solution.py:535
  10.7 12.8 %collective-permute-start.1 = (bf16[256,768]{1,0:T(8,128)(2,1)S(1)}, bf16[256,768]{1,0:T(8,128)(2,1)S(1)}, u32[]{:S(2)}, u32[]{:S(2)}) collective-permute-start(bf16[256,768]{1,0:T(8,128)(2,1)S(1)} %pair_kernel.4.pair_ref), channel_id=1, source_target_pairs={{0,2},{2,0},{1,3},{3,1},{4,6},{6,4},{5,7},{7,5},{8,10},{10,8},{9,1... | collective-permute-start | bytes 1179656 | tf_op jit(solution)/shard_map/ppermute | solution.py:538
  25.4 1.7 %collective-permute-start.2 = (bf16[256,768]{1,0:T(8,128)(2,1)S(1)}, bf16[256,768]{1,0:T(8,128)(2,1)S(1)}, u32[]{:S(2)}, u32[]{:S(2)}) collective-permute-start(bf16[256,768]{1,0:T(8,128)(2,1)S(1)} %get-tuple-element.80.mine_ref), channel_id=1, source_target_pairs={{0,1},{1,0},{2,3},{3,2},{4,5},{5,4},{6,7},{7,6},{8,9},{9,8},{10,11... | collective-permute-start | bytes 1179656 | tf_op jit(solution)/shard_map/ppermute | solution.py:535
  30.9 1.8 %collective-permute-start.3 = (bf16[256,768]{1,0:T(8,128)(2,1)S(1)}, bf16[256,768]{1,0:T(8,128)(2,1)S(1)}, u32[]{:S(2)}, u32[]{:S(2)}) collective-permute-start(bf16[256,768]{1,0:T(8,128)(2,1)S(1)} %get-tuple-element.82), channel_id=1, source_target_pairs={{0,1},{1,0},{2,3},{3,2},{4,5},{5,4},{6,7},{7,6},{8,9},{9,8},{10,11... | collective-permute-start | bytes 1179656 | tf_op jit(solution)/shard_map/ppermute | solution.py:535
  35.6 44.8 %all-to-all-start = ((bf16[16,96,768]{2,1,0:T(8,128)(2,1)}), bf16[16,96,768]{2,1,0:T(8,128)(2,1)S(1)}, u32[]{:S(2)}, u32[]{:S(2)}) async-start(bf16[16,96,768]{2,1,0:T(8,128)(2,1)} %copy-done.9), calls=%async_computation | async-start | bytes 4718592 | tf_op jit(solution)/shard_map/all_to_all | solution.py:547
  43.5 12.5 %collective-permute-start.4 = (bf16[256,768]{1,0:T(8,128)(2,1)S(1)}, bf16[256,768]{1,0:T(8,128)(2,1)S(1)}, u32[]{:S(2)}, u32[]{:S(2)}) collective-permute-start(bf16[256,768]{1,0:T(8,128)(2,1)S(1)} %pair_kernel.5.pair_ref), channel_id=1, source_target_pairs={{0,2},{2,0},{1,3},{3,1},{4,6},{6,4},{5,7},{7,5},{8,10},{10,8},{9,1... | collective-permute-start | bytes 1179656 | tf_op jit(solution)/shard_map/ppermute | solution.py:538
  49.2 6.8 %copy-start.5 = (bf16[1,512,768]{2,1,0:T(8,128)(2,1)S(1)}, bf16[1,512,768]{2,1,0:T(8,128)(2,1)}, u32[]{:S(2)}) copy-start(bf16[1,512,768]{2,1,0:T(8,128)(2,1)} %param.29) | copy-start | bytes 2359300
  49.2 6.8 %copy-start.7 = (f32[256,768]{1,0:T(8,128)S(1)}, f32[256,768]{1,0:T(8,128)}, u32[]{:S(2)}) copy-start(f32[256,768]{1,0:T(8,128)} %copy-done.6) | copy-start | bytes 2359300
  56.0 1.7 %collective-permute-start.5 = (bf16[256,768]{1,0:T(8,128)(2,1)S(1)}, bf16[256,768]{1,0:T(8,128)(2,1)S(1)}, u32[]{:S(2)}, u32[]{:S(2)}) collective-permute-start(bf16[256,768]{1,0:T(8,128)(2,1)S(1)} %get-tuple-element.88), channel_id=1, source_target_pairs={{0,1},{1,0},{2,3},{3,2},{4,5},{5,4},{6,7},{7,6},{8,9},{9,8},{10,11... | collective-permute-start | bytes 1179656 | tf_op jit(solution)/shard_map/ppermute | solution.py:535
  56.0 5.1 %copy-start.10 = (bf16[3,512,512]{2,1,0:T(8,128)(2,1)S(1)}, bf16[3,512,512]{2,1,0:T(8,128)(2,1)}, u32[]{:S(2)}) copy-start(bf16[3,512,512]{2,1,0:T(8,128)(2,1)} %get-tuple-element.90.probs_ref) | copy-start | bytes 4718596
  56.0 5.1 %copy-start.13 = (bf16[192,768]{1,0:T(8,128)(2,1)S(1)}, bf16[192,768]{1,0:T(8,128)(2,1)}, u32[]{:S(2)}) copy-start(bf16[192,768]{1,0:T(8,128)(2,1)} %out_ref.3) | copy-start | bytes 884740
  56.9 7.5 %copy-start.28 = (f32[8,768]{1,0:T(8,128)}, f32[8,768]{1,0:T(8,128)S(1)}, u32[]{:S(2)}) copy-start(f32[8,768]{1,0:T(8,128)S(1)} %get-tuple-element.102.rows_ref) | copy-start | bytes 73732
  56.9 4.1 %collective-permute-start.6 = (bf16[256,768]{1,0:T(8,128)(2,1)S(1)}, bf16[256,768]{1,0:T(8,128)(2,1)S(1)}, u32[]{:S(2)}, u32[]{:S(2)}) collective-permute-start(bf16[256,768]{1,0:T(8,128)(2,1)S(1)} %get-tuple-element.89.mine_ref), channel_id=1, source_target_pairs={{0,1},{1,0},{2,3},{3,2},{4,5},{5,4},{6,7},{7,6},{8,9},{9,8},{10,11... | collective-permute-start | bytes 1179656 | tf_op jit(solution)/shard_map/ppermute | solution.py:535
  57.8 6.7 %copy-start.11 = (bf16[256,768]{1,0:T(8,128)(2,1)}, bf16[256,768]{1,0:T(8,128)(2,1)S(1)}, u32[]{:S(2)}) copy-start(bf16[256,768]{1,0:T(8,128)(2,1)S(1)} %pair_kernel.6.pair_ref) | copy-start | bytes 1179652
  57.8 12.7 %collective-permute-start.7 = (bf16[256,768]{1,0:T(8,128)(2,1)S(1)}, bf16[256,768]{1,0:T(8,128)(2,1)S(1)}, u32[]{:S(2)}, u32[]{:S(2)}) collective-permute-start(bf16[256,768]{1,0:T(8,128)(2,1)S(1)} %pair_kernel.6.pair_ref), channel_id=1, source_target_pairs={{0,2},{2,0},{1,3},{3,1},{4,6},{6,4},{5,7},{7,5},{8,10},{10,8},{9,1... | collective-permute-start | bytes 1179656 | tf_op jit(solution)/shard_map/ppermute | solution.py:538
  61.1 9.4 %copy-start.3 = (bf16[768,3,192]{0,2,1:T(8,128)(2,1)S(1)}, bf16[768,3,192]{0,2,1:T(8,128)(2,1)}, u32[]{:S(2)}) copy-start(bf16[768,3,192]{0,2,1:T(8,128)(2,1)} %param.19) | copy-start | bytes 2654212
  64.4 8.8 %copy-start.15 = (bf16[16,48,768]{2,1,0:T(8,128)(2,1)}, bf16[16,48,768]{2,1,0:T(8,128)(2,1)S(1)}, u32[]{:S(2)}) copy-start(bf16[16,48,768]{2,1,0:T(8,128)(2,1)S(1)} %get-tuple-element.114) | copy-start | bytes 3538948
  64.4 8.8 %copy-start.30 = (f32[8,576]{1,0:T(8,128)}, f32[8,576]{1,0:T(8,128)S(1)}, u32[]{:S(2)}) copy-start(f32[8,576]{1,0:T(8,128)S(1)} %get-tuple-element.104.qkv_ref) | copy-start | bytes 55300
  71.3 1.8 %collective-permute-start.9 = (bf16[256,768]{1,0:T(8,128)(2,1)S(1)}, bf16[256,768]{1,0:T(8,128)(2,1)S(1)}, u32[]{:S(2)}, u32[]{:S(2)}) collective-permute-start(bf16[256,768]{1,0:T(8,128)(2,1)S(1)} %get-tuple-element.98), channel_id=1, source_target_pairs={{0,1},{1,0},{2,3},{3,2},{4,5},{5,4},{6,7},{7,6},{8,9},{9,8},{10,11... | collective-permute-start | bytes 1179656 | tf_op jit(solution)/shard_map/ppermute | solution.py:535
  73.2 13.6 %collective-permute-start.11 = (bf16[256,768]{1,0:T(8,128)(2,1)S(1)}, bf16[256,768]{1,0:T(8,128)(2,1)}, u32[]{:S(2)}, u32[]{:S(2)}) collective-permute-start(bf16[256,768]{1,0:T(8,128)(2,1)S(1)} %pair_kernel.7.pair_ref), channel_id=1, source_target_pairs={{0,2},{2,0},{1,3},{3,1},{4,6},{6,4},{5,7},{7,5},{8,10},{10,8},{9,1... | collective-permute-start | bytes 1179656 | tf_op jit(solution)/shard_map/ppermute | solution.py:538
  80.4 23.2 %all-to-all-start.1 = ((bf16[16,48,768]{2,1,0:T(8,128)(2,1)}), bf16[16,48,768]{2,1,0:T(8,128)(2,1)}, u32[]{:S(2)}, u32[]{:S(2)}) async-start(bf16[16,48,768]{2,1,0:T(8,128)(2,1)} %copy-done.15), calls=%async_computation.1 | async-start | bytes 2359296 | tf_op jit(solution)/shard_map/all_to_all | solution.py:547
  84.8 5.6 %copy-start.18 = (f32[256,768]{1,0:T(8,128)S(1)}, f32[256,768]{1,0:T(8,128)}, u32[]{:S(2)}) copy-start(f32[256,768]{1,0:T(8,128)} %copy-done.17) | copy-start | bytes 2359300
  84.8 5.6 %copy-start.29 = (f32[8,768]{1,0:T(8,128)S(1)}, f32[8,768]{1,0:T(8,128)}, u32[]{:S(2)}) copy-start(f32[8,768]{1,0:T(8,128)} %copy-done.28) | copy-start | bytes 73732
  84.8 5.6 %copy-start.33 = (f32[768]{0:T(1024)S(1)}, f32[768]{0:T(1024)}, u32[]{:S(2)}) copy-start(f32[768]{0:T(1024)} %gain_ref.7) | copy-start | bytes 9220
  85.1 5.2 %collective-permute-start.10 = (bf16[96,768]{1,0:T(8,128)(2,1)S(1)}, bf16[96,768]{1,0:T(8,128)(2,1)S(1)}, u32[]{:S(2)}, u32[]{:S(2)}) collective-permute-start(bf16[96,768]{1,0:T(8,128)(2,1)S(1)} %total_kernel.1.pair_ref), channel_id=1, source_target_pairs={{0,4},{4,0},{1,5},{5,1},{2,6},{6,2},{3,7},{7,3},{8,12},{12,8},{9,1... | collective-permute-start | bytes 442376 | tf_op jit(solution)/shard_map/ppermute | solution.py:541
  90.3 10.8 %copy-start.31 = (f32[8,576]{1,0:T(8,128)S(1)}, f32[8,576]{1,0:T(8,128)}, u32[]{:S(2)}) copy-start(f32[8,576]{1,0:T(8,128)} %copy-done.30) | copy-start | bytes 55300
  92.1 9.0 %collective-permute-start.12 = (f32[264,768]{1,0:T(8,128)S(1)}, f32[264,768]{1,0:T(8,128)S(1)}, u32[]{:S(2)}, u32[]{:S(2)}) collective-permute-start(f32[264,768]{1,0:T(8,128)S(1)} %first_norm_kernel.1.mine_ref), channel_id=1, source_target_pairs={{0,1},{1,0},{2,3},{3,2},{4,5},{5,4},{6,7},{7,6},{8,9},{9,8},{10,11... | collective-permute-start | bytes 2433032 | tf_op jit(solution)/shard_map/ppermute | solution.py:535
  92.2 8.9 %collective-permute-start.13 = (bf16[48,768]{1,0:T(8,128)(2,1)S(1)}, bf16[48,768]{1,0:T(8,128)(2,1)S(1)}, u32[]{:S(2)}, u32[]{:S(2)}) collective-permute-start(bf16[48,768]{1,0:T(8,128)(2,1)S(1)} %get-tuple-element.107.refs_0_), channel_id=1, source_target_pairs={{0,32},{32,0},{64,96},{96,64},{1,33},{33,1},{65,97},{97,65},{2,34}... | collective-permute-start | bytes 221192 | tf_op jit(solution)/shard_map/ppermute | solution.py:554
  94.0 7.0 %collective-permute-start.14 = (bf16[48,768]{1,0:T(8,128)(2,1)S(1)}, bf16[48,768]{1,0:T(8,128)(2,1)S(1)}, u32[]{:S(2)}, u32[]{:S(2)}) collective-permute-start(bf16[48,768]{1,0:T(8,128)(2,1)S(1)} %get-tuple-element.108.refs_1_), channel_id=1, source_target_pairs={{0,8},{8,0},{16,24},{24,16},{1,9},{9,1},{17,25},{25,17},{2,10},{10... | collective-permute-start | bytes 221192 | tf_op jit(solution)/shard_map/ppermute | solution.py:554
  105.0 6.4 %collective-permute-start.16 = (bf16[96,768]{1,0:T(8,128)(2,1)S(1)}, bf16[96,768]{1,0:T(8,128)(2,1)S(1)}, u32[]{:S(2)}, u32[]{:S(2)}) collective-permute-start(bf16[96,768]{1,0:T(8,128)(2,1)S(1)} %get-tuple-element.117.refs_0_), channel_id=1, source_target_pairs={{0,96},{32,64},{64,32},{96,0},{1,97},{33,65},{65,33},{97,1},{2,98}... | collective-permute-start | bytes 442376 | tf_op jit(solution)/shard_map/ppermute | solution.py:554
  106.2 6.4 %collective-permute-start.17 = (bf16[96,768]{1,0:T(8,128)(2,1)S(1)}, bf16[96,768]{1,0:T(8,128)(2,1)S(1)}, u32[]{:S(2)}, u32[]{:S(2)}) collective-permute-start(bf16[96,768]{1,0:T(8,128)(2,1)S(1)} %get-tuple-element.118.refs_1_), channel_id=1, source_target_pairs={{0,24},{8,16},{16,8},{24,0},{1,25},{9,17},{17,9},{25,1},{2,26},{10... | collective-permute-start | bytes 442376 | tf_op jit(solution)/shard_map/ppermute | solution.py:554
  113.3 12.9 %copy-start.25 = (bf16[192,768]{1,0:T(8,128)(2,1)}, bf16[192,768]{1,0:T(8,128)(2,1)S(1)}, u32[]{:S(2)}) copy-start(bf16[192,768]{1,0:T(8,128)(2,1)S(1)} %get-tuple-element.120.refs_3_) | copy-start | bytes 884740
  113.3 8.7 %collective-permute-start.19 = (bf16[192,768]{1,0:T(8,128)(2,1)}, bf16[192,768]{1,0:T(8,128)(2,1)S(1)}, u32[]{:S(2)}, u32[]{:S(2)}) collective-permute-start(bf16[192,768]{1,0:T(8,128)(2,1)} %get-tuple-element.119.refs_0_), channel_id=1, source_target_pairs={{0,24},{8,0},{16,8},{24,16},{1,25},{9,1},{17,9},{25,17},{2,26},{10... | collective-permute-start | bytes 884744 | tf_op jit(solution)/shard_map/ppermute | solution.py:565
  115.4 8.6 %collective-permute-start.18 = (bf16[192,768]{1,0:T(8,128)(2,1)}, bf16[192,768]{1,0:T(8,128)(2,1)S(1)}, u32[]{:S(2)}, u32[]{:S(2)}) collective-permute-start(bf16[192,768]{1,0:T(8,128)(2,1)} %get-tuple-element.119.refs_0_), channel_id=1, source_target_pairs={{0,8},{8,16},{16,24},{24,0},{1,9},{9,17},{17,25},{25,1},{2,10},{10... | collective-permute-start | bytes 884744 | tf_op jit(solution)/shard_map/ppermute | solution.py:565
  115.4 8.6 %collective-permute-start.21 = (bf16[192,768]{1,0:T(8,128)(2,1)S(1)}, bf16[192,768]{1,0:T(8,128)(2,1)S(1)}, u32[]{:S(2)}, u32[]{:S(2)}) collective-permute-start(bf16[192,768]{1,0:T(8,128)(2,1)S(1)} %get-tuple-element.120.refs_3_), channel_id=1, source_target_pairs={{0,96},{32,0},{64,32},{96,64},{1,97},{33,1},{65,33},{97,65},{2,98}... | collective-permute-start | bytes 884744 | tf_op jit(solution)/shard_map/ppermute | solution.py:565
  117.5 8.7 %collective-permute-start.20 = (bf16[192,768]{1,0:T(8,128)(2,1)S(1)}, bf16[192,768]{1,0:T(8,128)(2,1)}, u32[]{:S(2)}, u32[]{:S(2)}) collective-permute-start(bf16[192,768]{1,0:T(8,128)(2,1)S(1)} %get-tuple-element.120.refs_3_), channel_id=1, source_target_pairs={{0,32},{32,64},{64,96},{96,0},{1,33},{33,65},{65,97},{97,1},{2,34}... | collective-permute-start | bytes 884744 | tf_op jit(solution)/shard_map/ppermute | solution.py:565
  117.5 4.5 %collective-permute-start.15 = (bf16[56,768]{1,0:T(8,128)(2,1)S(1)}, bf16[56,768]{1,0:T(8,128)(2,1)S(1)}, u32[]{:S(2)}, u32[]{:S(2)}) collective-permute-start(bf16[56,768]{1,0:T(8,128)(2,1)S(1)} %attend_total_kernel.1.pair_ref), channel_id=1, source_target_pairs={{0,4},{4,0},{1,5},{5,1},{2,6},{6,2},{3,7},{7,3},{8,12},{12,8},{9,1... | collective-permute-start | bytes 258056 | tf_op jit(solution)/shard_map/ppermute | solution.py:541
  127.4 27.9 %all-to-all-start.2 = ((bf16[16,56,768]{2,1,0:T(8,128)(2,1)}), bf16[16,56,768]{2,1,0:T(8,128)(2,1)S(1)}, u32[]{:S(2)}, u32[]{:S(2)}) async-start(bf16[16,56,768]{2,1,0:T(8,128)(2,1)} %attend_finish_kernel.1), calls=%async_computation.2 | async-start | bytes 2752512 | tf_op jit(solution)/shard_map/all_to_all | solution.py:547
  132.4 6.6 %collective-permute-start.8 = (bf16[256,768]{1,0:T(8,128)(2,1)S(1)}, bf16[256,768]{1,0:T(8,128)(2,1)S(1)}, u32[]{:S(2)}, u32[]{:S(2)}) collective-permute-start(bf16[256,768]{1,0:T(8,128)(2,1)S(1)} %mixed_kernel.1.mine_ref), channel_id=1, source_target_pairs={{0,1},{1,0},{2,3},{3,2},{4,5},{5,4},{6,7},{7,6},{8,9},{9,8},{10,11... | collective-permute-start | bytes 1179656 | tf_op jit(solution)/shard_map/ppermute | solution.py:535
  132.5 22.3 %collective-permute-start.22 = (bf16[192,768]{1,0:T(8,128)(2,1)}, bf16[192,768]{1,0:T(8,128)(2,1)S(1)}, u32[]{:S(2)}, u32[]{:S(2)}) collective-permute-start(bf16[192,768]{1,0:T(8,128)(2,1)} %get-tuple-element.119.refs_0_), channel_id=1, source_target_pairs={{0,16},{8,24},{16,0},{24,8},{1,17},{9,25},{17,1},{25,9},{2,18},{10... | collective-permute-start | bytes 884744 | tf_op jit(solution)/shard_map/ppermute | solution.py:565
  136.0 19.3 %collective-permute-start.23 = (bf16[192,768]{1,0:T(8,128)(2,1)S(1)}, bf16[192,768]{1,0:T(8,128)(2,1)S(1)}, u32[]{:S(2)}, u32[]{:S(2)}) collective-permute-start(bf16[192,768]{1,0:T(8,128)(2,1)S(1)} %copy-done.26), channel_id=1, source_target_pairs={{0,64},{32,96},{64,0},{96,32},{1,65},{33,97},{65,1},{97,33},{2,66}... | collective-permute-start | bytes 884744 | tf_op jit(solution)/shard_map/ppermute | solution.py:565
  (20 other events, 58.3 us)

commit v4 on v3

--- a/solution.py
+++ b/solution.py
@@ -456,11 +456,13 @@
         copies_ref[copy] = total
 
 
-def last_kernel(parts_ref, a_ref, b_ref, down_in, up_in, down_ref, up_ref, qkv_ref, out_ref, qv_ref, *refs):
+def last_kernel(parts_ref, a_low, a_high, b_low, b_high, down_in, up_in, down_ref, up_ref, qkv_ref, out_ref, qv_ref, *refs):
     *vector_refs, a_full, b_full, semaphores = refs
-    rows = a_ref.shape[0]
+    half = a_low.shape[0]
+    rows = 2 * half
     side = down_ref.shape[0] // rows
-    a_full[...] = a_ref[...].astype(F32)
+    a_full[:half, :] = a_low[...].astype(F32)
+    a_full[half:, :] = a_high[...].astype(F32)
     leaving = []
     source = lax.rem(lax.axis_index("x") + 2, side)
     for z in range(side):
@@ -473,7 +475,8 @@
             )
         )
         leaving[-1].start()
-    b_full[...] = b_ref[...].astype(F32)
+    b_full[:half, :] = b_low[...].astype(F32)
+    b_full[half:, :] = b_high[...].astype(F32)
     at = pl.multiple_of(lax.rem(lax.axis_index("z") + 2, side) * rows, rows)
     leaving.append(
         pltpu.make_async_copy(b_full, up_ref.at[pl.ds(at, rows)], semaphores.at[side])
@@ -560,10 +563,8 @@
         kernel.__name__ = "join_kernel"
         return kernel
 
-    def along(block, axis):
-        moves = [[(i, (i + shift) % side) for i in range(side)] for shift in range(1, side)]
-        far, near, back = (lax.ppermute(block, axis, moves[i]) for i in (1, 0, 2))
-        return (block, near, far, back)
+    def onward(block, axis, shift):
+        return lax.ppermute(block, axis, [(i, (i + shift) % side) for i in range(side)])
 
     half_low, half_full = ((half, features), BF), ((half, features), F32)
     row_low, row_full = ((length, features), BF), ((length, features), F32)
@@ -648,18 +649,19 @@
     blocks, pair = lax.optimization_barrier((blocks, pair))
     step = (exchange(blocks[0], "z", 1), exchange(blocks[1], "x", 1))
     blocks = call(joiner(("z", "x"), 1), (((4 * each, features), BF),) * 2)(*blocks, *step)
-    down_blocks, up_blocks = along(blocks[0], "x"), along(blocks[1], "z")
+    down_own, up_own = blocks
+    down_near, down_back = onward(down_own, "x", 1), onward(down_own, "x", side - 1)
+    up_near, up_back = onward(up_own, "z", 1), onward(up_own, "z", side - 1)
     (mixed,) = call(mixed_kernel, (half_low,))(resid, mixed_pair, mixed_come, down_bias)
     (mixed,) = call(mixed_order_kernel, (row_low,))(mixed, core_swap(mixed))
 
     rows = pair.shape[0]
     come = near_swap(pair)
-    down_own, down_near, down_far, down_back = down_blocks
-    up_own, up_near, up_far, up_back = up_blocks
     come, down_near, down_back, up_near, up_back = lax.optimization_barrier(
         (come, down_near, down_back, up_near, up_back)
     )
     (copies,) = call(attend_finish_kernel, (((plane, rows, features), BF),))(pair, come)
+    halves = (down_near[: 2 * each], down_back[2 * each :], up_near[: 2 * each], up_back[2 * each :])
     gathered = scatter(copies)
     down_grad, up_weight_grad = call(
         expert_most_kernel,
@@ -667,16 +669,22 @@
         place=None,
         limit=60 << 20,
     )(down_own, down_near, down_back, up_own, up_near, up_back)
-    block = down_far.shape
+    far = (
+        onward(halves[0], "x", 1),
+        onward(halves[1], "x", side - 1),
+        onward(halves[2], "z", 1),
+        onward(halves[3], "z", side - 1),
+    )
+    block = down_own.shape
     down_grad, up_weight_grad, qkv_grads, out_weight_grad, qv_bias_grad, *vectors = call(
         last_kernel,
         (((units, features), F32), ((features, units), F32))
         + (((width, features), F32), ((count, features), F32), (qv_bias.shape, F32))
         + (((features,), F32),) * 7,
         ((block, F32), (block, F32), pltpu.SemaphoreType.DMA((1 + side,))),
-        aliases=((3, 0), (4, 1)),
-        far=(3, 4, 5, 6),
-    )(gathered, down_far, up_far, down_grad, up_weight_grad)
+        aliases=((5, 0), (6, 1)),
+        far=(5, 6, 7, 8),
+    )(gathered, *far, down_grad, up_weight_grad)
     return (
         mixed[None],
         tokens_grad[None],

time: 159 us -> 155 us (0.975)
  waiting for transfers between devices: 64.2 us -> 60.2 us
  local copies, waits for them, and re-layouts: 7.95 us -> 9.67 us
    ppermute x6 -> x8, waiting for transfers between devices: 14.3 us -> 9.33 us  [onward(): lax.ppermute(block, axis, [(i, (i + shift) % side) for i in range(side)])]
    unnamed x82 -> x88, local copies, waits for them, and re-layouts: 7.95 us -> 8.72 us
    ppermute x6 -> x8, starting transfers between devices: 10.7 us -> 10.2 us  [onward(): lax.ppermute(block, axis, [(i, (i + shift) % side) for i in range(side)])]
  transfers between devices with their start and end apart: 27 -> 29, of which waited for: 18 -> 20; matrix products, arithmetic and copies ran while one was open for 0% -> 1% of each run, Pallas kernels for 9% -> 9%
where the time goes in v4:
time: 155 us
  waiting for transfers between devices  60.2 us (39%)
  starting transfers between devices  51.6 us (33%)
  Pallas kernels  31.7 us (20%)
  local copies, waits for them, and re-layouts  9.67 us (6%)
    pallas_call x24, Pallas kernels, run(): pl.pallas_call(body, out_shape=[jax.ShapeDtypeStruct(s, d) for s, d in ou...  31.7 us
    ppermute x4, waiting for transfers between devices, chip_swap(): return lax.ppermute(array_in, 'far', [(0, 1), (1, 0)])  21.5 us
    all_to_all x3, starting transfers between devices, scatter(): return lax.all_to_all(chunks, PLANE, 0, 0, tiled=True)  17.1 us
    ppermute x4, starting transfers between devices, chip_swap(): return lax.ppermute(array_in, 'far', [(0, 1), (1, 0)])  13.2 us
    ppermute x8, starting transfers between devices, onward(): lax.ppermute(block, axis, [(i, (i + shift) % side) for i in range(side)])  10.2 us
    ppermute x4, waiting for transfers between devices, exchange(): return lax.ppermute(block, axis, [(i, partner(i)) for i in range(side)])  9.82 us
    ppermute x8, waiting for transfers between devices, onward(): lax.ppermute(block, axis, [(i, (i + shift) % side) for i in range(side)])  9.33 us
    unnamed x88, local copies, waits for them, and re-layouts  8.72 us
  transfers between devices with their start and end apart: 29, of which 20 were waited for; matrix products, arithmetic and copies ran while one was open for 1% of the time, Pallas kernels for 9%

profile of v4, /device:TPU:0, one launch (start us, length us, event | category | flops | bytes accessed | tf_op | source)
XLA Modules:
  0.0 154.5 jit_solution(17889646353622819895)
XLA Ops:
  0.7 6.9 %attend_kernel.1 = (bf16[512,768]{1,0:T(8,128)(2,1)}, bf16[576,512]{1,0:T(8,128)(2,1)}, bf16[3,512,512]{2,1,0:T(8,128)(2,1)}, bf16[192,512]{1,0:T(8,128)(2,1)}, ...) custom-call(s32[1,8]{1,0:T(1,128)} %lens_ref.1, bf16[512,768]{1,0:T(8,128)(2,1)} %bitcast.10, f32[768]{0:T(1024)} %gain_ref.7, ...), custom_call_target="tpu_custom_call" | custom-call | flops 1000 | bytes 1000 | tf_op jit(solution)/shard_map/attend_kernel/pallas_call | solution.py:30
  7.7 1.9 %collective-permute-done.come_ref = bf16[256,768]{1,0:T(8,128)(2,1)S(1)} collective-permute-done((bf16[256,768]{1,0:T(8,128)(2,1)}, bf16[256,768]{1,0:T(8,128)(2,1)S(1)}, u32[]{:S(2)}, u32[]{:S(2)}) %collective-permute-start) | collective-permute-done | bytes 393248 | tf_op jit(solution)/shard_map/ppermute | solution.py:538
  9.6 1.0 copy-done.22
  10.7 3.4 %collective-permute-start.1 = (bf16[256,768]{1,0:T(8,128)(2,1)S(1)}, bf16[256,768]{1,0:T(8,128)(2,1)S(1)}, u32[]{:S(2)}, u32[]{:S(2)}) collective-permute-start(bf16[256,768]{1,0:T(8,128)(2,1)S(1)} %pair_kernel.4.pair_ref), channel_id=1, source_target_pairs={{0,2},{2,0},{1,3},{3,1},{4,6},{6,4},{5,7},{7,5},{8,10},{10,8},{9,1... | collective-permute-start | bytes 1179656 | tf_op jit(solution)/shard_map/ppermute | solution.py:541
  14.0 9.4 %collective-permute-done.1.come_ref = bf16[256,768]{1,0:T(8,128)(2,1)S(1)} collective-permute-done((bf16[256,768]{1,0:T(8,128)(2,1)S(1)}, bf16[256,768]{1,0:T(8,128)(2,1)S(1)}, u32[]{:S(2)}, u32[]{:S(2)}) %collective-permute-start.1) | collective-permute-done | bytes 393248 | tf_op jit(solution)/shard_map/ppermute | solution.py:541
  25.4 1.7 %collective-permute-done.2.theirs_ref = bf16[256,768]{1,0:T(8,128)(2,1)S(1)} collective-permute-done((bf16[256,768]{1,0:T(8,128)(2,1)S(1)}, bf16[256,768]{1,0:T(8,128)(2,1)S(1)}, u32[]{:S(2)}, u32[]{:S(2)}) %collective-permute-start.2) | collective-permute-done | bytes 393248 | tf_op jit(solution)/shard_map/ppermute | solution.py:538
  27.2 3.7 %expert_kernel.1 = (bf16[512,768]{1,0:T(8,128)(2,1)S(1)}, bf16[512,768]{1,0:T(8,128)(2,1)S(1)}, bf16[256,768]{1,0:T(8,128)(2,1)S(1)}, bf16[256,768]{1,0:T(8,128)(2,1)S(1)}, f32[1,768]{1,0:T(1,128)S(1)}) custom-call(bf16[256,768]{1,0:T(8,128)(2,1)S(1)} %get-tuple-element.80.mine_ref, bf16[256,768]{1,0:T(8,128)(2,1)S(1)} %collective-permute-done.2.theirs_ref, ...), custom_call_target="tpu_custom_call" | custom-call | flops 1000 | bytes 1000 | tf_op jit(solution)/shard_map/expert_kernel/pallas_call | solution.py:30
  31.1 1.6 %collective-permute-done.3.come_ref = bf16[256,768]{1,0:T(8,128)(2,1)S(1)} collective-permute-done((bf16[256,768]{1,0:T(8,128)(2,1)S(1)}, bf16[256,768]{1,0:T(8,128)(2,1)S(1)}, u32[]{:S(2)}, u32[]{:S(2)}) %collective-permute-start.3) | collective-permute-done | bytes 393248 | tf_op jit(solution)/shard_map/ppermute | solution.py:538
  32.7 1.5 expert_weights_kernel.1
  34.2 1.4 copy-done.9
  35.6 7.9 %all-to-all-start = ((bf16[16,96,768]{2,1,0:T(8,128)(2,1)}), bf16[16,96,768]{2,1,0:T(8,128)(2,1)S(1)}, u32[]{:S(2)}, u32[]{:S(2)}) async-start(bf16[16,96,768]{2,1,0:T(8,128)(2,1)} %copy-done.9), calls=%async_computation | async-start | bytes 4718592 | tf_op jit(solution)/shard_map/all_to_all | solution.py:550
  43.5 3.3 %collective-permute-start.4 = (bf16[256,768]{1,0:T(8,128)(2,1)S(1)}, bf16[256,768]{1,0:T(8,128)(2,1)S(1)}, u32[]{:S(2)}, u32[]{:S(2)}) collective-permute-start(bf16[256,768]{1,0:T(8,128)(2,1)S(1)} %pair_kernel.5.pair_ref), channel_id=1, source_target_pairs={{0,2},{2,0},{1,3},{3,1},{4,6},{6,4},{5,7},{7,5},{8,10},{10,8},{9,1... | collective-permute-start | bytes 1179656 | tf_op jit(solution)/shard_map/ppermute | solution.py:541
  46.8 1.3 copy-done.2
  48.1 1.1 copy-done.20
  50.0 6.0 %collective-permute-done.4.come_ref = bf16[256,768]{1,0:T(8,128)(2,1)S(1)} collective-permute-done((bf16[256,768]{1,0:T(8,128)(2,1)S(1)}, bf16[256,768]{1,0:T(8,128)(2,1)S(1)}, u32[]{:S(2)}, u32[]{:S(2)}) %collective-permute-start.4) | collective-permute-done | bytes 393248 | tf_op jit(solution)/shard_map/ppermute | solution.py:541
  57.8 3.3 %collective-permute-start.7 = (bf16[256,768]{1,0:T(8,128)(2,1)S(1)}, bf16[256,768]{1,0:T(8,128)(2,1)S(1)}, u32[]{:S(2)}, u32[]{:S(2)}) collective-permute-start(bf16[256,768]{1,0:T(8,128)(2,1)S(1)} %pair_kernel.6.pair_ref), channel_id=1, source_target_pairs={{0,2},{2,0},{1,3},{3,1},{4,6},{6,4},{5,7},{7,5},{8,10},{10,8},{9,1... | collective-permute-start | bytes 1179656 | tf_op jit(solution)/shard_map/ppermute | solution.py:541
  61.1 3.3 %attend_back_kernel.1 = (bf16[576,512]{1,0:T(8,128)(2,1)S(1)}, bf16[16,48,768]{2,1,0:T(8,128)(2,1)S(1)}, f32[8,576]{1,0:T(8,128)S(1)}) custom-call(bf16[256,768]{1,0:T(8,128)(2,1)S(1)} %get-tuple-element.89.mine_ref, bf16[256,768]{1,0:T(8,128)(2,1)S(1)} %collective-permute-done.6.theirs_ref, bf16[192,768]{1,0:T(8,128)(2,1)S(1)} %copy-done.13, ...), custom_call_target="tpu_custom_call" | custom-call | flops 1000 | bytes 1000 | tf_op jit(solution)/shard_map/attend_back_kernel/pallas_call | solution.py:30
  64.5 6.1 %collective-permute-done.7.come_ref = bf16[256,768]{1,0:T(8,128)(2,1)S(1)} collective-permute-done((bf16[256,768]{1,0:T(8,128)(2,1)S(1)}, bf16[256,768]{1,0:T(8,128)(2,1)S(1)}, u32[]{:S(2)}, u32[]{:S(2)}) %collective-permute-start.7) | collective-permute-done | bytes 393248 | tf_op jit(solution)/shard_map/ppermute | solution.py:541
  71.4 1.7 %collective-permute-done.9.come_ref = bf16[256,768]{1,0:T(8,128)(2,1)S(1)} collective-permute-done((bf16[256,768]{1,0:T(8,128)(2,1)S(1)}, bf16[256,768]{1,0:T(8,128)(2,1)S(1)}, u32[]{:S(2)}, u32[]{:S(2)}) %collective-permute-start.9) | collective-permute-done | bytes 393248 | tf_op jit(solution)/shard_map/ppermute | solution.py:538
  73.2 3.3 %collective-permute-start.11 = (bf16[256,768]{1,0:T(8,128)(2,1)S(1)}, bf16[256,768]{1,0:T(8,128)(2,1)}, u32[]{:S(2)}, u32[]{:S(2)}) collective-permute-start(bf16[256,768]{1,0:T(8,128)(2,1)S(1)} %pair_kernel.7.pair_ref), channel_id=1, source_target_pairs={{0,2},{2,0},{1,3},{3,1},{4,6},{6,4},{5,7},{7,5},{8,10},{10,8},{9,1... | collective-permute-start | bytes 1179656 | tf_op jit(solution)/shard_map/ppermute | solution.py:541
  76.5 3.9 %all-to-all-done.parts_ref = bf16[16,96,768]{2,1,0:T(8,128)(2,1)S(1)} async-done(((bf16[16,96,768]{2,1,0:T(8,128)(2,1)}), bf16[16,96,768]{2,1,0:T(8,128)(2,1)S(1)}, u32[]{:S(2)}, u32[]{:S(2)}) %all-to-all-start) | async-done | bytes 2359328 | tf_op jit(solution)/shard_map/all_to_all | solution.py:550
  80.4 4.4 %all-to-all-start.1 = ((bf16[16,48,768]{2,1,0:T(8,128)(2,1)}), bf16[16,48,768]{2,1,0:T(8,128)(2,1)}, u32[]{:S(2)}, u32[]{:S(2)}) async-start(bf16[16,48,768]{2,1,0:T(8,128)(2,1)} %copy-done.15), calls=%async_computation.1 | async-start | bytes 2359296 | tf_op jit(solution)/shard_map/all_to_all | solution.py:550
  85.1 1.7 %collective-permute-start.10 = (bf16[96,768]{1,0:T(8,128)(2,1)S(1)}, bf16[96,768]{1,0:T(8,128)(2,1)S(1)}, u32[]{:S(2)}, u32[]{:S(2)}) collective-permute-start(bf16[96,768]{1,0:T(8,128)(2,1)S(1)} %total_kernel.1.pair_ref), channel_id=1, source_target_pairs={{0,4},{4,0},{1,5},{5,1},{2,6},{6,2},{3,7},{7,3},{8,12},{12,8},{9,1... | collective-permute-start | bytes 442376 | tf_op jit(solution)/shard_map/ppermute | solution.py:544
  86.8 3.6 %collective-permute-done.10.come_ref = bf16[96,768]{1,0:T(8,128)(2,1)S(1)} collective-permute-done((bf16[96,768]{1,0:T(8,128)(2,1)S(1)}, bf16[96,768]{1,0:T(8,128)(2,1)S(1)}, u32[]{:S(2)}, u32[]{:S(2)}) %collective-permute-start.10) | collective-permute-done | bytes 147488 | tf_op jit(solution)/shard_map/ppermute | solution.py:544
  90.4 1.7 %first_norm_kernel.1.mine_ref = f32[264,768]{1,0:T(8,128)S(1)} custom-call(bf16[512,768]{1,0:T(8,128)(2,1)S(1)} %bitcast.12, bf16[256,768]{1,0:T(8,128)(2,1)S(1)} %pair_kernel.7.pair_ref, bf16[256,768]{1,0:T(8,128)(2,1)} %collective-permute-done.11.come_ref, f32[768]{0:T(1024)S(1)} %copy-done.33, f32[256,768]{1,0:T(8,128)S(1)} %copy-done.18, ...), custom_call_target="tpu_custom_call" | custom-call | flops 1000 | bytes 1000 | tf_op jit(solution)/shard_map/first_norm_kernel/pallas_call | solution.py:30
  92.2 1.8 %collective-permute-start.13 = (bf16[48,768]{1,0:T(8,128)(2,1)S(1)}, bf16[48,768]{1,0:T(8,128)(2,1)S(1)}, u32[]{:S(2)}, u32[]{:S(2)}) collective-permute-start(bf16[48,768]{1,0:T(8,128)(2,1)S(1)} %get-tuple-element.107.refs_0_), channel_id=1, source_target_pairs={{0,32},{32,0},{64,96},{96,64},{1,33},{33,1},{65,97},{97,65},{2,34}... | collective-permute-start | bytes 221192 | tf_op jit(solution)/shard_map/ppermute | solution.py:557
  94.1 1.5 collective-permute-start.14
  95.5 5.5 %collective-permute-done.13.refs_2_ = bf16[48,768]{1,0:T(8,128)(2,1)S(1)} collective-permute-done((bf16[48,768]{1,0:T(8,128)(2,1)S(1)}, bf16[48,768]{1,0:T(8,128)(2,1)S(1)}, u32[]{:S(2)}, u32[]{:S(2)}) %collective-permute-start.13) | collective-permute-done | bytes 73760 | tf_op jit(solution)/shard_map/ppermute | solution.py:557
  101.1 1.3 token_order_kernel.1
  102.4 1.2 all-to-all-done.1.parts_ref
  103.6 1.4 attend_total_kernel.1.pair_ref
  105.0 1.1 collective-permute-start.16
  106.2 2.1 %collective-permute-start.17 = (bf16[96,768]{1,0:T(8,128)(2,1)S(1)}, bf16[96,768]{1,0:T(8,128)(2,1)S(1)}, u32[]{:S(2)}, u32[]{:S(2)}) collective-permute-start(bf16[96,768]{1,0:T(8,128)(2,1)S(1)} %get-tuple-element.118.refs_1_), channel_id=1, source_target_pairs={{0,24},{8,16},{16,8},{24,0},{1,25},{9,17},{17,9},{25,1},{2,26},{10... | collective-permute-start | bytes 442376 | tf_op jit(solution)/shard_map/ppermute | solution.py:557
  108.2 3.2 %collective-permute-done.16.refs_2_ = bf16[96,768]{1,0:T(8,128)(2,1)S(1)} collective-permute-done((bf16[96,768]{1,0:T(8,128)(2,1)S(1)}, bf16[96,768]{1,0:T(8,128)(2,1)S(1)}, u32[]{:S(2)}, u32[]{:S(2)}) %collective-permute-start.16) | collective-permute-done | bytes 147488 | tf_op jit(solution)/shard_map/ppermute | solution.py:557
  111.5 1.1 collective-permute-done.17.refs_3_
  112.6 2.1 %collective-permute-start.19 = (bf16[192,768]{1,0:T(8,128)(2,1)S(1)}, bf16[192,768]{1,0:T(8,128)(2,1)S(1)}, u32[]{:S(2)}, u32[]{:S(2)}) collective-permute-start(bf16[192,768]{1,0:T(8,128)(2,1)S(1)} %get-tuple-element.119.refs_0_), channel_id=1, source_target_pairs={{0,24},{8,0},{16,8},{24,16},{1,25},{9,1},{17,9},{25,17},{2,26},{10... | collective-permute-start | bytes 884744 | tf_op jit(solution)/shard_map/ppermute | solution.py:567
  114.7 2.2 %collective-permute-start.21 = (bf16[192,768]{1,0:T(8,128)(2,1)S(1)}, bf16[192,768]{1,0:T(8,128)(2,1)S(1)}, u32[]{:S(2)}, u32[]{:S(2)}) collective-permute-start(bf16[192,768]{1,0:T(8,128)(2,1)S(1)} %get-tuple-element.120.refs_3_), channel_id=1, source_target_pairs={{0,96},{32,0},{64,32},{96,64},{1,97},{33,1},{65,33},{97,65},{2,98}... | collective-permute-start | bytes 884744 | tf_op jit(solution)/shard_map/ppermute | solution.py:567
  116.9 1.6 %collective-permute-start.15 = (bf16[56,768]{1,0:T(8,128)(2,1)S(1)}, bf16[56,768]{1,0:T(8,128)(2,1)S(1)}, u32[]{:S(2)}, u32[]{:S(2)}) collective-permute-start(bf16[56,768]{1,0:T(8,128)(2,1)S(1)} %attend_total_kernel.1.pair_ref), channel_id=1, source_target_pairs={{0,4},{4,0},{1,5},{5,1},{2,6},{6,2},{3,7},{7,3},{8,12},{12,8},{9,1... | collective-permute-start | bytes 258056 | tf_op jit(solution)/shard_map/ppermute | solution.py:544
  118.5 2.9 %collective-permute-done.15.come_ref = bf16[56,768]{1,0:T(8,128)(2,1)S(1)} collective-permute-done((bf16[56,768]{1,0:T(8,128)(2,1)S(1)}, bf16[56,768]{1,0:T(8,128)(2,1)S(1)}, u32[]{:S(2)}, u32[]{:S(2)}) %collective-permute-start.15) | collective-permute-done | bytes 86048 | tf_op jit(solution)/shard_map/ppermute | solution.py:544
  121.4 1.7 %collective-permute-done.18.refs_1_ = bf16[192,768]{1,0:T(8,128)(2,1)S(1)} collective-permute-done((bf16[192,768]{1,0:T(8,128)(2,1)S(1)}, bf16[192,768]{1,0:T(8,128)(2,1)S(1)}, u32[]{:S(2)}, u32[]{:S(2)}) %collective-permute-start.18) | collective-permute-done | bytes 294944 | tf_op jit(solution)/shard_map/ppermute | solution.py:567
  124.6 1.0 collective-permute-done.20.refs_4_
  125.6 1.2 attend_finish_kernel.1
  126.8 4.8 %all-to-all-start.2 = ((bf16[16,56,768]{2,1,0:T(8,128)(2,1)}), bf16[16,56,768]{2,1,0:T(8,128)(2,1)S(1)}, u32[]{:S(2)}, u32[]{:S(2)}) async-start(bf16[16,56,768]{2,1,0:T(8,128)(2,1)} %attend_finish_kernel.1), calls=%async_computation.2 | async-start | bytes 2752512 | tf_op jit(solution)/shard_map/all_to_all | solution.py:550
  133.7 3.2 %collective-permute-start.25 = (bf16[96,768]{1,0:T(8,128)(2,1)S(1)}, bf16[96,768]{1,0:T(8,128)(2,1)S(1)}, u32[]{:S(2)}, u32[]{:S(2)}) collective-permute-start(bf16[96,768]{1,0:T(8,128)(2,1)S(1)} %slice.15), channel_id=1, source_target_pairs={{0,96},{32,0},{64,32},{96,64},{1,97},{33,1},{65,33},{97,65},{2,98}... | collective-permute-start | bytes 442376 | tf_op jit(solution)/shard_map/ppermute | solution.py:567
  136.9 2.7 %collective-permute-start.23 = (bf16[96,768]{1,0:T(8,128)(2,1)S(1)}, bf16[96,768]{1,0:T(8,128)(2,1)S(1)}, u32[]{:S(2)}, u32[]{:S(2)}) collective-permute-start(bf16[96,768]{1,0:T(8,128)(2,1)S(1)} %slice.13), channel_id=1, source_target_pairs={{0,24},{8,0},{16,8},{24,16},{1,25},{9,1},{17,9},{25,17},{2,26},{10... | collective-permute-start | bytes 442376 | tf_op jit(solution)/shard_map/ppermute | solution.py:567
  140.5 3.8 %expert_most_kernel.1 = (f32[768,768]{1,0:T(8,128)}, f32[768,768]{1,0:T(8,128)}) custom-call(bf16[192,768]{1,0:T(8,128)(2,1)} %copy-done.25, bf16[192,768]{1,0:T(8,128)(2,1)} %copy-done.40, bf16[192,768]{1,0:T(8,128)(2,1)} %copy-done.38, bf16[192,768]{1,0:T(8,128)(2,1)} %copy-done.26, bf16[192,768]{1,0:T(8,128)(2,1)} %collective-permute-done.20.refs_4_, ...), custom_call_target="tpu_custom_call" | custom-call | flops 1000 | bytes 1000 | tf_op jit(solution)/shard_map/expert_most_kernel/pallas_call | solution.py:30
  144.3 5.9 %collective-permute-done.25.b_high = bf16[96,768]{1,0:T(8,128)(2,1)S(1)} collective-permute-done((bf16[96,768]{1,0:T(8,128)(2,1)S(1)}, bf16[96,768]{1,0:T(8,128)(2,1)S(1)}, u32[]{:S(2)}, u32[]{:S(2)}) %collective-permute-start.25) | collective-permute-done | bytes 147488 | tf_op jit(solution)/shard_map/ppermute | solution.py:567
  151.8 2.5 %last_kernel.1 = (f32[768,768]{1,0:T(8,128)}, f32[768,768]{1,0:T(8,128)}, f32[576,768]{1,0:T(8,128)}, f32[192,768]{1,0:T(8,128)}, f32[3,128]{1,0:T(4,128)}, /*in...) custom-call(bf16[16,56,768]{2,1,0:T(8,128)(2,1)S(1)} %all-to-all-don, ...), custom_call_target="tpu_custom_call", output_to_operand_aliasing={{0}: (5, {}), {1}: (6, {})} | custom-call | flops 1000 | bytes 1000 | tf_op jit(solution)/shard_map/last_kernel/pallas_call | solution.py:30
  (126 shorter events, 12.4 us)
Async XLA Ops:
  0.6 26.5 %copy-start.36 = (f32[768]{0:T(1024)S(1)}, f32[768]{0:T(1024)}, u32[]{:S(2)}) copy-start(f32[768]{0:T(1024)} %bias_ref.6) | copy-start | bytes 9220
  0.7 22.8 %copy-start = (bf16[1,512,768]{2,1,0:T(8,128)(2,1)S(1)}, bf16[1,512,768]{2,1,0:T(8,128)(2,1)}, u32[]{:S(2)}) copy-start(bf16[1,512,768]{2,1,0:T(8,128)(2,1)} %param.15) | copy-start | bytes 2359300
  0.7 22.8 %copy-start.32 = (f32[768]{0:T(1024)S(1)}, f32[768]{0:T(1024)}, u32[]{:S(2)}) copy-start(f32[768]{0:T(1024)} %gain_ref.6) | copy-start | bytes 9220
  0.7 22.8 %copy-start.34 = (f32[768]{0:T(1024)S(1)}, f32[768]{0:T(1024)}, u32[]{:S(2)}) copy-start(f32[768]{0:T(1024)} %bias_ref.5) | copy-start | bytes 9220
  0.7 26.5 %copy-start.14 = (bf16[768,768]{1,0:T(8,128)(2,1)S(1)}, bf16[768,768]{1,0:T(8,128)(2,1)}, u32[]{:S(2)}) copy-start(bf16[768,768]{1,0:T(8,128)(2,1)} %up_ref.1) | copy-start | bytes 3538948
  7.6 19.6 %copy-start.1 = (bf16[768,768]{1,0:T(8,128)(2,1)S(1)}, bf16[768,768]{1,0:T(8,128)(2,1)}, u32[]{:S(2)}) copy-start(bf16[768,768]{1,0:T(8,128)(2,1)} %down_ref.3) | copy-start | bytes 3538948
  7.6 19.6 %copy-start.4 = (bf16[1,512,768]{2,1,0:T(8,128)(2,1)S(1)}, bf16[1,512,768]{2,1,0:T(8,128)(2,1)}, u32[]{:S(2)}) copy-start(bf16[1,512,768]{2,1,0:T(8,128)(2,1)} %param.29) | copy-start | bytes 2359300
  7.6 2.0 %collective-permute-start = (bf16[256,768]{1,0:T(8,128)(2,1)}, bf16[256,768]{1,0:T(8,128)(2,1)S(1)}, u32[]{:S(2)}, u32[]{:S(2)}) collective-permute-start(bf16[256,768]{1,0:T(8,128)(2,1)} %get-tuple-element.78), channel_id=1, source_target_pairs={{0,1},{1,0},{2,3},{3,2},{4,5},{5,4},{6,7},{7,6},{8,9},{9,8},{10,11... | collective-permute-start | bytes 1179656 | tf_op jit(solution)/shard_map/ppermute | solution.py:538
  10.7 12.8 %collective-permute-start.1 = (bf16[256,768]{1,0:T(8,128)(2,1)S(1)}, bf16[256,768]{1,0:T(8,128)(2,1)S(1)}, u32[]{:S(2)}, u32[]{:S(2)}) collective-permute-start(bf16[256,768]{1,0:T(8,128)(2,1)S(1)} %pair_kernel.4.pair_ref), channel_id=1, source_target_pairs={{0,2},{2,0},{1,3},{3,1},{4,6},{6,4},{5,7},{7,5},{8,10},{10,8},{9,1... | collective-permute-start | bytes 1179656 | tf_op jit(solution)/shard_map/ppermute | solution.py:541
  25.4 1.7 %collective-permute-start.2 = (bf16[256,768]{1,0:T(8,128)(2,1)S(1)}, bf16[256,768]{1,0:T(8,128)(2,1)S(1)}, u32[]{:S(2)}, u32[]{:S(2)}) collective-permute-start(bf16[256,768]{1,0:T(8,128)(2,1)S(1)} %get-tuple-element.80.mine_ref), channel_id=1, source_target_pairs={{0,1},{1,0},{2,3},{3,2},{4,5},{5,4},{6,7},{7,6},{8,9},{9,8},{10,11... | collective-permute-start | bytes 1179656 | tf_op jit(solution)/shard_map/ppermute | solution.py:538
  30.9 1.8 %collective-permute-start.3 = (bf16[256,768]{1,0:T(8,128)(2,1)S(1)}, bf16[256,768]{1,0:T(8,128)(2,1)S(1)}, u32[]{:S(2)}, u32[]{:S(2)}) collective-permute-start(bf16[256,768]{1,0:T(8,128)(2,1)S(1)} %get-tuple-element.82), channel_id=1, source_target_pairs={{0,1},{1,0},{2,3},{3,2},{4,5},{5,4},{6,7},{7,6},{8,9},{9,8},{10,11... | collective-permute-start | bytes 1179656 | tf_op jit(solution)/shard_map/ppermute | solution.py:538
  35.6 44.8 %all-to-all-start = ((bf16[16,96,768]{2,1,0:T(8,128)(2,1)}), bf16[16,96,768]{2,1,0:T(8,128)(2,1)S(1)}, u32[]{:S(2)}, u32[]{:S(2)}) async-start(bf16[16,96,768]{2,1,0:T(8,128)(2,1)} %copy-done.9), calls=%async_computation | async-start | bytes 4718592 | tf_op jit(solution)/shard_map/all_to_all | solution.py:550
  43.5 12.5 %collective-permute-start.4 = (bf16[256,768]{1,0:T(8,128)(2,1)S(1)}, bf16[256,768]{1,0:T(8,128)(2,1)S(1)}, u32[]{:S(2)}, u32[]{:S(2)}) collective-permute-start(bf16[256,768]{1,0:T(8,128)(2,1)S(1)} %pair_kernel.5.pair_ref), channel_id=1, source_target_pairs={{0,2},{2,0},{1,3},{3,1},{4,6},{6,4},{5,7},{7,5},{8,10},{10,8},{9,1... | collective-permute-start | bytes 1179656 | tf_op jit(solution)/shard_map/ppermute | solution.py:541
  49.2 6.8 %copy-start.5 = (bf16[1,512,768]{2,1,0:T(8,128)(2,1)S(1)}, bf16[1,512,768]{2,1,0:T(8,128)(2,1)}, u32[]{:S(2)}) copy-start(bf16[1,512,768]{2,1,0:T(8,128)(2,1)} %param.29) | copy-start | bytes 2359300
  49.2 6.8 %copy-start.7 = (f32[256,768]{1,0:T(8,128)S(1)}, f32[256,768]{1,0:T(8,128)}, u32[]{:S(2)}) copy-start(f32[256,768]{1,0:T(8,128)} %copy-done.6) | copy-start | bytes 2359300
  56.0 1.7 %collective-permute-start.5 = (bf16[256,768]{1,0:T(8,128)(2,1)S(1)}, bf16[256,768]{1,0:T(8,128)(2,1)S(1)}, u32[]{:S(2)}, u32[]{:S(2)}) collective-permute-start(bf16[256,768]{1,0:T(8,128)(2,1)S(1)} %get-tuple-element.88), channel_id=1, source_target_pairs={{0,1},{1,0},{2,3},{3,2},{4,5},{5,4},{6,7},{7,6},{8,9},{9,8},{10,11... | collective-permute-start | bytes 1179656 | tf_op jit(solution)/shard_map/ppermute | solution.py:538
  56.9 7.5 %copy-start.28 = (f32[8,768]{1,0:T(8,128)}, f32[8,768]{1,0:T(8,128)S(1)}, u32[]{:S(2)}) copy-start(f32[8,768]{1,0:T(8,128)S(1)} %get-tuple-element.102.rows_ref) | copy-start | bytes 73732
  56.9 4.1 %collective-permute-start.6 = (bf16[256,768]{1,0:T(8,128)(2,1)S(1)}, bf16[256,768]{1,0:T(8,128)(2,1)S(1)}, u32[]{:S(2)}, u32[]{:S(2)}) collective-permute-start(bf16[256,768]{1,0:T(8,128)(2,1)S(1)} %get-tuple-element.89.mine_ref), channel_id=1, source_target_pairs={{0,1},{1,0},{2,3},{3,2},{4,5},{5,4},{6,7},{7,6},{8,9},{9,8},{10,11... | collective-permute-start | bytes 1179656 | tf_op jit(solution)/shard_map/ppermute | solution.py:538
  57.8 6.7 %copy-start.11 = (bf16[256,768]{1,0:T(8,128)(2,1)}, bf16[256,768]{1,0:T(8,128)(2,1)S(1)}, u32[]{:S(2)}) copy-start(bf16[256,768]{1,0:T(8,128)(2,1)S(1)} %pair_kernel.6.pair_ref) | copy-start | bytes 1179652
  57.8 12.7 %collective-permute-start.7 = (bf16[256,768]{1,0:T(8,128)(2,1)S(1)}, bf16[256,768]{1,0:T(8,128)(2,1)S(1)}, u32[]{:S(2)}, u32[]{:S(2)}) collective-permute-start(bf16[256,768]{1,0:T(8,128)(2,1)S(1)} %pair_kernel.6.pair_ref), channel_id=1, source_target_pairs={{0,2},{2,0},{1,3},{3,1},{4,6},{6,4},{5,7},{7,5},{8,10},{10,8},{9,1... | collective-permute-start | bytes 1179656 | tf_op jit(solution)/shard_map/ppermute | solution.py:541
  61.1 9.4 %copy-start.3 = (bf16[768,3,192]{0,2,1:T(8,128)(2,1)S(1)}, bf16[768,3,192]{0,2,1:T(8,128)(2,1)}, u32[]{:S(2)}) copy-start(bf16[768,3,192]{0,2,1:T(8,128)(2,1)} %param.19) | copy-start | bytes 2654212
  64.4 8.8 %copy-start.15 = (bf16[16,48,768]{2,1,0:T(8,128)(2,1)}, bf16[16,48,768]{2,1,0:T(8,128)(2,1)S(1)}, u32[]{:S(2)}) copy-start(bf16[16,48,768]{2,1,0:T(8,128)(2,1)S(1)} %get-tuple-element.114) | copy-start | bytes 3538948
  64.4 8.8 %copy-start.30 = (f32[8,576]{1,0:T(8,128)}, f32[8,576]{1,0:T(8,128)S(1)}, u32[]{:S(2)}) copy-start(f32[8,576]{1,0:T(8,128)S(1)} %get-tuple-element.104.qkv_ref) | copy-start | bytes 55300
  71.3 1.8 %collective-permute-start.9 = (bf16[256,768]{1,0:T(8,128)(2,1)S(1)}, bf16[256,768]{1,0:T(8,128)(2,1)S(1)}, u32[]{:S(2)}, u32[]{:S(2)}) collective-permute-start(bf16[256,768]{1,0:T(8,128)(2,1)S(1)} %get-tuple-element.98), channel_id=1, source_target_pairs={{0,1},{1,0},{2,3},{3,2},{4,5},{5,4},{6,7},{7,6},{8,9},{9,8},{10,11... | collective-permute-start | bytes 1179656 | tf_op jit(solution)/shard_map/ppermute | solution.py:538
  73.2 13.6 %collective-permute-start.11 = (bf16[256,768]{1,0:T(8,128)(2,1)S(1)}, bf16[256,768]{1,0:T(8,128)(2,1)}, u32[]{:S(2)}, u32[]{:S(2)}) collective-permute-start(bf16[256,768]{1,0:T(8,128)(2,1)S(1)} %pair_kernel.7.pair_ref), channel_id=1, source_target_pairs={{0,2},{2,0},{1,3},{3,1},{4,6},{6,4},{5,7},{7,5},{8,10},{10,8},{9,1... | collective-permute-start | bytes 1179656 | tf_op jit(solution)/shard_map/ppermute | solution.py:541
  80.4 23.2 %all-to-all-start.1 = ((bf16[16,48,768]{2,1,0:T(8,128)(2,1)}), bf16[16,48,768]{2,1,0:T(8,128)(2,1)}, u32[]{:S(2)}, u32[]{:S(2)}) async-start(bf16[16,48,768]{2,1,0:T(8,128)(2,1)} %copy-done.15), calls=%async_computation.1 | async-start | bytes 2359296 | tf_op jit(solution)/shard_map/all_to_all | solution.py:550
  84.8 5.6 %copy-start.18 = (f32[256,768]{1,0:T(8,128)S(1)}, f32[256,768]{1,0:T(8,128)}, u32[]{:S(2)}) copy-start(f32[256,768]{1,0:T(8,128)} %copy-done.17) | copy-start | bytes 2359300
  84.8 5.6 %copy-start.29 = (f32[8,768]{1,0:T(8,128)S(1)}, f32[8,768]{1,0:T(8,128)}, u32[]{:S(2)}) copy-start(f32[8,768]{1,0:T(8,128)} %copy-done.28) | copy-start | bytes 73732
  85.1 5.2 %collective-permute-start.10 = (bf16[96,768]{1,0:T(8,128)(2,1)S(1)}, bf16[96,768]{1,0:T(8,128)(2,1)S(1)}, u32[]{:S(2)}, u32[]{:S(2)}) collective-permute-start(bf16[96,768]{1,0:T(8,128)(2,1)S(1)} %total_kernel.1.pair_ref), channel_id=1, source_target_pairs={{0,4},{4,0},{1,5},{5,1},{2,6},{6,2},{3,7},{7,3},{8,12},{12,8},{9,1... | collective-permute-start | bytes 442376 | tf_op jit(solution)/shard_map/ppermute | solution.py:544
  90.4 10.8 %copy-start.31 = (f32[8,576]{1,0:T(8,128)S(1)}, f32[8,576]{1,0:T(8,128)}, u32[]{:S(2)}) copy-start(f32[8,576]{1,0:T(8,128)} %copy-done.30) | copy-start | bytes 55300
  92.1 9.0 %collective-permute-start.12 = (f32[264,768]{1,0:T(8,128)S(1)}, f32[264,768]{1,0:T(8,128)S(1)}, u32[]{:S(2)}, u32[]{:S(2)}) collective-permute-start(f32[264,768]{1,0:T(8,128)S(1)} %first_norm_kernel.1.mine_ref), channel_id=1, source_target_pairs={{0,1},{1,0},{2,3},{3,2},{4,5},{5,4},{6,7},{7,6},{8,9},{9,8},{10,11... | collective-permute-start | bytes 2433032 | tf_op jit(solution)/shard_map/ppermute | solution.py:538
  92.2 8.9 %collective-permute-start.13 = (bf16[48,768]{1,0:T(8,128)(2,1)S(1)}, bf16[48,768]{1,0:T(8,128)(2,1)S(1)}, u32[]{:S(2)}, u32[]{:S(2)}) collective-permute-start(bf16[48,768]{1,0:T(8,128)(2,1)S(1)} %get-tuple-element.107.refs_0_), channel_id=1, source_target_pairs={{0,32},{32,0},{64,96},{96,64},{1,33},{33,1},{65,97},{97,65},{2,34}... | collective-permute-start | bytes 221192 | tf_op jit(solution)/shard_map/ppermute | solution.py:557
  94.1 7.0 %collective-permute-start.14 = (bf16[48,768]{1,0:T(8,128)(2,1)S(1)}, bf16[48,768]{1,0:T(8,128)(2,1)S(1)}, u32[]{:S(2)}, u32[]{:S(2)}) collective-permute-start(bf16[48,768]{1,0:T(8,128)(2,1)S(1)} %get-tuple-element.108.refs_1_), channel_id=1, source_target_pairs={{0,8},{8,0},{16,24},{24,16},{1,9},{9,1},{17,25},{25,17},{2,10},{10... | collective-permute-start | bytes 221192 | tf_op jit(solution)/shard_map/ppermute | solution.py:557
  105.0 6.4 %collective-permute-start.16 = (bf16[96,768]{1,0:T(8,128)(2,1)S(1)}, bf16[96,768]{1,0:T(8,128)(2,1)S(1)}, u32[]{:S(2)}, u32[]{:S(2)}) collective-permute-start(bf16[96,768]{1,0:T(8,128)(2,1)S(1)} %get-tuple-element.117.refs_0_), channel_id=1, source_target_pairs={{0,96},{32,64},{64,32},{96,0},{1,97},{33,65},{65,33},{97,1},{2,98}... | collective-permute-start | bytes 442376 | tf_op jit(solution)/shard_map/ppermute | solution.py:557
  106.2 6.4 %collective-permute-start.17 = (bf16[96,768]{1,0:T(8,128)(2,1)S(1)}, bf16[96,768]{1,0:T(8,128)(2,1)S(1)}, u32[]{:S(2)}, u32[]{:S(2)}) collective-permute-start(bf16[96,768]{1,0:T(8,128)(2,1)S(1)} %get-tuple-element.118.refs_1_), channel_id=1, source_target_pairs={{0,24},{8,16},{16,8},{24,0},{1,25},{9,17},{17,9},{25,1},{2,26},{10... | collective-permute-start | bytes 442376 | tf_op jit(solution)/shard_map/ppermute | solution.py:557
  112.6 14.2 %copy-start.25 = (bf16[192,768]{1,0:T(8,128)(2,1)}, bf16[192,768]{1,0:T(8,128)(2,1)S(1)}, u32[]{:S(2)}) copy-start(bf16[192,768]{1,0:T(8,128)(2,1)S(1)} %get-tuple-element.119.refs_0_) | copy-start | bytes 884740
  112.6 14.2 %copy-start.26 = (bf16[192,768]{1,0:T(8,128)(2,1)}, bf16[192,768]{1,0:T(8,128)(2,1)S(1)}, u32[]{:S(2)}) copy-start(bf16[192,768]{1,0:T(8,128)(2,1)S(1)} %get-tuple-element.120.refs_3_) | copy-start | bytes 884740
  112.6 8.8 %collective-permute-start.19 = (bf16[192,768]{1,0:T(8,128)(2,1)S(1)}, bf16[192,768]{1,0:T(8,128)(2,1)S(1)}, u32[]{:S(2)}, u32[]{:S(2)}) collective-permute-start(bf16[192,768]{1,0:T(8,128)(2,1)S(1)} %get-tuple-element.119.refs_0_), channel_id=1, source_target_pairs={{0,24},{8,0},{16,8},{24,16},{1,25},{9,1},{17,9},{25,17},{2,26},{10... | collective-permute-start | bytes 884744 | tf_op jit(solution)/shard_map/ppermute | solution.py:567
  114.7 8.4 %collective-permute-start.18 = (bf16[192,768]{1,0:T(8,128)(2,1)S(1)}, bf16[192,768]{1,0:T(8,128)(2,1)S(1)}, u32[]{:S(2)}, u32[]{:S(2)}) collective-permute-start(bf16[192,768]{1,0:T(8,128)(2,1)S(1)} %get-tuple-element.119.refs_0_), channel_id=1, source_target_pairs={{0,8},{8,16},{16,24},{24,0},{1,9},{9,17},{17,25},{25,1},{2,10},{10... | collective-permute-start | bytes 884744 | tf_op jit(solution)/shard_map/ppermute | solution.py:567
  114.7 8.4 %collective-permute-start.21 = (bf16[192,768]{1,0:T(8,128)(2,1)S(1)}, bf16[192,768]{1,0:T(8,128)(2,1)S(1)}, u32[]{:S(2)}, u32[]{:S(2)}) collective-permute-start(bf16[192,768]{1,0:T(8,128)(2,1)S(1)} %get-tuple-element.120.refs_3_), channel_id=1, source_target_pairs={{0,96},{32,0},{64,32},{96,64},{1,97},{33,1},{65,33},{97,65},{2,98}... | collective-permute-start | bytes 884744 | tf_op jit(solution)/shard_map/ppermute | solution.py:567
  116.9 8.7 %collective-permute-start.20 = (bf16[192,768]{1,0:T(8,128)(2,1)S(1)}, bf16[192,768]{1,0:T(8,128)(2,1)}, u32[]{:S(2)}, u32[]{:S(2)}) collective-permute-start(bf16[192,768]{1,0:T(8,128)(2,1)S(1)} %get-tuple-element.120.refs_3_), channel_id=1, source_target_pairs={{0,32},{32,64},{64,96},{96,0},{1,33},{33,65},{65,97},{97,1},{2,34}... | collective-permute-start | bytes 884744 | tf_op jit(solution)/shard_map/ppermute | solution.py:567
  116.9 4.5 %collective-permute-start.15 = (bf16[56,768]{1,0:T(8,128)(2,1)S(1)}, bf16[56,768]{1,0:T(8,128)(2,1)S(1)}, u32[]{:S(2)}, u32[]{:S(2)}) collective-permute-start(bf16[56,768]{1,0:T(8,128)(2,1)S(1)} %attend_total_kernel.1.pair_ref), channel_id=1, source_target_pairs={{0,4},{4,0},{1,5},{5,1},{2,6},{6,2},{3,7},{7,3},{8,12},{12,8},{9,1... | collective-permute-start | bytes 258056 | tf_op jit(solution)/shard_map/ppermute | solution.py:544
  126.8 25.0 %all-to-all-start.2 = ((bf16[16,56,768]{2,1,0:T(8,128)(2,1)}), bf16[16,56,768]{2,1,0:T(8,128)(2,1)S(1)}, u32[]{:S(2)}, u32[]{:S(2)}) async-start(bf16[16,56,768]{2,1,0:T(8,128)(2,1)} %attend_finish_kernel.1), calls=%async_computation.2 | async-start | bytes 2752512 | tf_op jit(solution)/shard_map/all_to_all | solution.py:550
  131.9 7.7 %collective-permute-start.8 = (bf16[256,768]{1,0:T(8,128)(2,1)S(1)}, bf16[256,768]{1,0:T(8,128)(2,1)S(1)}, u32[]{:S(2)}, u32[]{:S(2)}) collective-permute-start(bf16[256,768]{1,0:T(8,128)(2,1)S(1)} %mixed_kernel.1.mine_ref), channel_id=1, source_target_pairs={{0,1},{1,0},{2,3},{3,2},{4,5},{5,4},{6,7},{7,6},{8,9},{9,8},{10,11... | collective-permute-start | bytes 1179656 | tf_op jit(solution)/shard_map/ppermute | solution.py:538
  133.7 16.5 %collective-permute-start.25 = (bf16[96,768]{1,0:T(8,128)(2,1)S(1)}, bf16[96,768]{1,0:T(8,128)(2,1)S(1)}, u32[]{:S(2)}, u32[]{:S(2)}) collective-permute-start(bf16[96,768]{1,0:T(8,128)(2,1)S(1)} %slice.15), channel_id=1, source_target_pairs={{0,96},{32,0},{64,32},{96,64},{1,97},{33,1},{65,33},{97,65},{2,98}... | collective-permute-start | bytes 442376 | tf_op jit(solution)/shard_map/ppermute | solution.py:567
  136.9 13.5 %collective-permute-start.24 = (bf16[96,768]{1,0:T(8,128)(2,1)S(1)}, bf16[96,768]{1,0:T(8,128)(2,1)S(1)}, u32[]{:S(2)}, u32[]{:S(2)}) collective-permute-start(bf16[96,768]{1,0:T(8,128)(2,1)S(1)} %slice.14), channel_id=1, source_target_pairs={{0,32},{32,64},{64,96},{96,0},{1,33},{33,65},{65,97},{97,1},{2,34}... | collective-permute-start | bytes 442376 | tf_op jit(solution)/shard_map/ppermute | solution.py:567
  136.9 13.5 %collective-permute-start.23 = (bf16[96,768]{1,0:T(8,128)(2,1)S(1)}, bf16[96,768]{1,0:T(8,128)(2,1)S(1)}, u32[]{:S(2)}, u32[]{:S(2)}) collective-permute-start(bf16[96,768]{1,0:T(8,128)(2,1)S(1)} %slice.13), channel_id=1, source_target_pairs={{0,24},{8,0},{16,8},{24,16},{1,25},{9,1},{17,9},{25,17},{2,26},{10... | collective-permute-start | bytes 442376 | tf_op jit(solution)/shard_map/ppermute | solution.py:567
  139.6 11.3 %collective-permute-start.22 = (bf16[96,768]{1,0:T(8,128)(2,1)S(1)}, bf16[96,768]{1,0:T(8,128)(2,1)S(1)}, u32[]{:S(2)}, u32[]{:S(2)}) collective-permute-start(bf16[96,768]{1,0:T(8,128)(2,1)S(1)} %slice.12), channel_id=1, source_target_pairs={{0,8},{8,16},{16,24},{24,0},{1,9},{9,17},{17,25},{25,1},{2,10},{10... | collective-permute-start | bytes 442376 | tf_op jit(solution)/shard_map/ppermute | solution.py:567
  (25 other events, 72.6 us)

commit v5 on v4

--- a/solution.py
+++ b/solution.py
@@ -109,10 +109,10 @@
         copies[-1].start()
         return copies[-1]
 
-    piece = half // 2
+    piece = half
     pieces = []
     for which in range(2):
-        for part in range(2):
+        for part in range(1):
             start = half_at(which, half) + part * piece
             at = which * half + part * piece
             pieces.append(fetch(tok_ref.at[pl.ds(start, piece)], tok_at.at[pl.ds(at, piece)]))

time: 155 us -> 155 us (level)
  no operation moved by 1% of the time
where the time goes in v5:
time: 155 us; the launch traced here: 154 us
  waiting for transfers between devices  60.2 us (39%)
  starting transfers between devices  51.6 us (33%)
  Pallas kernels  31.3 us (20%)
  local copies, waits for them, and re-layouts  9.67 us (6%)
    pallas_call x24, Pallas kernels, run(): pl.pallas_call(body, out_shape=[jax.ShapeDtypeStruct(s, d) for s, d in ou...  31.3 us
    ppermute x4, waiting for transfers between devices, chip_swap(): return lax.ppermute(array_in, 'far', [(0, 1), (1, 0)])  21.5 us
    all_to_all x3, starting transfers between devices, scatter(): return lax.all_to_all(chunks, PLANE, 0, 0, tiled=True)  17.1 us
    ppermute x4, starting transfers between devices, chip_swap(): return lax.ppermute(array_in, 'far', [(0, 1), (1, 0)])  13.2 us
    ppermute x8, starting transfers between devices, onward(): lax.ppermute(block, axis, [(i, (i + shift) % side) for i in range(side)])  10.2 us
    ppermute x4, waiting for transfers between devices, exchange(): return lax.ppermute(block, axis, [(i, partner(i)) for i in range(side)])  9.82 us
    ppermute x8, waiting for transfers between devices, onward(): lax.ppermute(block, axis, [(i, (i + shift) % side) for i in range(side)])  9.33 us
    unnamed x88, local copies, waits for them, and re-layouts  8.72 us
  transfers between devices with their start and end apart: 29, of which 20 were waited for; matrix products, arithmetic and copies ran while one was open for 1% of the time, Pallas kernels for 9%

profile of v5, /device:TPU:0, one launch (start us, length us, event | category | flops | bytes accessed | tf_op | source)
XLA Modules:
  0.0 154.1 jit_solution(3659268326622297155)
XLA Ops:
  0.7 6.5 %attend_kernel.1 = (bf16[512,768]{1,0:T(8,128)(2,1)}, bf16[576,512]{1,0:T(8,128)(2,1)}, bf16[3,512,512]{2,1,0:T(8,128)(2,1)}, bf16[192,512]{1,0:T(8,128)(2,1)}, ...) custom-call(s32[1,8]{1,0:T(1,128)} %lens_ref.1, bf16[512,768]{1,0:T(8,128)(2,1)} %bitcast.10, f32[768]{0:T(1024)} %gain_ref.7, ...), custom_call_target="tpu_custom_call" | custom-call | flops 1000 | bytes 1000 | tf_op jit(solution)/shard_map/attend_kernel/pallas_call | solution.py:30
  7.3 1.9 %collective-permute-done.come_ref = bf16[256,768]{1,0:T(8,128)(2,1)S(1)} collective-permute-done((bf16[256,768]{1,0:T(8,128)(2,1)}, bf16[256,768]{1,0:T(8,128)(2,1)S(1)}, u32[]{:S(2)}, u32[]{:S(2)}) %collective-permute-start) | collective-permute-done | bytes 393248 | tf_op jit(solution)/shard_map/ppermute | solution.py:538
  9.2 1.0 copy-done.22
  10.3 3.4 %collective-permute-start.1 = (bf16[256,768]{1,0:T(8,128)(2,1)S(1)}, bf16[256,768]{1,0:T(8,128)(2,1)S(1)}, u32[]{:S(2)}, u32[]{:S(2)}) collective-permute-start(bf16[256,768]{1,0:T(8,128)(2,1)S(1)} %pair_kernel.4.pair_ref), channel_id=1, source_target_pairs={{0,2},{2,0},{1,3},{3,1},{4,6},{6,4},{5,7},{7,5},{8,10},{10,8},{9,1... | collective-permute-start | bytes 1179656 | tf_op jit(solution)/shard_map/ppermute | solution.py:541
  13.6 9.4 %collective-permute-done.1.come_ref = bf16[256,768]{1,0:T(8,128)(2,1)S(1)} collective-permute-done((bf16[256,768]{1,0:T(8,128)(2,1)S(1)}, bf16[256,768]{1,0:T(8,128)(2,1)S(1)}, u32[]{:S(2)}, u32[]{:S(2)}) %collective-permute-start.1) | collective-permute-done | bytes 393248 | tf_op jit(solution)/shard_map/ppermute | solution.py:541
  25.0 1.7 %collective-permute-done.2.theirs_ref = bf16[256,768]{1,0:T(8,128)(2,1)S(1)} collective-permute-done((bf16[256,768]{1,0:T(8,128)(2,1)S(1)}, bf16[256,768]{1,0:T(8,128)(2,1)S(1)}, u32[]{:S(2)}, u32[]{:S(2)}) %collective-permute-start.2) | collective-permute-done | bytes 393248 | tf_op jit(solution)/shard_map/ppermute | solution.py:538
  26.8 3.7 %expert_kernel.1 = (bf16[512,768]{1,0:T(8,128)(2,1)S(1)}, bf16[512,768]{1,0:T(8,128)(2,1)S(1)}, bf16[256,768]{1,0:T(8,128)(2,1)S(1)}, bf16[256,768]{1,0:T(8,128)(2,1)S(1)}, f32[1,768]{1,0:T(1,128)S(1)}) custom-call(bf16[256,768]{1,0:T(8,128)(2,1)S(1)} %get-tuple-element.80.mine_ref, bf16[256,768]{1,0:T(8,128)(2,1)S(1)} %collective-permute-done.2.theirs_ref, ...), custom_call_target="tpu_custom_call" | custom-call | flops 1000 | bytes 1000 | tf_op jit(solution)/shard_map/expert_kernel/pallas_call | solution.py:30
  30.7 1.6 %collective-permute-done.3.come_ref = bf16[256,768]{1,0:T(8,128)(2,1)S(1)} collective-permute-done((bf16[256,768]{1,0:T(8,128)(2,1)S(1)}, bf16[256,768]{1,0:T(8,128)(2,1)S(1)}, u32[]{:S(2)}, u32[]{:S(2)}) %collective-permute-start.3) | collective-permute-done | bytes 393248 | tf_op jit(solution)/shard_map/ppermute | solution.py:538
  32.3 1.5 expert_weights_kernel.1
  33.8 1.4 copy-done.9
  35.2 7.9 %all-to-all-start = ((bf16[16,96,768]{2,1,0:T(8,128)(2,1)}), bf16[16,96,768]{2,1,0:T(8,128)(2,1)S(1)}, u32[]{:S(2)}, u32[]{:S(2)}) async-start(bf16[16,96,768]{2,1,0:T(8,128)(2,1)} %copy-done.9), calls=%async_computation | async-start | bytes 4718592 | tf_op jit(solution)/shard_map/all_to_all | solution.py:550
  43.1 3.3 %collective-permute-start.4 = (bf16[256,768]{1,0:T(8,128)(2,1)S(1)}, bf16[256,768]{1,0:T(8,128)(2,1)S(1)}, u32[]{:S(2)}, u32[]{:S(2)}) collective-permute-start(bf16[256,768]{1,0:T(8,128)(2,1)S(1)} %pair_kernel.5.pair_ref), channel_id=1, source_target_pairs={{0,2},{2,0},{1,3},{3,1},{4,6},{6,4},{5,7},{7,5},{8,10},{10,8},{9,1... | collective-permute-start | bytes 1179656 | tf_op jit(solution)/shard_map/ppermute | solution.py:541
  46.4 1.3 copy-done.2
  47.7 1.1 copy-done.20
  49.6 6.0 %collective-permute-done.4.come_ref = bf16[256,768]{1,0:T(8,128)(2,1)S(1)} collective-permute-done((bf16[256,768]{1,0:T(8,128)(2,1)S(1)}, bf16[256,768]{1,0:T(8,128)(2,1)S(1)}, u32[]{:S(2)}, u32[]{:S(2)}) %collective-permute-start.4) | collective-permute-done | bytes 393248 | tf_op jit(solution)/shard_map/ppermute | solution.py:541
  57.4 3.3 %collective-permute-start.7 = (bf16[256,768]{1,0:T(8,128)(2,1)S(1)}, bf16[256,768]{1,0:T(8,128)(2,1)S(1)}, u32[]{:S(2)}, u32[]{:S(2)}) collective-permute-start(bf16[256,768]{1,0:T(8,128)(2,1)S(1)} %pair_kernel.6.pair_ref), channel_id=1, source_target_pairs={{0,2},{2,0},{1,3},{3,1},{4,6},{6,4},{5,7},{7,5},{8,10},{10,8},{9,1... | collective-permute-start | bytes 1179656 | tf_op jit(solution)/shard_map/ppermute | solution.py:541
  60.7 3.3 %attend_back_kernel.1 = (bf16[576,512]{1,0:T(8,128)(2,1)S(1)}, bf16[16,48,768]{2,1,0:T(8,128)(2,1)S(1)}, f32[8,576]{1,0:T(8,128)S(1)}) custom-call(bf16[256,768]{1,0:T(8,128)(2,1)S(1)} %get-tuple-element.89.mine_ref, bf16[256,768]{1,0:T(8,128)(2,1)S(1)} %collective-permute-done.6.theirs_ref, bf16[192,768]{1,0:T(8,128)(2,1)S(1)} %copy-done.13, ...), custom_call_target="tpu_custom_call" | custom-call | flops 1000 | bytes 1000 | tf_op jit(solution)/shard_map/attend_back_kernel/pallas_call | solution.py:30
  64.0 6.1 %collective-permute-done.7.come_ref = bf16[256,768]{1,0:T(8,128)(2,1)S(1)} collective-permute-done((bf16[256,768]{1,0:T(8,128)(2,1)S(1)}, bf16[256,768]{1,0:T(8,128)(2,1)S(1)}, u32[]{:S(2)}, u32[]{:S(2)}) %collective-permute-start.7) | collective-permute-done | bytes 393248 | tf_op jit(solution)/shard_map/ppermute | solution.py:541
  71.0 1.7 %collective-permute-done.9.come_ref = bf16[256,768]{1,0:T(8,128)(2,1)S(1)} collective-permute-done((bf16[256,768]{1,0:T(8,128)(2,1)S(1)}, bf16[256,768]{1,0:T(8,128)(2,1)S(1)}, u32[]{:S(2)}, u32[]{:S(2)}) %collective-permute-start.9) | collective-permute-done | bytes 393248 | tf_op jit(solution)/shard_map/ppermute | solution.py:538
  72.8 3.3 %collective-permute-start.11 = (bf16[256,768]{1,0:T(8,128)(2,1)S(1)}, bf16[256,768]{1,0:T(8,128)(2,1)}, u32[]{:S(2)}, u32[]{:S(2)}) collective-permute-start(bf16[256,768]{1,0:T(8,128)(2,1)S(1)} %pair_kernel.7.pair_ref), channel_id=1, source_target_pairs={{0,2},{2,0},{1,3},{3,1},{4,6},{6,4},{5,7},{7,5},{8,10},{10,8},{9,1... | collective-permute-start | bytes 1179656 | tf_op jit(solution)/shard_map/ppermute | solution.py:541
  76.1 3.9 %all-to-all-done.parts_ref = bf16[16,96,768]{2,1,0:T(8,128)(2,1)S(1)} async-done(((bf16[16,96,768]{2,1,0:T(8,128)(2,1)}), bf16[16,96,768]{2,1,0:T(8,128)(2,1)S(1)}, u32[]{:S(2)}, u32[]{:S(2)}) %all-to-all-start) | async-done | bytes 2359328 | tf_op jit(solution)/shard_map/all_to_all | solution.py:550
  80.0 4.4 %all-to-all-start.1 = ((bf16[16,48,768]{2,1,0:T(8,128)(2,1)}), bf16[16,48,768]{2,1,0:T(8,128)(2,1)}, u32[]{:S(2)}, u32[]{:S(2)}) async-start(bf16[16,48,768]{2,1,0:T(8,128)(2,1)} %copy-done.15), calls=%async_computation.1 | async-start | bytes 2359296 | tf_op jit(solution)/shard_map/all_to_all | solution.py:550
  84.7 1.7 %collective-permute-start.10 = (bf16[96,768]{1,0:T(8,128)(2,1)S(1)}, bf16[96,768]{1,0:T(8,128)(2,1)S(1)}, u32[]{:S(2)}, u32[]{:S(2)}) collective-permute-start(bf16[96,768]{1,0:T(8,128)(2,1)S(1)} %total_kernel.1.pair_ref), channel_id=1, source_target_pairs={{0,4},{4,0},{1,5},{5,1},{2,6},{6,2},{3,7},{7,3},{8,12},{12,8},{9,1... | collective-permute-start | bytes 442376 | tf_op jit(solution)/shard_map/ppermute | solution.py:544
  86.4 3.6 %collective-permute-done.10.come_ref = bf16[96,768]{1,0:T(8,128)(2,1)S(1)} collective-permute-done((bf16[96,768]{1,0:T(8,128)(2,1)S(1)}, bf16[96,768]{1,0:T(8,128)(2,1)S(1)}, u32[]{:S(2)}, u32[]{:S(2)}) %collective-permute-start.10) | collective-permute-done | bytes 147488 | tf_op jit(solution)/shard_map/ppermute | solution.py:544
  90.0 1.7 %first_norm_kernel.1.mine_ref = f32[264,768]{1,0:T(8,128)S(1)} custom-call(bf16[512,768]{1,0:T(8,128)(2,1)S(1)} %bitcast.12, bf16[256,768]{1,0:T(8,128)(2,1)S(1)} %pair_kernel.7.pair_ref, bf16[256,768]{1,0:T(8,128)(2,1)} %collective-permute-done.11.come_ref, f32[768]{0:T(1024)S(1)} %copy-done.33, f32[256,768]{1,0:T(8,128)S(1)} %copy-done.18, ...), custom_call_target="tpu_custom_call" | custom-call | flops 1000 | bytes 1000 | tf_op jit(solution)/shard_map/first_norm_kernel/pallas_call | solution.py:30
  91.8 1.8 %collective-permute-start.13 = (bf16[48,768]{1,0:T(8,128)(2,1)S(1)}, bf16[48,768]{1,0:T(8,128)(2,1)S(1)}, u32[]{:S(2)}, u32[]{:S(2)}) collective-permute-start(bf16[48,768]{1,0:T(8,128)(2,1)S(1)} %get-tuple-element.107.refs_0_), channel_id=1, source_target_pairs={{0,32},{32,0},{64,96},{96,64},{1,33},{33,1},{65,97},{97,65},{2,34}... | collective-permute-start | bytes 221192 | tf_op jit(solution)/shard_map/ppermute | solution.py:557
  93.7 1.5 collective-permute-start.14
  95.1 5.5 %collective-permute-done.13.refs_2_ = bf16[48,768]{1,0:T(8,128)(2,1)S(1)} collective-permute-done((bf16[48,768]{1,0:T(8,128)(2,1)S(1)}, bf16[48,768]{1,0:T(8,128)(2,1)S(1)}, u32[]{:S(2)}, u32[]{:S(2)}) %collective-permute-start.13) | collective-permute-done | bytes 73760 | tf_op jit(solution)/shard_map/ppermute | solution.py:557
  100.7 1.3 token_order_kernel.1
  102.0 1.2 all-to-all-done.1.parts_ref
  103.2 1.4 attend_total_kernel.1.pair_ref
  104.6 1.1 collective-permute-start.16
  105.8 2.1 %collective-permute-start.17 = (bf16[96,768]{1,0:T(8,128)(2,1)S(1)}, bf16[96,768]{1,0:T(8,128)(2,1)S(1)}, u32[]{:S(2)}, u32[]{:S(2)}) collective-permute-start(bf16[96,768]{1,0:T(8,128)(2,1)S(1)} %get-tuple-element.118.refs_1_), channel_id=1, source_target_pairs={{0,24},{8,16},{16,8},{24,0},{1,25},{9,17},{17,9},{25,1},{2,26},{10... | collective-permute-start | bytes 442376 | tf_op jit(solution)/shard_map/ppermute | solution.py:557
  107.8 3.2 %collective-permute-done.16.refs_2_ = bf16[96,768]{1,0:T(8,128)(2,1)S(1)} collective-permute-done((bf16[96,768]{1,0:T(8,128)(2,1)S(1)}, bf16[96,768]{1,0:T(8,128)(2,1)S(1)}, u32[]{:S(2)}, u32[]{:S(2)}) %collective-permute-start.16) | collective-permute-done | bytes 147488 | tf_op jit(solution)/shard_map/ppermute | solution.py:557
  111.1 1.1 collective-permute-done.17.refs_3_
  112.2 2.1 %collective-permute-start.19 = (bf16[192,768]{1,0:T(8,128)(2,1)S(1)}, bf16[192,768]{1,0:T(8,128)(2,1)S(1)}, u32[]{:S(2)}, u32[]{:S(2)}) collective-permute-start(bf16[192,768]{1,0:T(8,128)(2,1)S(1)} %get-tuple-element.119.refs_0_), channel_id=1, source_target_pairs={{0,24},{8,0},{16,8},{24,16},{1,25},{9,1},{17,9},{25,17},{2,26},{10... | collective-permute-start | bytes 884744 | tf_op jit(solution)/shard_map/ppermute | solution.py:567
  114.3 2.2 %collective-permute-start.21 = (bf16[192,768]{1,0:T(8,128)(2,1)S(1)}, bf16[192,768]{1,0:T(8,128)(2,1)S(1)}, u32[]{:S(2)}, u32[]{:S(2)}) collective-permute-start(bf16[192,768]{1,0:T(8,128)(2,1)S(1)} %get-tuple-element.120.refs_3_), channel_id=1, source_target_pairs={{0,96},{32,0},{64,32},{96,64},{1,97},{33,1},{65,33},{97,65},{2,98}... | collective-permute-start | bytes 884744 | tf_op jit(solution)/shard_map/ppermute | solution.py:567
  116.5 1.6 %collective-permute-start.15 = (bf16[56,768]{1,0:T(8,128)(2,1)S(1)}, bf16[56,768]{1,0:T(8,128)(2,1)S(1)}, u32[]{:S(2)}, u32[]{:S(2)}) collective-permute-start(bf16[56,768]{1,0:T(8,128)(2,1)S(1)} %attend_total_kernel.1.pair_ref), channel_id=1, source_target_pairs={{0,4},{4,0},{1,5},{5,1},{2,6},{6,2},{3,7},{7,3},{8,12},{12,8},{9,1... | collective-permute-start | bytes 258056 | tf_op jit(solution)/shard_map/ppermute | solution.py:544
  118.1 2.9 %collective-permute-done.15.come_ref = bf16[56,768]{1,0:T(8,128)(2,1)S(1)} collective-permute-done((bf16[56,768]{1,0:T(8,128)(2,1)S(1)}, bf16[56,768]{1,0:T(8,128)(2,1)S(1)}, u32[]{:S(2)}, u32[]{:S(2)}) %collective-permute-start.15) | collective-permute-done | bytes 86048 | tf_op jit(solution)/shard_map/ppermute | solution.py:544
  121.0 1.7 %collective-permute-done.18.refs_1_ = bf16[192,768]{1,0:T(8,128)(2,1)S(1)} collective-permute-done((bf16[192,768]{1,0:T(8,128)(2,1)S(1)}, bf16[192,768]{1,0:T(8,128)(2,1)S(1)}, u32[]{:S(2)}, u32[]{:S(2)}) %collective-permute-start.18) | collective-permute-done | bytes 294944 | tf_op jit(solution)/shard_map/ppermute | solution.py:567
  124.2 1.0 collective-permute-done.20.refs_4_
  125.2 1.2 attend_finish_kernel.1
  126.4 4.8 %all-to-all-start.2 = ((bf16[16,56,768]{2,1,0:T(8,128)(2,1)}), bf16[16,56,768]{2,1,0:T(8,128)(2,1)S(1)}, u32[]{:S(2)}, u32[]{:S(2)}) async-start(bf16[16,56,768]{2,1,0:T(8,128)(2,1)} %attend_finish_kernel.1), calls=%async_computation.2 | async-start | bytes 2752512 | tf_op jit(solution)/shard_map/all_to_all | solution.py:550
  133.3 3.2 %collective-permute-start.25 = (bf16[96,768]{1,0:T(8,128)(2,1)S(1)}, bf16[96,768]{1,0:T(8,128)(2,1)S(1)}, u32[]{:S(2)}, u32[]{:S(2)}) collective-permute-start(bf16[96,768]{1,0:T(8,128)(2,1)S(1)} %slice.15), channel_id=1, source_target_pairs={{0,96},{32,0},{64,32},{96,64},{1,97},{33,1},{65,33},{97,65},{2,98}... | collective-permute-start | bytes 442376 | tf_op jit(solution)/shard_map/ppermute | solution.py:567
  136.5 2.7 %collective-permute-start.23 = (bf16[96,768]{1,0:T(8,128)(2,1)S(1)}, bf16[96,768]{1,0:T(8,128)(2,1)S(1)}, u32[]{:S(2)}, u32[]{:S(2)}) collective-permute-start(bf16[96,768]{1,0:T(8,128)(2,1)S(1)} %slice.13), channel_id=1, source_target_pairs={{0,24},{8,0},{16,8},{24,16},{1,25},{9,1},{17,9},{25,17},{2,26},{10... | collective-permute-start | bytes 442376 | tf_op jit(solution)/shard_map/ppermute | solution.py:567
  140.1 3.8 %expert_most_kernel.1 = (f32[768,768]{1,0:T(8,128)}, f32[768,768]{1,0:T(8,128)}) custom-call(bf16[192,768]{1,0:T(8,128)(2,1)} %copy-done.25, bf16[192,768]{1,0:T(8,128)(2,1)} %copy-done.40, bf16[192,768]{1,0:T(8,128)(2,1)} %copy-done.38, bf16[192,768]{1,0:T(8,128)(2,1)} %copy-done.26, bf16[192,768]{1,0:T(8,128)(2,1)} %collective-permute-done.20.refs_4_, ...), custom_call_target="tpu_custom_call" | custom-call | flops 1000 | bytes 1000 | tf_op jit(solution)/shard_map/expert_most_kernel/pallas_call | solution.py:30
  143.9 5.9 %collective-permute-done.25.b_high = bf16[96,768]{1,0:T(8,128)(2,1)S(1)} collective-permute-done((bf16[96,768]{1,0:T(8,128)(2,1)S(1)}, bf16[96,768]{1,0:T(8,128)(2,1)S(1)}, u32[]{:S(2)}, u32[]{:S(2)}) %collective-permute-start.25) | collective-permute-done | bytes 147488 | tf_op jit(solution)/shard_map/ppermute | solution.py:567
  151.4 2.5 %last_kernel.1 = (f32[768,768]{1,0:T(8,128)}, f32[768,768]{1,0:T(8,128)}, f32[576,768]{1,0:T(8,128)}, f32[192,768]{1,0:T(8,128)}, f32[3,128]{1,0:T(4,128)}, /*in...) custom-call(bf16[16,56,768]{2,1,0:T(8,128)(2,1)S(1)} %all-to-all-don, ...), custom_call_target="tpu_custom_call", output_to_operand_aliasing={{0}: (5, {}), {1}: (6, {})} | custom-call | flops 1000 | bytes 1000 | tf_op jit(solution)/shard_map/last_kernel/pallas_call | solution.py:30
  (126 shorter events, 12.4 us)
Async XLA Ops:
  0.6 26.1 %copy-start.36 = (f32[768]{0:T(1024)S(1)}, f32[768]{0:T(1024)}, u32[]{:S(2)}) copy-start(f32[768]{0:T(1024)} %bias_ref.6) | copy-start | bytes 9220
  0.7 22.4 %copy-start = (bf16[1,512,768]{2,1,0:T(8,128)(2,1)S(1)}, bf16[1,512,768]{2,1,0:T(8,128)(2,1)}, u32[]{:S(2)}) copy-start(bf16[1,512,768]{2,1,0:T(8,128)(2,1)} %param.15) | copy-start | bytes 2359300
  0.7 22.4 %copy-start.32 = (f32[768]{0:T(1024)S(1)}, f32[768]{0:T(1024)}, u32[]{:S(2)}) copy-start(f32[768]{0:T(1024)} %gain_ref.6) | copy-start | bytes 9220
  0.7 22.4 %copy-start.34 = (f32[768]{0:T(1024)S(1)}, f32[768]{0:T(1024)}, u32[]{:S(2)}) copy-start(f32[768]{0:T(1024)} %bias_ref.5) | copy-start | bytes 9220
  0.7 26.1 %copy-start.14 = (bf16[768,768]{1,0:T(8,128)(2,1)S(1)}, bf16[768,768]{1,0:T(8,128)(2,1)}, u32[]{:S(2)}) copy-start(bf16[768,768]{1,0:T(8,128)(2,1)} %up_ref.1) | copy-start | bytes 3538948
  7.2 19.6 %copy-start.1 = (bf16[768,768]{1,0:T(8,128)(2,1)S(1)}, bf16[768,768]{1,0:T(8,128)(2,1)}, u32[]{:S(2)}) copy-start(bf16[768,768]{1,0:T(8,128)(2,1)} %down_ref.3) | copy-start | bytes 3538948
  7.2 19.6 %copy-start.4 = (bf16[1,512,768]{2,1,0:T(8,128)(2,1)S(1)}, bf16[1,512,768]{2,1,0:T(8,128)(2,1)}, u32[]{:S(2)}) copy-start(bf16[1,512,768]{2,1,0:T(8,128)(2,1)} %param.29) | copy-start | bytes 2359300
  7.2 2.0 %collective-permute-start = (bf16[256,768]{1,0:T(8,128)(2,1)}, bf16[256,768]{1,0:T(8,128)(2,1)S(1)}, u32[]{:S(2)}, u32[]{:S(2)}) collective-permute-start(bf16[256,768]{1,0:T(8,128)(2,1)} %get-tuple-element.78), channel_id=1, source_target_pairs={{0,1},{1,0},{2,3},{3,2},{4,5},{5,4},{6,7},{7,6},{8,9},{9,8},{10,11... | collective-permute-start | bytes 1179656 | tf_op jit(solution)/shard_map/ppermute | solution.py:538
  10.3 12.8 %collective-permute-start.1 = (bf16[256,768]{1,0:T(8,128)(2,1)S(1)}, bf16[256,768]{1,0:T(8,128)(2,1)S(1)}, u32[]{:S(2)}, u32[]{:S(2)}) collective-permute-start(bf16[256,768]{1,0:T(8,128)(2,1)S(1)} %pair_kernel.4.pair_ref), channel_id=1, source_target_pairs={{0,2},{2,0},{1,3},{3,1},{4,6},{6,4},{5,7},{7,5},{8,10},{10,8},{9,1... | collective-permute-start | bytes 1179656 | tf_op jit(solution)/shard_map/ppermute | solution.py:541
  25.0 1.7 %collective-permute-start.2 = (bf16[256,768]{1,0:T(8,128)(2,1)S(1)}, bf16[256,768]{1,0:T(8,128)(2,1)S(1)}, u32[]{:S(2)}, u32[]{:S(2)}) collective-permute-start(bf16[256,768]{1,0:T(8,128)(2,1)S(1)} %get-tuple-element.80.mine_ref), channel_id=1, source_target_pairs={{0,1},{1,0},{2,3},{3,2},{4,5},{5,4},{6,7},{7,6},{8,9},{9,8},{10,11... | collective-permute-start | bytes 1179656 | tf_op jit(solution)/shard_map/ppermute | solution.py:538
  30.5 1.8 %collective-permute-start.3 = (bf16[256,768]{1,0:T(8,128)(2,1)S(1)}, bf16[256,768]{1,0:T(8,128)(2,1)S(1)}, u32[]{:S(2)}, u32[]{:S(2)}) collective-permute-start(bf16[256,768]{1,0:T(8,128)(2,1)S(1)} %get-tuple-element.82), channel_id=1, source_target_pairs={{0,1},{1,0},{2,3},{3,2},{4,5},{5,4},{6,7},{7,6},{8,9},{9,8},{10,11... | collective-permute-start | bytes 1179656 | tf_op jit(solution)/shard_map/ppermute | solution.py:538
  35.2 44.8 %all-to-all-start = ((bf16[16,96,768]{2,1,0:T(8,128)(2,1)}), bf16[16,96,768]{2,1,0:T(8,128)(2,1)S(1)}, u32[]{:S(2)}, u32[]{:S(2)}) async-start(bf16[16,96,768]{2,1,0:T(8,128)(2,1)} %copy-done.9), calls=%async_computation | async-start | bytes 4718592 | tf_op jit(solution)/shard_map/all_to_all | solution.py:550
  43.1 12.5 %collective-permute-start.4 = (bf16[256,768]{1,0:T(8,128)(2,1)S(1)}, bf16[256,768]{1,0:T(8,128)(2,1)S(1)}, u32[]{:S(2)}, u32[]{:S(2)}) collective-permute-start(bf16[256,768]{1,0:T(8,128)(2,1)S(1)} %pair_kernel.5.pair_ref), channel_id=1, source_target_pairs={{0,2},{2,0},{1,3},{3,1},{4,6},{6,4},{5,7},{7,5},{8,10},{10,8},{9,1... | collective-permute-start | bytes 1179656 | tf_op jit(solution)/shard_map/ppermute | solution.py:541
  48.8 6.8 %copy-start.5 = (bf16[1,512,768]{2,1,0:T(8,128)(2,1)S(1)}, bf16[1,512,768]{2,1,0:T(8,128)(2,1)}, u32[]{:S(2)}) copy-start(bf16[1,512,768]{2,1,0:T(8,128)(2,1)} %param.29) | copy-start | bytes 2359300
  48.8 6.8 %copy-start.7 = (f32[256,768]{1,0:T(8,128)S(1)}, f32[256,768]{1,0:T(8,128)}, u32[]{:S(2)}) copy-start(f32[256,768]{1,0:T(8,128)} %copy-done.6) | copy-start | bytes 2359300
  55.6 1.7 %collective-permute-start.5 = (bf16[256,768]{1,0:T(8,128)(2,1)S(1)}, bf16[256,768]{1,0:T(8,128)(2,1)S(1)}, u32[]{:S(2)}, u32[]{:S(2)}) collective-permute-start(bf16[256,768]{1,0:T(8,128)(2,1)S(1)} %get-tuple-element.88), channel_id=1, source_target_pairs={{0,1},{1,0},{2,3},{3,2},{4,5},{5,4},{6,7},{7,6},{8,9},{9,8},{10,11... | collective-permute-start | bytes 1179656 | tf_op jit(solution)/shard_map/ppermute | solution.py:538
  56.5 7.5 %copy-start.28 = (f32[8,768]{1,0:T(8,128)}, f32[8,768]{1,0:T(8,128)S(1)}, u32[]{:S(2)}) copy-start(f32[8,768]{1,0:T(8,128)S(1)} %get-tuple-element.102.rows_ref) | copy-start | bytes 73732
  56.5 4.1 %collective-permute-start.6 = (bf16[256,768]{1,0:T(8,128)(2,1)S(1)}, bf16[256,768]{1,0:T(8,128)(2,1)S(1)}, u32[]{:S(2)}, u32[]{:S(2)}) collective-permute-start(bf16[256,768]{1,0:T(8,128)(2,1)S(1)} %get-tuple-element.89.mine_ref), channel_id=1, source_target_pairs={{0,1},{1,0},{2,3},{3,2},{4,5},{5,4},{6,7},{7,6},{8,9},{9,8},{10,11... | collective-permute-start | bytes 1179656 | tf_op jit(solution)/shard_map/ppermute | solution.py:538
  57.4 6.7 %copy-start.11 = (bf16[256,768]{1,0:T(8,128)(2,1)}, bf16[256,768]{1,0:T(8,128)(2,1)S(1)}, u32[]{:S(2)}) copy-start(bf16[256,768]{1,0:T(8,128)(2,1)S(1)} %pair_kernel.6.pair_ref) | copy-start | bytes 1179652
  57.4 12.7 %collective-permute-start.7 = (bf16[256,768]{1,0:T(8,128)(2,1)S(1)}, bf16[256,768]{1,0:T(8,128)(2,1)S(1)}, u32[]{:S(2)}, u32[]{:S(2)}) collective-permute-start(bf16[256,768]{1,0:T(8,128)(2,1)S(1)} %pair_kernel.6.pair_ref), channel_id=1, source_target_pairs={{0,2},{2,0},{1,3},{3,1},{4,6},{6,4},{5,7},{7,5},{8,10},{10,8},{9,1... | collective-permute-start | bytes 1179656 | tf_op jit(solution)/shard_map/ppermute | solution.py:541
  60.7 9.4 %copy-start.3 = (bf16[768,3,192]{0,2,1:T(8,128)(2,1)S(1)}, bf16[768,3,192]{0,2,1:T(8,128)(2,1)}, u32[]{:S(2)}) copy-start(bf16[768,3,192]{0,2,1:T(8,128)(2,1)} %param.19) | copy-start | bytes 2654212
  64.0 8.8 %copy-start.15 = (bf16[16,48,768]{2,1,0:T(8,128)(2,1)}, bf16[16,48,768]{2,1,0:T(8,128)(2,1)S(1)}, u32[]{:S(2)}) copy-start(bf16[16,48,768]{2,1,0:T(8,128)(2,1)S(1)} %get-tuple-element.114) | copy-start | bytes 3538948
  64.0 8.8 %copy-start.30 = (f32[8,576]{1,0:T(8,128)}, f32[8,576]{1,0:T(8,128)S(1)}, u32[]{:S(2)}) copy-start(f32[8,576]{1,0:T(8,128)S(1)} %get-tuple-element.104.qkv_ref) | copy-start | bytes 55300
  70.9 1.8 %collective-permute-start.9 = (bf16[256,768]{1,0:T(8,128)(2,1)S(1)}, bf16[256,768]{1,0:T(8,128)(2,1)S(1)}, u32[]{:S(2)}, u32[]{:S(2)}) collective-permute-start(bf16[256,768]{1,0:T(8,128)(2,1)S(1)} %get-tuple-element.98), channel_id=1, source_target_pairs={{0,1},{1,0},{2,3},{3,2},{4,5},{5,4},{6,7},{7,6},{8,9},{9,8},{10,11... | collective-permute-start | bytes 1179656 | tf_op jit(solution)/shard_map/ppermute | solution.py:538
  72.8 13.6 %collective-permute-start.11 = (bf16[256,768]{1,0:T(8,128)(2,1)S(1)}, bf16[256,768]{1,0:T(8,128)(2,1)}, u32[]{:S(2)}, u32[]{:S(2)}) collective-permute-start(bf16[256,768]{1,0:T(8,128)(2,1)S(1)} %pair_kernel.7.pair_ref), channel_id=1, source_target_pairs={{0,2},{2,0},{1,3},{3,1},{4,6},{6,4},{5,7},{7,5},{8,10},{10,8},{9,1... | collective-permute-start | bytes 1179656 | tf_op jit(solution)/shard_map/ppermute | solution.py:541
  80.0 23.2 %all-to-all-start.1 = ((bf16[16,48,768]{2,1,0:T(8,128)(2,1)}), bf16[16,48,768]{2,1,0:T(8,128)(2,1)}, u32[]{:S(2)}, u32[]{:S(2)}) async-start(bf16[16,48,768]{2,1,0:T(8,128)(2,1)} %copy-done.15), calls=%async_computation.1 | async-start | bytes 2359296 | tf_op jit(solution)/shard_map/all_to_all | solution.py:550
  84.4 5.6 %copy-start.18 = (f32[256,768]{1,0:T(8,128)S(1)}, f32[256,768]{1,0:T(8,128)}, u32[]{:S(2)}) copy-start(f32[256,768]{1,0:T(8,128)} %copy-done.17) | copy-start | bytes 2359300
  84.4 5.6 %copy-start.29 = (f32[8,768]{1,0:T(8,128)S(1)}, f32[8,768]{1,0:T(8,128)}, u32[]{:S(2)}) copy-start(f32[8,768]{1,0:T(8,128)} %copy-done.28) | copy-start | bytes 73732
  84.7 5.2 %collective-permute-start.10 = (bf16[96,768]{1,0:T(8,128)(2,1)S(1)}, bf16[96,768]{1,0:T(8,128)(2,1)S(1)}, u32[]{:S(2)}, u32[]{:S(2)}) collective-permute-start(bf16[96,768]{1,0:T(8,128)(2,1)S(1)} %total_kernel.1.pair_ref), channel_id=1, source_target_pairs={{0,4},{4,0},{1,5},{5,1},{2,6},{6,2},{3,7},{7,3},{8,12},{12,8},{9,1... | collective-permute-start | bytes 442376 | tf_op jit(solution)/shard_map/ppermute | solution.py:544
  90.0 10.8 %copy-start.31 = (f32[8,576]{1,0:T(8,128)S(1)}, f32[8,576]{1,0:T(8,128)}, u32[]{:S(2)}) copy-start(f32[8,576]{1,0:T(8,128)} %copy-done.30) | copy-start | bytes 55300
  91.7 9.0 %collective-permute-start.12 = (f32[264,768]{1,0:T(8,128)S(1)}, f32[264,768]{1,0:T(8,128)S(1)}, u32[]{:S(2)}, u32[]{:S(2)}) collective-permute-start(f32[264,768]{1,0:T(8,128)S(1)} %first_norm_kernel.1.mine_ref), channel_id=1, source_target_pairs={{0,1},{1,0},{2,3},{3,2},{4,5},{5,4},{6,7},{7,6},{8,9},{9,8},{10,11... | collective-permute-start | bytes 2433032 | tf_op jit(solution)/shard_map/ppermute | solution.py:538
  91.8 8.9 %collective-permute-start.13 = (bf16[48,768]{1,0:T(8,128)(2,1)S(1)}, bf16[48,768]{1,0:T(8,128)(2,1)S(1)}, u32[]{:S(2)}, u32[]{:S(2)}) collective-permute-start(bf16[48,768]{1,0:T(8,128)(2,1)S(1)} %get-tuple-element.107.refs_0_), channel_id=1, source_target_pairs={{0,32},{32,0},{64,96},{96,64},{1,33},{33,1},{65,97},{97,65},{2,34}... | collective-permute-start | bytes 221192 | tf_op jit(solution)/shard_map/ppermute | solution.py:557
  93.7 7.0 %collective-permute-start.14 = (bf16[48,768]{1,0:T(8,128)(2,1)S(1)}, bf16[48,768]{1,0:T(8,128)(2,1)S(1)}, u32[]{:S(2)}, u32[]{:S(2)}) collective-permute-start(bf16[48,768]{1,0:T(8,128)(2,1)S(1)} %get-tuple-element.108.refs_1_), channel_id=1, source_target_pairs={{0,8},{8,0},{16,24},{24,16},{1,9},{9,1},{17,25},{25,17},{2,10},{10... | collective-permute-start | bytes 221192 | tf_op jit(solution)/shard_map/ppermute | solution.py:557
  104.6 6.4 %collective-permute-start.16 = (bf16[96,768]{1,0:T(8,128)(2,1)S(1)}, bf16[96,768]{1,0:T(8,128)(2,1)S(1)}, u32[]{:S(2)}, u32[]{:S(2)}) collective-permute-start(bf16[96,768]{1,0:T(8,128)(2,1)S(1)} %get-tuple-element.117.refs_0_), channel_id=1, source_target_pairs={{0,96},{32,64},{64,32},{96,0},{1,97},{33,65},{65,33},{97,1},{2,98}... | collective-permute-start | bytes 442376 | tf_op jit(solution)/shard_map/ppermute | solution.py:557
  105.8 6.4 %collective-permute-start.17 = (bf16[96,768]{1,0:T(8,128)(2,1)S(1)}, bf16[96,768]{1,0:T(8,128)(2,1)S(1)}, u32[]{:S(2)}, u32[]{:S(2)}) collective-permute-start(bf16[96,768]{1,0:T(8,128)(2,1)S(1)} %get-tuple-element.118.refs_1_), channel_id=1, source_target_pairs={{0,24},{8,16},{16,8},{24,0},{1,25},{9,17},{17,9},{25,1},{2,26},{10... | collective-permute-start | bytes 442376 | tf_op jit(solution)/shard_map/ppermute | solution.py:557
  112.2 14.2 %copy-start.25 = (bf16[192,768]{1,0:T(8,128)(2,1)}, bf16[192,768]{1,0:T(8,128)(2,1)S(1)}, u32[]{:S(2)}) copy-start(bf16[192,768]{1,0:T(8,128)(2,1)S(1)} %get-tuple-element.119.refs_0_) | copy-start | bytes 884740
  112.2 14.2 %copy-start.26 = (bf16[192,768]{1,0:T(8,128)(2,1)}, bf16[192,768]{1,0:T(8,128)(2,1)S(1)}, u32[]{:S(2)}) copy-start(bf16[192,768]{1,0:T(8,128)(2,1)S(1)} %get-tuple-element.120.refs_3_) | copy-start | bytes 884740
  112.2 8.8 %collective-permute-start.19 = (bf16[192,768]{1,0:T(8,128)(2,1)S(1)}, bf16[192,768]{1,0:T(8,128)(2,1)S(1)}, u32[]{:S(2)}, u32[]{:S(2)}) collective-permute-start(bf16[192,768]{1,0:T(8,128)(2,1)S(1)} %get-tuple-element.119.refs_0_), channel_id=1, source_target_pairs={{0,24},{8,0},{16,8},{24,16},{1,25},{9,1},{17,9},{25,17},{2,26},{10... | collective-permute-start | bytes 884744 | tf_op jit(solution)/shard_map/ppermute | solution.py:567
  114.3 8.4 %collective-permute-start.18 = (bf16[192,768]{1,0:T(8,128)(2,1)S(1)}, bf16[192,768]{1,0:T(8,128)(2,1)S(1)}, u32[]{:S(2)}, u32[]{:S(2)}) collective-permute-start(bf16[192,768]{1,0:T(8,128)(2,1)S(1)} %get-tuple-element.119.refs_0_), channel_id=1, source_target_pairs={{0,8},{8,16},{16,24},{24,0},{1,9},{9,17},{17,25},{25,1},{2,10},{10... | collective-permute-start | bytes 884744 | tf_op jit(solution)/shard_map/ppermute | solution.py:567
  114.3 8.4 %collective-permute-start.21 = (bf16[192,768]{1,0:T(8,128)(2,1)S(1)}, bf16[192,768]{1,0:T(8,128)(2,1)S(1)}, u32[]{:S(2)}, u32[]{:S(2)}) collective-permute-start(bf16[192,768]{1,0:T(8,128)(2,1)S(1)} %get-tuple-element.120.refs_3_), channel_id=1, source_target_pairs={{0,96},{32,0},{64,32},{96,64},{1,97},{33,1},{65,33},{97,65},{2,98}... | collective-permute-start | bytes 884744 | tf_op jit(solution)/shard_map/ppermute | solution.py:567
  116.5 8.7 %collective-permute-start.20 = (bf16[192,768]{1,0:T(8,128)(2,1)S(1)}, bf16[192,768]{1,0:T(8,128)(2,1)}, u32[]{:S(2)}, u32[]{:S(2)}) collective-permute-start(bf16[192,768]{1,0:T(8,128)(2,1)S(1)} %get-tuple-element.120.refs_3_), channel_id=1, source_target_pairs={{0,32},{32,64},{64,96},{96,0},{1,33},{33,65},{65,97},{97,1},{2,34}... | collective-permute-start | bytes 884744 | tf_op jit(solution)/shard_map/ppermute | solution.py:567
  116.5 4.5 %collective-permute-start.15 = (bf16[56,768]{1,0:T(8,128)(2,1)S(1)}, bf16[56,768]{1,0:T(8,128)(2,1)S(1)}, u32[]{:S(2)}, u32[]{:S(2)}) collective-permute-start(bf16[56,768]{1,0:T(8,128)(2,1)S(1)} %attend_total_kernel.1.pair_ref), channel_id=1, source_target_pairs={{0,4},{4,0},{1,5},{5,1},{2,6},{6,2},{3,7},{7,3},{8,12},{12,8},{9,1... | collective-permute-start | bytes 258056 | tf_op jit(solution)/shard_map/ppermute | solution.py:544
  126.4 25.0 %all-to-all-start.2 = ((bf16[16,56,768]{2,1,0:T(8,128)(2,1)}), bf16[16,56,768]{2,1,0:T(8,128)(2,1)S(1)}, u32[]{:S(2)}, u32[]{:S(2)}) async-start(bf16[16,56,768]{2,1,0:T(8,128)(2,1)} %attend_finish_kernel.1), calls=%async_computation.2 | async-start | bytes 2752512 | tf_op jit(solution)/shard_map/all_to_all | solution.py:550
  131.5 7.7 %collective-permute-start.8 = (bf16[256,768]{1,0:T(8,128)(2,1)S(1)}, bf16[256,768]{1,0:T(8,128)(2,1)S(1)}, u32[]{:S(2)}, u32[]{:S(2)}) collective-permute-start(bf16[256,768]{1,0:T(8,128)(2,1)S(1)} %mixed_kernel.1.mine_ref), channel_id=1, source_target_pairs={{0,1},{1,0},{2,3},{3,2},{4,5},{5,4},{6,7},{7,6},{8,9},{9,8},{10,11... | collective-permute-start | bytes 1179656 | tf_op jit(solution)/shard_map/ppermute | solution.py:538
  133.3 16.5 %collective-permute-start.25 = (bf16[96,768]{1,0:T(8,128)(2,1)S(1)}, bf16[96,768]{1,0:T(8,128)(2,1)S(1)}, u32[]{:S(2)}, u32[]{:S(2)}) collective-permute-start(bf16[96,768]{1,0:T(8,128)(2,1)S(1)} %slice.15), channel_id=1, source_target_pairs={{0,96},{32,0},{64,32},{96,64},{1,97},{33,1},{65,33},{97,65},{2,98}... | collective-permute-start | bytes 442376 | tf_op jit(solution)/shard_map/ppermute | solution.py:567
  136.5 13.5 %collective-permute-start.24 = (bf16[96,768]{1,0:T(8,128)(2,1)S(1)}, bf16[96,768]{1,0:T(8,128)(2,1)S(1)}, u32[]{:S(2)}, u32[]{:S(2)}) collective-permute-start(bf16[96,768]{1,0:T(8,128)(2,1)S(1)} %slice.14), channel_id=1, source_target_pairs={{0,32},{32,64},{64,96},{96,0},{1,33},{33,65},{65,97},{97,1},{2,34}... | collective-permute-start | bytes 442376 | tf_op jit(solution)/shard_map/ppermute | solution.py:567
  136.5 13.5 %collective-permute-start.23 = (bf16[96,768]{1,0:T(8,128)(2,1)S(1)}, bf16[96,768]{1,0:T(8,128)(2,1)S(1)}, u32[]{:S(2)}, u32[]{:S(2)}) collective-permute-start(bf16[96,768]{1,0:T(8,128)(2,1)S(1)} %slice.13), channel_id=1, source_target_pairs={{0,24},{8,0},{16,8},{24,16},{1,25},{9,1},{17,9},{25,17},{2,26},{10... | collective-permute-start | bytes 442376 | tf_op jit(solution)/shard_map/ppermute | solution.py:567
  139.2 11.3 %collective-permute-start.22 = (bf16[96,768]{1,0:T(8,128)(2,1)S(1)}, bf16[96,768]{1,0:T(8,128)(2,1)S(1)}, u32[]{:S(2)}, u32[]{:S(2)}) collective-permute-start(bf16[96,768]{1,0:T(8,128)(2,1)S(1)} %slice.12), channel_id=1, source_target_pairs={{0,8},{8,16},{16,24},{24,0},{1,9},{9,17},{17,25},{25,1},{2,10},{10... | collective-permute-start | bytes 442376 | tf_op jit(solution)/shard_map/ppermute | solution.py:567
  (25 other events, 72.6 us)
